TPU v7x, 32 devices: a whole 2x2x4 slice. The times are simulated.
32 devices in a mesh: zt: 16 (over z, x, core), xy: 2 (over y).
Axes of the slice: x: 2, y: 2, z: 4, core: 2. Of those that a mesh axis runs over, the one named last changes fastest.
Arguments:
- fine_vectors: bfloat16 [64, 2, 12, 16, 512], P('zt', None, None, None, 'xy'), may hold values from -6 to 6
- null_vectors: bfloat16 [64, 2, 12, 32, 512], P('zt', None, None, None, 'xy'), may hold values from -0.75 to 0.75
- coarse_operator: bfloat16 [16, 9, 2, 2, 2, 128, 128], P('zt'), may hold values from -0.3125 to 0.3125
Outputs:
- fine_correction: bfloat16 [64, 2, 12, 16, 512], P('zt', None, None, None, 'xy')
- coarse_iterate: bfloat16 [16, 2, 2, 2, 16, 128], P('zt')
All inputs are finite; a program needn't handle non-finite values.
Results may differ from a plain program's by a relative error of at most 0.018.
Values may be sent and summed in bfloat16 or wider, within the bound.
No kernel may reach another device: no remote copies, remote signals or barrier semaphores. Data moves between devices by JAX's collectives and lax.ppermute only.
A program may use at most 128 MiB of HBM per device.

v0:
```python
import jax
import jax.numpy as jnp
from jax import lax
from jax.sharding import PartitionSpec as P

CZ = 2
APPLIES = 4


RELAX_WEIGHT = 0.3
DIAGONAL_SHIFT = 3.0


def padded_2(array, sides, width):
    for axis, dim in sides:
        devices, length = (lax.axis_size(axis), array.shape[dim])
        up = [(i, (i + 1) % devices) for i in range(devices)]
        down = [(j, i) for i, j in up]
        last = lax.slice_in_dim(array, length - width, length, axis=dim)
        initial = lax.slice_in_dim(array, 0, width, axis=dim)
        before = lax.ppermute(last, axis, up)
        after = lax.ppermute(initial, axis, down)
        array = jnp.concatenate([before, array, after], axis=dim)
    return array


def local_restrict(fine_block, null_block):
    rhs_count = fine_block.shape[3]
    vectors = null_block.shape[3]
    coarse_y = fine_block.shape[4] // (64 * CZ)
    fine_view = fine_block.reshape(4, 2, 2, 6, rhs_count, 4, CZ, 4, coarse_y, 4)
    null_view = null_block.reshape(4, 2, 2, 6, vectors, 4, CZ, 4, coarse_y, 4)
    turned = jnp.stack([fine_view[:, 1], -fine_view[:, 0]], axis=1)
    real_sum = jnp.einsum(
        "tqhgkxzayb,tqhgrxzayb->yzrhk", null_view, fine_view, preferred_element_type=jnp.float32
    )
    imag_sum = jnp.einsum(
        "tqhgkxzayb,tqhgrxzayb->yzrhk", null_view, turned, preferred_element_type=jnp.float32
    )
    stacked = jnp.stack([real_sum, imag_sum], axis=3)
    return stacked.reshape(1, coarse_y, CZ, 1, rhs_count, 4 * vectors)


def local_prolong(coarse_block, null_block):
    coarse_y, depth, rhs_count, columns = coarse_block.shape
    vectors = columns // 4
    weights = coarse_block.reshape(coarse_y, depth, rhs_count, 2, 2, vectors)
    real_w = weights[:, :, :, 0]
    imag_w = weights[:, :, :, 1]
    mixer = jnp.stack([jnp.stack([real_w, -imag_w]), jnp.stack([imag_w, real_w])])
    null_view = null_block.reshape(4, 2, 2, 6, vectors, 4, depth, 4, coarse_y, 4)
    result = jnp.einsum(
        "tphgkxzayb,qpyzrhk->tqhgrxzayb", null_view, mixer, preferred_element_type=jnp.float32
    )
    return result.reshape(4, 2, 12, rhs_count, 4 * depth * 16 * coarse_y).astype(jnp.bfloat16)


def stencil_product(field, shifted, operator_block):
    stacked = jnp.stack(shifted, axis=1)
    image = jnp.einsum(
        "tdyzxij,tdyzxrj->tyzxri", operator_block, stacked, preferred_element_type=jnp.float32
    )
    return image + DIAGONAL_SHIFT * field.astype(jnp.float32)


def apply_whole(field, operator_block):
    padded = padded_2(field, (("zt", 0),), 1)
    shifted = [
        field,
        padded[2:],
        padded[:-2],
        jnp.roll(field, -1, 1),
        jnp.roll(field, 1, 1),
        jnp.roll(field, -1, 2),
        jnp.roll(field, 1, 2),
        jnp.roll(field, -1, 3),
        jnp.roll(field, 1, 3),
    ]
    return stencil_product(field, shifted, operator_block)


def per_device(fine_vectors, null_vectors, coarse_operator):
    position = lax.axis_index("xy")
    coarse_rhs = local_restrict(fine_vectors, null_vectors).astype(jnp.bfloat16)
    whole_rhs = lax.all_gather(coarse_rhs, "xy", axis=3, tiled=True)
    target = whole_rhs.astype(jnp.float32)
    iterate = RELAX_WEIGHT * target
    for sweep_index in range(APPLIES):
        image = apply_whole(iterate.astype(jnp.bfloat16), coarse_operator)
        iterate = iterate + RELAX_WEIGHT * (target - image)
    coarse_iterate = iterate.astype(jnp.bfloat16)
    column = lax.dynamic_slice_in_dim(coarse_iterate, position, 1, 3)
    fine_correction = local_prolong(column[0, :, :, 0], null_vectors)
    return (fine_correction, coarse_iterate)


def solution(mesh):
    return jax.shard_map(
        per_device,
        mesh=mesh,
        in_specs=(
            P("zt", None, None, None, "xy"),
            P("zt", None, None, None, "xy"),
            P("zt", None, None, None, None, None, None),
        ),
        out_specs=(P("zt", None, None, None, "xy"), P("zt", None, None, None, None, None)),
        check_vma=False,
    )
```

profile of v0, /device:TPU:0, one launch (start us, length us, event | category | flops | bytes accessed | tf_op | source)
XLA Modules:
  0.0 120.9 jit_solution(3107072517315403098)
XLA Ops:
  0.7 6.5 %copy.24 = bf16[4,2,12,32,256]{3,4,2,1,0:T(8,128)(2,1)} copy(bf16[4,2,12,32,256]{4,3,2,1,0:T(8,128)(2,1)} %param.4) | data formatting | bytes 3145728 | tf_op args[1]
  7.1 4.5 %copy.23 = bf16[4,2,12,16,256]{3,4,2,1,0:T(8,128)(2,1)} copy(bf16[4,2,12,16,256]{4,3,2,1,0:T(8,128)(2,1)S(1)} %copy-done.3) | data formatting | bytes 1572864 | tf_op args[0]
  11.6 8.0 %fusion.70 = (bf16[4,1,2,6,16,4,2,4,2,4]{4,9,8,7,6,5,3,2,1,0:T(4,128)(2,1)}, bf16[4,1,2,6,16,4,2,4,2,4]{4,9,8,7,6,5,3,2,1,0:T(4,128)(2,1)S(1)}) fusion(bf16[4,2,2,6,16,4,2,4,2,4]{4,9,8,7,6,5,3,2,1,0:T(4,128)(2,1)} %bitcast.228), kind=kLoop, calls=%fused_computation.110 | loop fusion | bytes 1572864 | tf_op jit(solution)/shard_map/slice | solution.py:33
  19.6 7.1 %fusion.44 = bf16[2,2,16,1,2,32]{5,2,4,1,0,3:T(8,128)(2,1)S(1)} fusion(bf16[4,2,2,6,32,4,2,4,2,4]{4,9,8,7,6,5,3,2,1,0:T(4,128)(2,1)S(1)} %bitcast.226, bf16[4,2,2,6,16,4,2,4,2,4]{4,9,8,7,6,5,3,2,1,0:T(4,128)(2,1)S(1)} %bitcast.229), kind=kOutput, calls=%fused_computation.27 | convolution fusion | flops 25169920 | bytes 2367488 | tf_op jit(solution)/shard_map/tqhgkxzayb,tqhgrxzayb->yzrhk/dot_general | solution.py:34
  26.7 4.1 %copy.82 = bf16[4,1,2,6,16,4,2,4,2,4]{4,3,5,0,1,9,7,2,6,8:T(8,128)(2,1)S(1)} copy(bf16[4,1,2,6,16,4,2,4,2,4]{4,9,8,7,6,5,3,2,1,0:T(4,128)(2,1)} %get-tuple-element.10) | data formatting | bytes 786432
  30.7 2.7 %copy_negate_fusion = bf16[4,1,2,6,16,4,2,4,2,4]{4,3,5,0,1,9,7,2,6,8:T(8,128)(2,1)S(1)} fusion(bf16[4,1,2,6,16,4,2,4,2,4]{4,9,8,7,6,5,3,2,1,0:T(4,128)(2,1)S(1)} %get-tuple-element.11), kind=kLoop, calls=%fused_computation.11 | loop fusion | flops 196608 | bytes 786432 | tf_op jit(solution)/shard_map/neg | solution.py:33
  33.5 16.0 %fusion.3 = bf16[2,2,2,16,32,1,1,1,1,1]{4,3,9,8,7,0,1,2,6,5:T(8,128)(2,1)S(1)} fusion(bf16[4,2,2,6,32,4,2,4,2,4]{4,9,8,7,6,5,3,2,1,0:T(4,128)(2,1)S(1)} %bitcast.227, bf16[4,1,2,6,16,4,2,4,2,4]{4,3,5,0,1,9,7,2,6,8:T(8,128)(2,1)S(1)} %copy_negate_fusion, bf16[4,1,2,6,16,4,2,4,2,4]{4,3,5,0,1,9,7,2,6,8:T(8,128)(2,1)S(1)} %copy.82), kind=kOutput, calls=%fused_computation.5 | convolution fusion | flops 25559040 | bytes 2367488 | tf_op jit(solution)/shard_map/tqhgkxzayb,tqhgrxzayb->yzrhk/dot_general | solution.py:37
  49.5 0.1 copy.30
  49.6 0.1 convert_element_type.51
  49.7 5.5 %all_gather.3 = bf16[1,2,2,2,16,128]{5,4,3,2,1,0:T(8,128)(2,1)S(1)} all-gather(bf16[1,2,2,1,16,128]{5,4,3,2,1,0:T(8,128)(2,1)S(1)} %bitcast.232), channel_id=1, replica_groups=mesh['zt'=16,'xy'=2] {'xy'}, dimensions={3}, use_global_device_ids=true | all-gather | bytes 49152 | tf_op jit(solution)/shard_map/all_gather | solution.py:85
  55.2 0.1 collective-permute-start.1
  55.3 4.4 %collective-permute-start = (bf16[1,2,2,2,16,128]{5,4,3,2,1,0:T(8,128)(2,1)S(1)}, bf16[1,2,2,2,16,128]{5,4,3,2,1,0:T(8,128)(2,1)S(1)}, u32[]{:S(2)}, u32[]{:S(2)}) collective-permute-start(bf16[1,2,2,2,16,128]{5,4,3,2,1,0:T(8,128)(2,1)S(1)} %fusion.55), channel_id=1, source_target_pairs={{2,0},{4,2},{6,4},{8,6},{10,8},{12,10},{14,12},{16,14},{18,16},{20... | collective-permute-start | bytes 98312 | tf_op jit(solution)/shard_map/ppermute | solution.py:22
  59.8 1.6 %collective-permute-done = bf16[1,2,2,2,16,128]{5,4,3,2,1,0:T(8,128)(2,1)S(1)} collective-permute-done((bf16[1,2,2,2,16,128]{5,4,3,2,1,0:T(8,128)(2,1)S(1)}, bf16[1,2,2,2,16,128]{5,4,3,2,1,0:T(8,128)(2,1)S(1)}, u32[]{:S(2)}, u32[]{:S(2)}) %collective-permute-start) | collective-permute-done | bytes 32800 | tf_op jit(solution)/shard_map/ppermute | solution.py:22
  61.4 0.8 constant_dynamic-update-slice_fusion.17
  62.3 4.5 %collective-permute-start.2 = (bf16[1,2,2,2,16,128]{5,4,3,2,1,0:T(8,128)(2,1)S(1)}, bf16[1,2,2,2,16,128]{5,4,3,2,1,0:T(8,128)(2,1)S(1)}, u32[]{:S(2)}, u32[]{:S(2)}) collective-permute-start(bf16[1,2,2,2,16,128]{5,4,3,2,1,0:T(8,128)(2,1)S(1)} %get-tuple-element.9), channel_id=1, source_target_pairs={{2,0},{4,2},{6,4},{8,6},{10,8},{12,10},{14,12},{16,14},{18,16},{20... | collective-permute-start | bytes 98312 | tf_op jit(solution)/shard_map/ppermute | solution.py:22
  66.8 1.6 %collective-permute-done.2 = bf16[1,2,2,2,16,128]{5,4,3,2,1,0:T(8,128)(2,1)S(1)} collective-permute-done((bf16[1,2,2,2,16,128]{5,4,3,2,1,0:T(8,128)(2,1)S(1)}, bf16[1,2,2,2,16,128]{5,4,3,2,1,0:T(8,128)(2,1)S(1)}, u32[]{:S(2)}, u32[]{:S(2)}) %collective-permute-start.2) | collective-permute-done | bytes 32800 | tf_op jit(solution)/shard_map/ppermute | solution.py:22
  68.4 4.5 %collective-permute-done.3 = bf16[1,2,2,2,16,128]{5,4,3,2,1,0:T(8,128)(2,1)S(1)} collective-permute-done((bf16[1,2,2,2,16,128]{5,4,3,2,1,0:T(8,128)(2,1)S(1)}, bf16[1,2,2,2,16,128]{5,4,3,2,1,0:T(8,128)(2,1)S(1)}, u32[]{:S(2)}, u32[]{:S(2)}) %collective-permute-start.3) | collective-permute-done | bytes 32800 | tf_op jit(solution)/shard_map/ppermute | solution.py:21
  73.0 0.8 fusion.17
  73.9 0.1 collective-permute-start.5
  73.9 4.4 %collective-permute-start.4 = (bf16[1,2,2,2,16,128]{5,4,3,2,1,0:T(8,128)(2,1)S(1)}, bf16[1,2,2,2,16,128]{5,4,3,2,1,0:T(8,128)(2,1)S(1)}, u32[]{:S(2)}, u32[]{:S(2)}) collective-permute-start(bf16[1,2,2,2,16,128]{5,4,3,2,1,0:T(8,128)(2,1)S(1)} %get-tuple-element.6), channel_id=1, source_target_pairs={{2,0},{4,2},{6,4},{8,6},{10,8},{12,10},{14,12},{16,14},{18,16},{20... | collective-permute-start | bytes 98312 | tf_op jit(solution)/shard_map/ppermute | solution.py:22
  78.4 1.6 %collective-permute-done.4 = bf16[1,2,2,2,16,128]{5,4,3,2,1,0:T(8,128)(2,1)S(1)} collective-permute-done((bf16[1,2,2,2,16,128]{5,4,3,2,1,0:T(8,128)(2,1)S(1)}, bf16[1,2,2,2,16,128]{5,4,3,2,1,0:T(8,128)(2,1)S(1)}, u32[]{:S(2)}, u32[]{:S(2)}) %collective-permute-start.4) | collective-permute-done | bytes 32800 | tf_op jit(solution)/shard_map/ppermute | solution.py:22
  80.0 0.1 collective-permute-done.5
  80.2 0.8 fusion.15
  81.0 4.4 %collective-permute-start.6 = (bf16[1,2,2,2,16,128]{5,4,3,2,1,0:T(8,128)(2,1)S(1)}, bf16[1,2,2,2,16,128]{5,4,3,2,1,0:T(8,128)(2,1)S(1)}, u32[]{:S(2)}, u32[]{:S(2)}) collective-permute-start(bf16[1,2,2,2,16,128]{5,4,3,2,1,0:T(8,128)(2,1)S(1)} %get-tuple-element.5), channel_id=1, source_target_pairs={{2,0},{4,2},{6,4},{8,6},{10,8},{12,10},{14,12},{16,14},{18,16},{20... | collective-permute-start | bytes 98312 | tf_op jit(solution)/shard_map/ppermute | solution.py:22
  85.4 1.6 %collective-permute-done.6 = bf16[1,2,2,2,16,128]{5,4,3,2,1,0:T(8,128)(2,1)S(1)} collective-permute-done((bf16[1,2,2,2,16,128]{5,4,3,2,1,0:T(8,128)(2,1)S(1)}, bf16[1,2,2,2,16,128]{5,4,3,2,1,0:T(8,128)(2,1)S(1)}, u32[]{:S(2)}, u32[]{:S(2)}) %collective-permute-start.6) | collective-permute-done | bytes 32800 | tf_op jit(solution)/shard_map/ppermute | solution.py:22
  87.0 4.4 %collective-permute-done.7 = bf16[1,2,2,2,16,128]{5,4,3,2,1,0:T(8,128)(2,1)S(1)} collective-permute-done((bf16[1,2,2,2,16,128]{5,4,3,2,1,0:T(8,128)(2,1)S(1)}, bf16[1,2,2,2,16,128]{5,4,3,2,1,0:T(8,128)(2,1)S(1)}, u32[]{:S(2)}, u32[]{:S(2)}) %collective-permute-start.7) | collective-permute-done | bytes 32800 | tf_op jit(solution)/shard_map/ppermute | solution.py:21
  91.6 0.8 fusion.13
  92.3 0.1 fusion.62
  92.4 0.1 reshape_squeeze.3
  92.7 12.6 %fusion = bf16[4,2,2,6,16,4,2,4,2,4]{4,3,9,7,5,0,1,8,6,2:T(8,128)(2,1)} fusion(bf16[4,2,2,6,32,4,2,4,2,4,1]{4,9,8,7,6,5,3,2,1,0,10:T(4,128)(2,1)} %bitcast.225, bf16[1,2,2,2,16,2,32]{6,4,1,0,2,3,5:T(8,128)(2,1)S(1)} %get-tuple-element.15, bf16[1,2,2,2,16,2,32]{6,4,1,0,2,3,5:T(8,128)(2,1)S(1)} %get-tuple-element.14), kind=kOutput, calls=%fused_computation.1 | convolution fusion | flops 50790400 | bytes 2392064 | tf_op jit(solution)/shard_map/tphgkxzayb,qpyzrhk->tqhgrxzayb/dot_general | solution.py:52
  105.3 9.5 %copy.50 = bf16[4,2,2,6,16,4,2,4,2,4]{4,9,8,7,6,5,3,2,1,0:T(4,128)(2,1)} copy(bf16[4,2,2,6,16,4,2,4,2,4]{4,3,9,7,5,0,1,8,6,2:T(8,128)(2,1)} %fusion) | data formatting | bytes 1572864 | tf_op jit(solution)/shard_map/convert_element_type | solution.py:55
  114.8 6.1 %copy.51 = bf16[4,2,12,16,256]{4,3,2,1,0:T(8,128)(2,1)} copy(bf16[4,2,12,16,256]{3,4,2,1,0:T(8,128)(2,1)} %bitcast.230) | data formatting | bytes 1572864
  (69 shorter events, 0.7 us)
Async XLA Ops:
  0.6 60.8 %copy-start = (bf16[1,9,2,2,2,128,128]{6,5,4,3,2,1,0:T(8,128)(2,1)S(1)}, bf16[1,9,2,2,2,128,128]{6,5,4,3,2,1,0:T(8,128)(2,1)}, u32[]{:S(2)}) copy-start(bf16[1,9,2,2,2,128,128]{6,5,4,3,2,1,0:T(8,128)(2,1)} %param.5) | copy-start | bytes 7077892
  0.6 6.5 %copy-start.3 = (bf16[4,2,12,16,256]{4,3,2,1,0:T(8,128)(2,1)S(1)}, bf16[4,2,12,16,256]{4,3,2,1,0:T(8,128)(2,1)}, u32[]{:S(2)}) copy-start(bf16[4,2,12,16,256]{4,3,2,1,0:T(8,128)(2,1)} %param.3) | copy-start | bytes 2359300
  11.6 8.0 %copy-start.1 = (bf16[4,2,12,32,256]{3,4,2,1,0:T(8,128)(2,1)S(1)}, bf16[4,2,12,32,256]{3,4,2,1,0:T(8,128)(2,1)}, u32[]{:S(2)}) copy-start(bf16[4,2,12,32,256]{3,4,2,1,0:T(8,128)(2,1)} %copy.24) | copy-start | bytes 4718596
  11.6 8.0 %copy-start.2 = (bf16[4,2,12,16,256]{3,4,2,1,0:T(8,128)(2,1)S(1)}, bf16[4,2,12,16,256]{3,4,2,1,0:T(8,128)(2,1)}, u32[]{:S(2)}) copy-start(bf16[4,2,12,16,256]{3,4,2,1,0:T(8,128)(2,1)} %copy.23) | copy-start | bytes 2359300
  55.2 6.1 %collective-permute-start.1 = (bf16[1,2,2,2,16,128]{5,4,3,2,1,0:T(8,128)(2,1)S(1)}, bf16[1,2,2,2,16,128]{5,4,3,2,1,0:T(8,128)(2,1)S(1)}, u32[]{:S(2)}, u32[]{:S(2)}) collective-permute-start(bf16[1,2,2,2,16,128]{5,4,3,2,1,0:T(8,128)(2,1)S(1)} %fusion.55), channel_id=1, source_target_pairs={{0,2},{2,4},{4,6},{6,8},{8,10},{10,12},{12,14},{14,16},{16,18},{18... | collective-permute-start | bytes 98312 | tf_op jit(solution)/shard_map/ppermute | solution.py:21
  55.3 6.0 %collective-permute-start = (bf16[1,2,2,2,16,128]{5,4,3,2,1,0:T(8,128)(2,1)S(1)}, bf16[1,2,2,2,16,128]{5,4,3,2,1,0:T(8,128)(2,1)S(1)}, u32[]{:S(2)}, u32[]{:S(2)}) collective-permute-start(bf16[1,2,2,2,16,128]{5,4,3,2,1,0:T(8,128)(2,1)S(1)} %fusion.55), channel_id=1, source_target_pairs={{2,0},{4,2},{6,4},{8,6},{10,8},{12,10},{14,12},{16,14},{18,16},{20... | collective-permute-start | bytes 98312 | tf_op jit(solution)/shard_map/ppermute | solution.py:22
  62.3 6.1 %collective-permute-start.2 = (bf16[1,2,2,2,16,128]{5,4,3,2,1,0:T(8,128)(2,1)S(1)}, bf16[1,2,2,2,16,128]{5,4,3,2,1,0:T(8,128)(2,1)S(1)}, u32[]{:S(2)}, u32[]{:S(2)}) collective-permute-start(bf16[1,2,2,2,16,128]{5,4,3,2,1,0:T(8,128)(2,1)S(1)} %get-tuple-element.9), channel_id=1, source_target_pairs={{2,0},{4,2},{6,4},{8,6},{10,8},{12,10},{14,12},{16,14},{18,16},{20... | collective-permute-start | bytes 98312 | tf_op jit(solution)/shard_map/ppermute | solution.py:22
  66.8 6.1 %collective-permute-start.3 = (bf16[1,2,2,2,16,128]{5,4,3,2,1,0:T(8,128)(2,1)S(1)}, bf16[1,2,2,2,16,128]{5,4,3,2,1,0:T(8,128)(2,1)S(1)}, u32[]{:S(2)}, u32[]{:S(2)}) collective-permute-start(bf16[1,2,2,2,16,128]{5,4,3,2,1,0:T(8,128)(2,1)S(1)} %get-tuple-element.9), channel_id=1, source_target_pairs={{0,2},{2,4},{4,6},{6,8},{8,10},{10,12},{12,14},{14,16},{16,18},{18... | collective-permute-start | bytes 98312 | tf_op jit(solution)/shard_map/ppermute | solution.py:21
  73.9 6.2 %collective-permute-start.5 = (bf16[1,2,2,2,16,128]{5,4,3,2,1,0:T(8,128)(2,1)S(1)}, bf16[1,2,2,2,16,128]{5,4,3,2,1,0:T(8,128)(2,1)S(1)}, u32[]{:S(2)}, u32[]{:S(2)}) collective-permute-start(bf16[1,2,2,2,16,128]{5,4,3,2,1,0:T(8,128)(2,1)S(1)} %get-tuple-element.6), channel_id=1, source_target_pairs={{0,2},{2,4},{4,6},{6,8},{8,10},{10,12},{12,14},{14,16},{16,18},{18... | collective-permute-start | bytes 98312 | tf_op jit(solution)/shard_map/ppermute | solution.py:21
  73.9 6.0 %collective-permute-start.4 = (bf16[1,2,2,2,16,128]{5,4,3,2,1,0:T(8,128)(2,1)S(1)}, bf16[1,2,2,2,16,128]{5,4,3,2,1,0:T(8,128)(2,1)S(1)}, u32[]{:S(2)}, u32[]{:S(2)}) collective-permute-start(bf16[1,2,2,2,16,128]{5,4,3,2,1,0:T(8,128)(2,1)S(1)} %get-tuple-element.6), channel_id=1, source_target_pairs={{2,0},{4,2},{6,4},{8,6},{10,8},{12,10},{14,12},{16,14},{18,16},{20... | collective-permute-start | bytes 98312 | tf_op jit(solution)/shard_map/ppermute | solution.py:22
  81.0 6.0 %collective-permute-start.6 = (bf16[1,2,2,2,16,128]{5,4,3,2,1,0:T(8,128)(2,1)S(1)}, bf16[1,2,2,2,16,128]{5,4,3,2,1,0:T(8,128)(2,1)S(1)}, u32[]{:S(2)}, u32[]{:S(2)}) collective-permute-start(bf16[1,2,2,2,16,128]{5,4,3,2,1,0:T(8,128)(2,1)S(1)} %get-tuple-element.5), channel_id=1, source_target_pairs={{2,0},{4,2},{6,4},{8,6},{10,8},{12,10},{14,12},{16,14},{18,16},{20... | collective-permute-start | bytes 98312 | tf_op jit(solution)/shard_map/ppermute | solution.py:22
  85.4 6.0 %collective-permute-start.7 = (bf16[1,2,2,2,16,128]{5,4,3,2,1,0:T(8,128)(2,1)S(1)}, bf16[1,2,2,2,16,128]{5,4,3,2,1,0:T(8,128)(2,1)S(1)}, u32[]{:S(2)}, u32[]{:S(2)}) collective-permute-start(bf16[1,2,2,2,16,128]{5,4,3,2,1,0:T(8,128)(2,1)S(1)} %get-tuple-element.5), channel_id=1, source_target_pairs={{0,2},{2,4},{4,6},{6,8},{8,10},{10,12},{12,14},{14,16},{16,18},{18... | collective-permute-start | bytes 98312 | tf_op jit(solution)/shard_map/ppermute | solution.py:21
  92.4 12.9 %copy-start.4 = (bf16[1,2,2,2,16,128]{5,4,3,2,1,0:T(8,128)(2,1)}, bf16[1,2,2,2,16,128]{5,4,3,2,1,0:T(8,128)(2,1)S(1)}, u32[]{:S(2)}) copy-start(bf16[1,2,2,2,16,128]{5,4,3,2,1,0:T(8,128)(2,1)S(1)} %fusion.62) | copy-start | bytes 98308
where the time goes:
time: 121 us
  local copies, waits for them, and re-layouts  39.1 us (32%)
  matrix products  38.8 us (32%)
  starting transfers between devices  17.9 us (15%)
  waiting for transfers between devices  15.4 us (13%)
  blocking collectives  5.52 us (5%)
  other arithmetic  3.23 us (3%)
    unnamed x22, local copies, waits for them, and re-layouts  21.3 us
    ppermute x4, starting transfers between devices, padded_2(): after = lax.ppermute(initial, axis, down)  17.8 us
    dot_general x1, matrix products, local_restrict(): jnp.einsum('tqhgkxzayb,tqhgrxzayb->yzrhk', null_view, turned, preferred_e...  16 us
    dot_general x1, matrix products, local_prolong(): jnp.einsum('tphgkxzayb,qpyzrhk->tqhgrxzayb', null_view, mixer, preferred_...  12.6 us
    convert_element_type x1, local copies, waits for them, and re-layouts, local_prolong(): result.reshape(4, 2, 12, rhs_count, 4 * depth * 16 * coarse_y)  9.5 us
    ppermute x4, waiting for transfers between devices, padded_2(): before = lax.ppermute(last, axis, up)  9.06 us
    slice x1, local copies, waits for them, and re-layouts, local_restrict(): turned = jnp.stack([fine_view[:, 1], -fine_view[:, 0]], axis=1)  7.95 us
    dot_general x1, matrix products, local_restrict(): jnp.einsum('tqhgkxzayb,tqhgrxzayb->yzrhk', null_view, fine_view, preferre...  7.08 us
  transfers between devices with their start and end apart: 8, of which 7 were waited for; matrix products, arithmetic and copies ran while one was open for 0% of the time, Pallas kernels for 0%

commit v1 on v0

v1 whole, which is shorter than its diff:
```python
import functools

import jax
import jax.numpy as jnp
from jax import lax
from jax.experimental import pallas as pl
from jax.experimental.pallas import tpu as pltpu
from jax.sharding import PartitionSpec as P

CZ = 2
APPLIES = 4
RELAX_WEIGHT = 0.3
DIAGONAL_SHIFT = 3.0
LANES = (((1,), (1,)), ((), ()))


def aggregate_ids(shape, coarse_y):
    site = lax.broadcasted_iota(jnp.int32, shape, len(shape) - 1)
    row = 4 * coarse_y
    y = lax.rem(site, row) // 4
    z = lax.rem(site, row * 4 * CZ) // (row * 4)
    return y * CZ + z


def restrict_kernel(coarse_y, fine_ref, null_ref, out_ref, sums):
    step = pl.program_id(0)
    aggregates = coarse_y * CZ
    rhs, sites = fine_ref.shape[3:]
    vectors = null_ref.shape[3]
    ids = aggregate_ids((2 * rhs, sites), coarse_y)
    masks = [(ids == a).astype(jnp.float32).astype(jnp.bfloat16) for a in range(aggregates)]

    @pl.when(step == 0)
    def _():
        sums[...] = jnp.zeros_like(sums)

    for h in range(2):
        left, right = [], []
        for g in range(6):
            c = h * 6 + g
            fine = jnp.concatenate([fine_ref[0, 0, c], fine_ref[0, 1, c]], axis=0)
            left.append(jnp.concatenate([fine * m for m in masks], axis=0))
            right.append(jnp.concatenate([null_ref[0, 0, c], null_ref[0, 1, c]], axis=0))
        sums[h] += lax.dot_general(
            jnp.concatenate(left, axis=1),
            jnp.concatenate(right, axis=1),
            LANES,
            preferred_element_type=jnp.float32,
        )

    @pl.when(step == pl.num_programs(0) - 1)
    def _():
        for a in range(aggregates):
            real, imag = [], []
            for h in range(2):
                top = sums[h, a * 2 * rhs : a * 2 * rhs + rhs]
                low = sums[h, a * 2 * rhs + rhs : (a + 1) * 2 * rhs]
                real.append(top[:, :vectors] + low[:, vectors:])
                imag.append(low[:, :vectors] - top[:, vectors:])
            out_ref[a] = jnp.concatenate(real + imag, axis=1).astype(out_ref.dtype)


def restrict(fine, null):
    times, _, _, rhs, sites = fine.shape
    vectors = null.shape[3]
    coarse_y = sites // (64 * CZ)
    aggregates = coarse_y * CZ
    return pl.pallas_call(
        functools.partial(restrict_kernel, coarse_y),
        grid=(times,),
        in_specs=[
            pl.BlockSpec((1, 2, 12, rhs, sites), lambda t: (t, 0, 0, 0, 0)),
            pl.BlockSpec((1, 2, 12, vectors, sites), lambda t: (t, 0, 0, 0, 0)),
        ],
        out_specs=pl.BlockSpec((aggregates, rhs, 4 * vectors), lambda t: (0, 0, 0)),
        out_shape=jax.ShapeDtypeStruct((aggregates, rhs, 4 * vectors), jnp.bfloat16),
        scratch_shapes=[pltpu.VMEM((2, aggregates * 2 * rhs, 2 * vectors), jnp.float32)],
        name="restrict",
    )(fine, null)


def prolong_kernel(coarse_y, coarse_ref, null_ref, out_ref):
    aggregates = coarse_y * CZ
    rhs, sites = out_ref.shape[3:]
    vectors = null_ref.shape[3]
    ids = aggregate_ids((2 * rhs, sites), coarse_y)
    masks = [ids == a for a in range(aggregates)]
    for h in range(2):
        mixer = []
        for a in range(aggregates):
            weights = coarse_ref[a]
            real = weights[:, h * vectors : (h + 1) * vectors]
            imag = weights[:, (2 + h) * vectors : (3 + h) * vectors]
            mixer.append(jnp.concatenate([real, -imag], axis=1))
            mixer.append(jnp.concatenate([imag, real], axis=1))
        mixer = jnp.concatenate(mixer, axis=0)
        for g in range(6):
            c = h * 6 + g
            null = jnp.concatenate([null_ref[0, 0, c], null_ref[0, 1, c]], axis=0)
            every = jnp.dot(mixer, null, preferred_element_type=jnp.float32)
            result = every[: 2 * rhs]
            for a in range(1, aggregates):
                result = jnp.where(masks[a], every[a * 2 * rhs : (a + 1) * 2 * rhs], result)
            result = result.astype(out_ref.dtype)
            out_ref[0, 0, c] = result[:rhs]
            out_ref[0, 1, c] = result[rhs:]


def prolong(coarse, null):
    aggregates, rhs, _ = coarse.shape
    times, _, _, vectors, sites = null.shape
    return pl.pallas_call(
        functools.partial(prolong_kernel, aggregates // CZ),
        grid=(times,),
        in_specs=[
            pl.BlockSpec(coarse.shape, lambda t: (0, 0, 0)),
            pl.BlockSpec((1, 2, 12, vectors, sites), lambda t: (t, 0, 0, 0, 0)),
        ],
        out_specs=pl.BlockSpec((1, 2, 12, rhs, sites), lambda t: (t, 0, 0, 0, 0)),
        out_shape=jax.ShapeDtypeStruct((times, 2, 12, rhs, sites), jnp.bfloat16),
        name="prolong",
    )(coarse, null)


def padded_2(array, sides, width):
    for axis, dim in sides:
        devices, length = (lax.axis_size(axis), array.shape[dim])
        up = [(i, (i + 1) % devices) for i in range(devices)]
        down = [(j, i) for i, j in up]
        last = lax.slice_in_dim(array, length - width, length, axis=dim)
        initial = lax.slice_in_dim(array, 0, width, axis=dim)
        before = lax.ppermute(last, axis, up)
        after = lax.ppermute(initial, axis, down)
        array = jnp.concatenate([before, array, after], axis=dim)
    return array


def stencil_product(field, shifted, operator_block):
    stacked = jnp.stack(shifted, axis=1)
    image = jnp.einsum(
        "tdyzxij,tdyzxrj->tyzxri", operator_block, stacked, preferred_element_type=jnp.float32
    )
    return image + DIAGONAL_SHIFT * field.astype(jnp.float32)


def apply_whole(field, operator_block):
    padded = padded_2(field, (("zt", 0),), 1)
    shifted = [
        field,
        padded[2:],
        padded[:-2],
        jnp.roll(field, -1, 1),
        jnp.roll(field, 1, 1),
        jnp.roll(field, -1, 2),
        jnp.roll(field, 1, 2),
        jnp.roll(field, -1, 3),
        jnp.roll(field, 1, 3),
    ]
    return stencil_product(field, shifted, operator_block)


def per_device(fine_vectors, null_vectors, coarse_operator):
    position = lax.axis_index("xy")
    sums = restrict(fine_vectors, null_vectors)
    aggregates, rhs, columns = sums.shape
    coarse_rhs = sums.reshape(1, aggregates // CZ, CZ, 1, rhs, columns)
    whole_rhs = lax.all_gather(coarse_rhs, "xy", axis=3, tiled=True)
    target = whole_rhs.astype(jnp.float32)
    iterate = RELAX_WEIGHT * target
    for sweep_index in range(APPLIES):
        image = apply_whole(iterate.astype(jnp.bfloat16), coarse_operator)
        iterate = iterate + RELAX_WEIGHT * (target - image)
    coarse_iterate = iterate.astype(jnp.bfloat16)
    column = lax.dynamic_slice_in_dim(coarse_iterate, position, 1, 3)
    fine_correction = prolong(column.reshape(sums.shape), null_vectors)
    return (fine_correction, coarse_iterate)


def solution(mesh):
    return jax.shard_map(
        per_device,
        mesh=mesh,
        in_specs=(
            P("zt", None, None, None, "xy"),
            P("zt", None, None, None, "xy"),
            P("zt", None, None, None, None, None, None),
        ),
        out_specs=(P("zt", None, None, None, "xy"), P("zt", None, None, None, None, None)),
        check_vma=False,
    )
```

time: 121 us -> 47 us (0.39)
  local copies, waits for them, and re-layouts: 39.1 us -> 0.74 us
  matrix products: 38.8 us -> 3.12 us
  starting transfers between devices: 17.9 us -> 4.99 us
  Pallas kernels: 0 us -> 8.44 us
  waiting for transfers between devices: 15.4 us -> 22.7 us
  other arithmetic: 3.23 us -> 0.42 us
    dot_general x3 -> x0, matrix products: 35.7 us -> none  [the longest x1 16 us: local_restrict(): jnp.einsum('tqhgkxzayb,tqhgrxzayb->yzrhk', null_view, turned, preferred_e...]
    unnamed x22 -> x12, local copies, waits for them, and re-layouts: 21.3 us -> 0.09 us
    ppermute x4, starting transfers between devices: 17.8 us -> 3.51 us  [padded_2(): after = lax.ppermute(initial, axis, down)]
    convert_element_type x2 -> x0, local copies, waits for them, and re-layouts: 9.59 us -> none  [the longest x1 9.5 us: local_prolong(): result.reshape(4, 2, 12, rhs_count, 4 * depth * 16 * coarse_y)]
    ppermute x4, waiting for transfers between devices: 9.06 us -> 17.9 us  [padded_2(): before = lax.ppermute(last, axis, up)]
    pallas_call x0 -> x2, Pallas kernels: none -> 8.44 us  [the longest x1 4.25 us: restrict(): pl.pallas_call(functools.partial(restrict_kernel, coarse_y), grid=(times,...]
    slice x2 -> x0, local copies, waits for them, and re-layouts: 8 us -> none  [the longest x1 7.95 us: local_restrict(): turned = jnp.stack([fine_view[:, 1], -fine_view[:, 0]], axis=1)]
    neg x2 -> x0, other arithmetic: 2.76 us -> none  [the longest x1 2.75 us: local_restrict(): turned = jnp.stack([fine_view[:, 1], -fine_view[:, 0]], axis=1)]
  transfers between devices with their start and end apart: 8 -> 8, of which waited for: 7 -> 8; matrix products, arithmetic and copies ran while one was open for 0% -> 0% of each run, Pallas kernels for 0% -> 0%
where the time goes in v1:
time: 47 us; the launch traced here: 46.8 us
  waiting for transfers between devices  22.7 us (48%)
  Pallas kernels  8.44 us (18%)
  blocking collectives  5.6 us (12%)
  starting transfers between devices  4.99 us (11%)
  matrix products  3.12 us (7%)
  between operations  0.86 us (2%)
  local copies, waits for them, and re-layouts  0.74 us (2%)
    ppermute x4, waiting for transfers between devices, padded_2(): before = lax.ppermute(last, axis, up)  17.9 us
    all_gather x1, blocking collectives, per_device(): whole_rhs = lax.all_gather(coarse_rhs, 'xy', axis=3, tiled=True)  5.6 us
    ppermute x4, waiting for transfers between devices, padded_2(): after = lax.ppermute(initial, axis, down)  4.78 us
    pallas_call x1, Pallas kernels, restrict(): pl.pallas_call(functools.partial(restrict_kernel, coarse_y), grid=(times,...  4.25 us
    pallas_call x1, Pallas kernels, prolong(): pl.pallas_call(functools.partial(prolong_kernel, aggregates // CZ), grid=...  4.19 us
    ppermute x4, starting transfers between devices, padded_2(): after = lax.ppermute(initial, axis, down)  3.51 us
    dot_general x4, matrix products, stencil_product(): jnp.einsum('tdyzxij,tdyzxrj->tyzxri', operator_block, stacked, preferred_...  3.12 us
    ppermute x4, starting transfers between devices, padded_2(): before = lax.ppermute(last, axis, up)  1.48 us
  transfers between devices with their start and end apart: 8, of which 8 were waited for; matrix products, arithmetic and copies ran while one was open for 0% of the time, Pallas kernels for 0%

profile of v1, /device:TPU:0, one launch (start us, length us, event | category | flops | bytes accessed | tf_op | source)
XLA Modules:
  0.0 46.8 jit_solution(6694057708070452461)
XLA Ops:
  0.6 0.0 copy-start
  0.6 4.3 %restrict.1 = bf16[4,16,128]{2,1,0:T(8,128)(2,1)} custom-call(bf16[4,2,12,16,256]{4,3,2,1,0:T(8,128)(2,1)} %fine_ref.1, bf16[4,2,12,32,256]{4,3,2,1,0:T(8,128)(2,1)} %null_ref.3), custom_call_target="tpu_custom_call" | custom-call | tf_op jit(solution)/shard_map/restrict/pallas_call | solution.py:68
  4.9 5.6 %all_gather.3 = bf16[1,2,2,2,16,128]{5,4,3,2,1,0:T(8,128)(2,1)S(1)} all-gather(bf16[1,2,2,1,16,128]{5,4,3,2,1,0:T(8,128)(2,1)} %bitcast.175), channel_id=1, replica_groups=mesh['zt'=16,'xy'=2] {'xy'}, dimensions={3}, use_global_device_ids=true | all-gather | bytes 49152 | tf_op jit(solution)/shard_map/all_gather | solution.py:167
  10.5 3.3 %collective-permute-start = (bf16[1,2,2,2,16,128]{5,4,3,2,1,0:T(8,128)(2,1)S(1)}, bf16[1,2,2,2,16,128]{5,4,3,2,1,0:T(8,128)(2,1)S(1)}, u32[]{:S(2)}, u32[]{:S(2)}) collective-permute-start(bf16[1,2,2,2,16,128]{5,4,3,2,1,0:T(8,128)(2,1)S(1)} %fusion.27), channel_id=1, source_target_pairs={{2,0},{4,2},{6,4},{8,6},{10,8},{12,10},{14,12},{16,14},{18,16},{20... | collective-permute-start | bytes 98312 | tf_op jit(solution)/shard_map/ppermute | solution.py:133
  13.8 0.0 collective-permute-start.1
  13.9 1.5 %collective-permute-done = bf16[1,2,2,2,16,128]{5,4,3,2,1,0:T(8,128)(2,1)S(1)} collective-permute-done((bf16[1,2,2,2,16,128]{5,4,3,2,1,0:T(8,128)(2,1)S(1)}, bf16[1,2,2,2,16,128]{5,4,3,2,1,0:T(8,128)(2,1)S(1)}, u32[]{:S(2)}, u32[]{:S(2)}) %collective-permute-start) | collective-permute-done | bytes 32800 | tf_op jit(solution)/shard_map/ppermute | solution.py:133
  15.5 4.4 %collective-permute-done.1 = bf16[1,2,2,2,16,128]{5,4,3,2,1,0:T(8,128)(2,1)S(1)} collective-permute-done((bf16[1,2,2,2,16,128]{5,4,3,2,1,0:T(8,128)(2,1)S(1)}, bf16[1,2,2,2,16,128]{5,4,3,2,1,0:T(8,128)(2,1)S(1)}, u32[]{:S(2)}, u32[]{:S(2)}) %collective-permute-start.1) | collective-permute-done | bytes 32800 | tf_op jit(solution)/shard_map/ppermute | solution.py:132
  20.0 0.0 copy-done
  20.0 0.8 %constant_dynamic-update-slice_fusion.17 = (bf16[1,9,2,2,2,16,128]{6,5,4,3,2,1,0:T(8,128)(2,1)S(1)}, bf16[1,2,2,2,16,128]{5,4,3,2,1,0:T(8,128)(2,1)S(1)}, f32[1,2,2,2,16,128]{5,4,3,2,1,0:T(8,128)S(1)}) fusion(bf16[1,9,2,2,2,16,128]{6,5,1,4,3,2,0:T(8,128)(2,1)S(1)} %constant_dynamic-update-slice_fusion, bf16[1,2,2,2,16,128]{5,4,3,2,1,0:T(8,128)(2,1)S(1)} %all_gather.3, ...), kind=kOutput, calls=%fused_computation.39 | convolution fusion | flops 37912576 | bytes 2818048 | tf_op jit(solution)/shard_map/tdyzxij,tdyzxrj->tyzxri/dot_general | solution.py:140
  20.8 0.1 collective-permute-start.2
  20.8 0.5 %collective-permute-start.3 = (bf16[1,2,2,2,16,128]{5,4,3,2,1,0:T(8,128)(2,1)S(1)}, bf16[1,2,2,2,16,128]{5,4,3,2,1,0:T(8,128)(2,1)S(1)}, u32[]{:S(2)}, u32[]{:S(2)}) collective-permute-start(bf16[1,2,2,2,16,128]{5,4,3,2,1,0:T(8,128)(2,1)S(1)} %get-tuple-element.7), channel_id=1, source_target_pairs={{0,2},{2,4},{4,6},{6,8},{8,10},{10,12},{12,14},{14,16},{16,18},{18... | collective-permute-start | bytes 98312 | tf_op jit(solution)/shard_map/ppermute | solution.py:132
  21.3 1.1 %collective-permute-done.2 = bf16[1,2,2,2,16,128]{5,4,3,2,1,0:T(8,128)(2,1)S(1)} collective-permute-done((bf16[1,2,2,2,16,128]{5,4,3,2,1,0:T(8,128)(2,1)S(1)}, bf16[1,2,2,2,16,128]{5,4,3,2,1,0:T(8,128)(2,1)S(1)}, u32[]{:S(2)}, u32[]{:S(2)}) %collective-permute-start.2) | collective-permute-done | bytes 32800 | tf_op jit(solution)/shard_map/ppermute | solution.py:133
  22.4 4.5 %collective-permute-done.3 = bf16[1,2,2,2,16,128]{5,4,3,2,1,0:T(8,128)(2,1)S(1)} collective-permute-done((bf16[1,2,2,2,16,128]{5,4,3,2,1,0:T(8,128)(2,1)S(1)}, bf16[1,2,2,2,16,128]{5,4,3,2,1,0:T(8,128)(2,1)S(1)}, u32[]{:S(2)}, u32[]{:S(2)}) %collective-permute-start.3) | collective-permute-done | bytes 32800 | tf_op jit(solution)/shard_map/ppermute | solution.py:132
  27.0 0.8 %fusion.6 = f32[2,2,2,16,128,1]{4,3,0,2,1,5:T(8,128)S(1)} fusion(bf16[1,9,2,2,2,128,128]{6,5,4,3,2,1,0:T(8,128)(2,1)S(1)} %copy-done, bf16[1,9,2,2,2,16,128]{6,5,4,3,2,1,0:T(8,128)(2,1)S(1)} %constant_dynamic-update-slice_fusion.9), kind=kOutput, calls=%fused_computation.6 | convolution fusion | flops 37748736 | bytes 2719744 | tf_op jit(solution)/shard_map/tdyzxij,tdyzxrj->tyzxri/dot_general | solution.py:140
  27.8 0.1 collective-permute-start.4
  27.9 0.5 %collective-permute-start.5 = (bf16[1,2,2,2,16,128]{5,4,3,2,1,0:T(8,128)(2,1)S(1)}, bf16[1,2,2,2,16,128]{5,4,3,2,1,0:T(8,128)(2,1)S(1)}, u32[]{:S(2)}, u32[]{:S(2)}) collective-permute-start(bf16[1,2,2,2,16,128]{5,4,3,2,1,0:T(8,128)(2,1)S(1)} %get-tuple-element.4), channel_id=1, source_target_pairs={{0,2},{2,4},{4,6},{6,8},{8,10},{10,12},{12,14},{14,16},{16,18},{18... | collective-permute-start | bytes 98312 | tf_op jit(solution)/shard_map/ppermute | solution.py:132
  28.4 1.1 %collective-permute-done.4 = bf16[1,2,2,2,16,128]{5,4,3,2,1,0:T(8,128)(2,1)S(1)} collective-permute-done((bf16[1,2,2,2,16,128]{5,4,3,2,1,0:T(8,128)(2,1)S(1)}, bf16[1,2,2,2,16,128]{5,4,3,2,1,0:T(8,128)(2,1)S(1)}, u32[]{:S(2)}, u32[]{:S(2)}) %collective-permute-start.4) | collective-permute-done | bytes 32800 | tf_op jit(solution)/shard_map/ppermute | solution.py:133
  29.5 4.5 %collective-permute-done.5 = bf16[1,2,2,2,16,128]{5,4,3,2,1,0:T(8,128)(2,1)S(1)} collective-permute-done((bf16[1,2,2,2,16,128]{5,4,3,2,1,0:T(8,128)(2,1)S(1)}, bf16[1,2,2,2,16,128]{5,4,3,2,1,0:T(8,128)(2,1)S(1)}, u32[]{:S(2)}, u32[]{:S(2)}) %collective-permute-start.5) | collective-permute-done | bytes 32800 | tf_op jit(solution)/shard_map/ppermute | solution.py:132
  34.1 0.8 %fusion.4 = f32[2,2,2,16,128,1]{4,3,0,2,1,5:T(8,128)S(1)} fusion(bf16[1,9,2,2,2,128,128]{6,5,4,3,2,1,0:T(8,128)(2,1)S(1)} %copy-done, bf16[1,9,2,2,2,16,128]{6,5,4,3,2,1,0:T(8,128)(2,1)S(1)} %constant_dynamic-update-slice_fusion.18), kind=kOutput, calls=%fused_computation.4 | convolution fusion | flops 37748736 | bytes 2719744 | tf_op jit(solution)/shard_map/tdyzxij,tdyzxrj->tyzxri/dot_general | solution.py:140
  34.9 0.1 collective-permute-start.6
  35.0 0.5 %collective-permute-start.7 = (bf16[1,2,2,2,16,128]{5,4,3,2,1,0:T(8,128)(2,1)S(1)}, bf16[1,2,2,2,16,128]{5,4,3,2,1,0:T(8,128)(2,1)S(1)}, u32[]{:S(2)}, u32[]{:S(2)}) collective-permute-start(bf16[1,2,2,2,16,128]{5,4,3,2,1,0:T(8,128)(2,1)S(1)} %get-tuple-element.3), channel_id=1, source_target_pairs={{0,2},{2,4},{4,6},{6,8},{8,10},{10,12},{12,14},{14,16},{16,18},{18... | collective-permute-start | bytes 98312 | tf_op jit(solution)/shard_map/ppermute | solution.py:132
  35.5 1.1 %collective-permute-done.6 = bf16[1,2,2,2,16,128]{5,4,3,2,1,0:T(8,128)(2,1)S(1)} collective-permute-done((bf16[1,2,2,2,16,128]{5,4,3,2,1,0:T(8,128)(2,1)S(1)}, bf16[1,2,2,2,16,128]{5,4,3,2,1,0:T(8,128)(2,1)S(1)}, u32[]{:S(2)}, u32[]{:S(2)}) %collective-permute-start.6) | collective-permute-done | bytes 32800 | tf_op jit(solution)/shard_map/ppermute | solution.py:133
  36.6 4.5 %collective-permute-done.7 = bf16[1,2,2,2,16,128]{5,4,3,2,1,0:T(8,128)(2,1)S(1)} collective-permute-done((bf16[1,2,2,2,16,128]{5,4,3,2,1,0:T(8,128)(2,1)S(1)}, bf16[1,2,2,2,16,128]{5,4,3,2,1,0:T(8,128)(2,1)S(1)}, u32[]{:S(2)}, u32[]{:S(2)}) %collective-permute-start.7) | collective-permute-done | bytes 32800 | tf_op jit(solution)/shard_map/ppermute | solution.py:132
  41.2 0.8 %fusion.2 = f32[2,2,2,16,128,1]{4,3,0,2,1,5:T(8,128)S(1)} fusion(bf16[1,9,2,2,2,128,128]{6,5,4,3,2,1,0:T(8,128)(2,1)S(1)} %copy-done, bf16[1,9,2,2,2,16,128]{6,5,4,3,2,1,0:T(8,128)(2,1)S(1)} %constant_dynamic-update-slice_fusion.27), kind=kOutput, calls=%fused_computation.2 | convolution fusion | flops 37748736 | bytes 2719744 | tf_op jit(solution)/shard_map/tdyzxij,tdyzxrj->tyzxri/dot_general | solution.py:140
  42.0 0.1 fusion.34
  42.0 0.0 copy-start.1
  42.0 0.6 %constant_dynamic-slice_fusion = bf16[1,2,2,1,16,128]{5,4,3,2,1,0:T(8,128)(2,1)} fusion(bf16[1,2,2,2,16,128]{5,4,3,2,1,0:T(8,128)(2,1)S(1)} %fusion.34, s32[]{:T(128)S(6)} %select_n.3), kind=kLoop, calls=%fused_computation.80 | loop fusion | bytes 32772 | tf_op jit(solution)/shard_map/dynamic_slice | solution.py:174
  42.6 4.2 %prolong.1 = bf16[4,2,12,16,256]{4,3,2,1,0:T(8,128)(2,1)} custom-call(bf16[4,16,128]{2,1,0:T(8,128)(2,1)} %bitcast.176, bf16[4,2,12,32,256]{4,3,2,1,0:T(8,128)(2,1)} %null_ref.3), custom_call_target="tpu_custom_call" | custom-call | tf_op jit(solution)/shard_map/prolong/pallas_call | solution.py:112
  46.8 0.0 copy-done.1
  (49 shorter events, 0.5 us)
Async XLA Ops:
  0.6 19.4 %copy-start = (bf16[1,9,2,2,2,128,128]{6,5,4,3,2,1,0:T(8,128)(2,1)S(1)}, bf16[1,9,2,2,2,128,128]{6,5,4,3,2,1,0:T(8,128)(2,1)}, u32[]{:S(2)}) copy-start(bf16[1,9,2,2,2,128,128]{6,5,4,3,2,1,0:T(8,128)(2,1)} %param.5) | copy-start | bytes 7077892
  10.5 4.9 %collective-permute-start = (bf16[1,2,2,2,16,128]{5,4,3,2,1,0:T(8,128)(2,1)S(1)}, bf16[1,2,2,2,16,128]{5,4,3,2,1,0:T(8,128)(2,1)S(1)}, u32[]{:S(2)}, u32[]{:S(2)}) collective-permute-start(bf16[1,2,2,2,16,128]{5,4,3,2,1,0:T(8,128)(2,1)S(1)} %fusion.27), channel_id=1, source_target_pairs={{2,0},{4,2},{6,4},{8,6},{10,8},{12,10},{14,12},{16,14},{18,16},{20... | collective-permute-start | bytes 98312 | tf_op jit(solution)/shard_map/ppermute | solution.py:133
  13.8 6.0 %collective-permute-start.1 = (bf16[1,2,2,2,16,128]{5,4,3,2,1,0:T(8,128)(2,1)S(1)}, bf16[1,2,2,2,16,128]{5,4,3,2,1,0:T(8,128)(2,1)S(1)}, u32[]{:S(2)}, u32[]{:S(2)}) collective-permute-start(bf16[1,2,2,2,16,128]{5,4,3,2,1,0:T(8,128)(2,1)S(1)} %fusion.27), channel_id=1, source_target_pairs={{0,2},{2,4},{4,6},{6,8},{8,10},{10,12},{12,14},{14,16},{16,18},{18... | collective-permute-start | bytes 98312 | tf_op jit(solution)/shard_map/ppermute | solution.py:132
  20.8 1.7 %collective-permute-start.2 = (bf16[1,2,2,2,16,128]{5,4,3,2,1,0:T(8,128)(2,1)S(1)}, bf16[1,2,2,2,16,128]{5,4,3,2,1,0:T(8,128)(2,1)S(1)}, u32[]{:S(2)}, u32[]{:S(2)}) collective-permute-start(bf16[1,2,2,2,16,128]{5,4,3,2,1,0:T(8,128)(2,1)S(1)} %get-tuple-element.7), channel_id=1, source_target_pairs={{2,0},{4,2},{6,4},{8,6},{10,8},{12,10},{14,12},{16,14},{18,16},{20... | collective-permute-start | bytes 98312 | tf_op jit(solution)/shard_map/ppermute | solution.py:133
  20.8 6.1 %collective-permute-start.3 = (bf16[1,2,2,2,16,128]{5,4,3,2,1,0:T(8,128)(2,1)S(1)}, bf16[1,2,2,2,16,128]{5,4,3,2,1,0:T(8,128)(2,1)S(1)}, u32[]{:S(2)}, u32[]{:S(2)}) collective-permute-start(bf16[1,2,2,2,16,128]{5,4,3,2,1,0:T(8,128)(2,1)S(1)} %get-tuple-element.7), channel_id=1, source_target_pairs={{0,2},{2,4},{4,6},{6,8},{8,10},{10,12},{12,14},{14,16},{16,18},{18... | collective-permute-start | bytes 98312 | tf_op jit(solution)/shard_map/ppermute | solution.py:132
  27.8 1.7 %collective-permute-start.4 = (bf16[1,2,2,2,16,128]{5,4,3,2,1,0:T(8,128)(2,1)S(1)}, bf16[1,2,2,2,16,128]{5,4,3,2,1,0:T(8,128)(2,1)S(1)}, u32[]{:S(2)}, u32[]{:S(2)}) collective-permute-start(bf16[1,2,2,2,16,128]{5,4,3,2,1,0:T(8,128)(2,1)S(1)} %get-tuple-element.4), channel_id=1, source_target_pairs={{2,0},{4,2},{6,4},{8,6},{10,8},{12,10},{14,12},{16,14},{18,16},{20... | collective-permute-start | bytes 98312 | tf_op jit(solution)/shard_map/ppermute | solution.py:133
  27.9 6.1 %collective-permute-start.5 = (bf16[1,2,2,2,16,128]{5,4,3,2,1,0:T(8,128)(2,1)S(1)}, bf16[1,2,2,2,16,128]{5,4,3,2,1,0:T(8,128)(2,1)S(1)}, u32[]{:S(2)}, u32[]{:S(2)}) collective-permute-start(bf16[1,2,2,2,16,128]{5,4,3,2,1,0:T(8,128)(2,1)S(1)} %get-tuple-element.4), channel_id=1, source_target_pairs={{0,2},{2,4},{4,6},{6,8},{8,10},{10,12},{12,14},{14,16},{16,18},{18... | collective-permute-start | bytes 98312 | tf_op jit(solution)/shard_map/ppermute | solution.py:132
  34.9 1.7 %collective-permute-start.6 = (bf16[1,2,2,2,16,128]{5,4,3,2,1,0:T(8,128)(2,1)S(1)}, bf16[1,2,2,2,16,128]{5,4,3,2,1,0:T(8,128)(2,1)S(1)}, u32[]{:S(2)}, u32[]{:S(2)}) collective-permute-start(bf16[1,2,2,2,16,128]{5,4,3,2,1,0:T(8,128)(2,1)S(1)} %get-tuple-element.3), channel_id=1, source_target_pairs={{2,0},{4,2},{6,4},{8,6},{10,8},{12,10},{14,12},{16,14},{18,16},{20... | collective-permute-start | bytes 98312 | tf_op jit(solution)/shard_map/ppermute | solution.py:133
  35.0 6.1 %collective-permute-start.7 = (bf16[1,2,2,2,16,128]{5,4,3,2,1,0:T(8,128)(2,1)S(1)}, bf16[1,2,2,2,16,128]{5,4,3,2,1,0:T(8,128)(2,1)S(1)}, u32[]{:S(2)}, u32[]{:S(2)}) collective-permute-start(bf16[1,2,2,2,16,128]{5,4,3,2,1,0:T(8,128)(2,1)S(1)} %get-tuple-element.3), channel_id=1, source_target_pairs={{0,2},{2,4},{4,6},{6,8},{8,10},{10,12},{12,14},{14,16},{16,18},{18... | collective-permute-start | bytes 98312 | tf_op jit(solution)/shard_map/ppermute | solution.py:132
  42.0 4.8 %copy-start.1 = (bf16[1,2,2,2,16,128]{5,4,3,2,1,0:T(8,128)(2,1)}, bf16[1,2,2,2,16,128]{5,4,3,2,1,0:T(8,128)(2,1)S(1)}, u32[]{:S(2)}) copy-start(bf16[1,2,2,2,16,128]{5,4,3,2,1,0:T(8,128)(2,1)S(1)} %fusion.34) | copy-start | bytes 98308

commit v2 on v1

v2 whole, which is shorter than its diff:
```python
import functools

import jax
import jax.numpy as jnp
from jax import lax
from jax.experimental import pallas as pl
from jax.experimental.pallas import tpu as pltpu
from jax.sharding import PartitionSpec as P

CZ = 2
APPLIES = 4
RELAX_WEIGHT = 0.3
DIAGONAL_SHIFT = 3.0
LANES = (((1,), (1,)), ((), ()))
KERNEL_VMEM = 16 * 1024 * 1024


def aggregate_ids(shape, coarse_y):
    site = lax.broadcasted_iota(jnp.int32, shape, len(shape) - 1)
    row = 4 * coarse_y
    y = lax.rem(site, row) // 4
    z = lax.rem(site, row * 4 * CZ) // (row * 4)
    return y * CZ + z


def restrict_kernel(coarse_y, fine_hbm, null_hbm, operator, out_ref, null_ref, block, fine_ref, loaded):
    aggregates = coarse_y * CZ
    times, _, _, rhs, sites = fine_ref.shape
    vectors = null_ref.shape[3]
    _, odd = time_sides(True)
    loads = []
    for t in range(times):
        loads.append(pltpu.make_async_copy(fine_hbm.at[t], fine_ref.at[t], loaded.at[2 * t]))
        loads.append(pltpu.make_async_copy(null_hbm.at[t], null_ref.at[t], loaded.at[2 * t + 1]))
    loads.append(pltpu.make_async_copy(operator.at[0, odd], block, loaded.at[2 * times]))
    for load in loads:
        load.start()
    ids = aggregate_ids((2 * rhs, sites), coarse_y)
    masks = [(ids == a).astype(jnp.float32).astype(jnp.bfloat16) for a in range(aggregates)]
    sums = [None, None]
    for t in range(times):
        loads[2 * t].wait()
        loads[2 * t + 1].wait()
        for h in range(2):
            left, right = [], []
            for c in range(h * 6, h * 6 + 6):
                fine = jnp.concatenate([fine_ref[t, 0, c], fine_ref[t, 1, c]], axis=0)
                left.append(jnp.concatenate([fine * m for m in masks], axis=0))
                right.append(jnp.concatenate([null_ref[t, 0, c], null_ref[t, 1, c]], axis=0))
            part = lax.dot_general(
                jnp.concatenate(left, axis=1),
                jnp.concatenate(right, axis=1),
                LANES,
                preferred_element_type=jnp.float32,
            )
            sums[h] = part if sums[h] is None else sums[h] + part
    for a in range(aggregates):
        real, imag = [], []
        for h in range(2):
            top = sums[h][a * 2 * rhs : a * 2 * rhs + rhs]
            low = sums[h][a * 2 * rhs + rhs : (a + 1) * 2 * rhs]
            real.append(top[:, :vectors] + low[:, vectors:])
            imag.append(low[:, :vectors] - top[:, vectors:])
        out_ref[a] = jnp.concatenate(real + imag, axis=1).astype(out_ref.dtype)
    loads[-1].wait()


def restrict(fine, null, operator):
    times, _, _, rhs, sites = fine.shape
    coarse_y = sites // (64 * CZ)
    return pl.pallas_call(
        functools.partial(restrict_kernel, coarse_y),
        in_specs=[pl.BlockSpec(memory_space=pl.ANY)] * 3,
        out_specs=[pl.BlockSpec(memory_space=pltpu.VMEM)] * 3,
        out_shape=[
            pltpu.VMEM((coarse_y * CZ, rhs, 4 * null.shape[3]), jnp.bfloat16),
            pltpu.VMEM(null.shape, null.dtype),
            pltpu.VMEM(operator.shape[2:], operator.dtype),
        ],
        scratch_shapes=[pltpu.VMEM(fine.shape, fine.dtype), pltpu.SemaphoreType.DMA((2 * times + 1,))],
        compiler_params=pltpu.CompilerParams(vmem_limit_bytes=KERNEL_VMEM),
        name="restrict",
    )(in_hbm(fine), in_hbm(null), in_hbm(operator))


def prolong_kernel(coarse_y, coarse_ref, null_ref, out_ref, held, done):
    aggregates = coarse_y * CZ
    times, _, _, rhs, sites = held.shape
    vectors = null_ref.shape[3]
    ids = aggregate_ids((2 * rhs, sites), coarse_y)
    masks = [ids == a for a in range(aggregates)]
    mixers = []
    for h in range(2):
        mixer = []
        for a in range(aggregates):
            weights = coarse_ref[a]
            real = weights[:, h * vectors : (h + 1) * vectors]
            imag = weights[:, (2 + h) * vectors : (3 + h) * vectors]
            mixer.append(jnp.concatenate([real, -imag], axis=1))
            mixer.append(jnp.concatenate([imag, real], axis=1))
        mixers.append(jnp.concatenate(mixer, axis=0))
    copies = []
    for t in range(times):
        for c in range(12):
            null = jnp.concatenate([null_ref[t, 0, c], null_ref[t, 1, c]], axis=0)
            every = jnp.dot(mixers[c // 6], null, preferred_element_type=jnp.float32)
            result = every[: 2 * rhs]
            for a in range(1, aggregates):
                result = jnp.where(masks[a], every[a * 2 * rhs : (a + 1) * 2 * rhs], result)
            result = result.astype(held.dtype)
            held[t, 0, c] = result[:rhs]
            held[t, 1, c] = result[rhs:]
        copies.append(pltpu.make_async_copy(held.at[t], out_ref.at[t], done.at[t]))
        copies[-1].start()
    for copy in copies:
        copy.wait()


def prolong(coarse, null):
    aggregates, rhs, _ = coarse.shape
    times, _, _, _, sites = null.shape
    shape = (times, 2, 12, rhs, sites)
    return pl.pallas_call(
        functools.partial(prolong_kernel, aggregates // CZ),
        in_specs=[pl.BlockSpec(memory_space=pltpu.VMEM)] * 2,
        out_specs=pl.BlockSpec(memory_space=pl.ANY),
        out_shape=jax.ShapeDtypeStruct(shape, jnp.bfloat16),
        scratch_shapes=[pltpu.VMEM(shape, jnp.bfloat16), pltpu.SemaphoreType.DMA((times,))],
        compiler_params=pltpu.CompilerParams(vmem_limit_bytes=KERNEL_VMEM),
        name="prolong",
    )(in_vmem(coarse), in_vmem(null))


def time_sides(even_slice):
    parity = lax.rem(lax.axis_index("zt"), 2)
    if not even_slice:
        parity = 1 - parity
    return 1 + parity, 2 - parity


def for_sites(extent, body):
    for y in range(extent[0]):
        for z in range(extent[1]):
            if extent[2] <= 2:
                for x in range(extent[2]):
                    body((y, z, x))
            else:
                lax.fori_loop(0, extent[2], lambda x, c, y=y, z=z: (body((y, z, x)), c)[1], 0)


def around(operator, site, extent):
    found = [(operator[(0, 0) + site], site)]
    for axis in range(3):
        up, down = [
            site[:axis] + (lax.rem(site[axis] + step, extent[axis]) if axis == 2 else (site[axis] + step) % extent[axis],)
            + site[axis + 1 :]
            for step in (1, extent[axis] - 1)
        ]
        ahead, behind = operator[(0, 3 + 2 * axis) + site], operator[(0, 4 + 2 * axis) + site]
        if extent[axis] == 2:
            both = ahead.astype(jnp.float32) + behind.astype(jnp.float32)
            found.append((both.astype(jnp.bfloat16), up))
        else:
            found += [(ahead, up), (behind, down)]
    return found


def products(pairs):
    return lax.dot_general(
        jnp.concatenate([field for _, field in pairs], axis=1),
        jnp.concatenate([block for block, _ in pairs], axis=1),
        LANES,
        preferred_element_type=jnp.float32,
    )


def stencil(operator, site, here, times):
    extent = operator.shape[2:5]
    pairs = [(block, here[near]) for block, near in around(operator, site, extent)]
    pairs += [(operator[(0, d) + site], field[site]) for d, field in times]
    return products(pairs)


def relaxed(value, rounded, target, sums):
    image = sums + DIAGONAL_SHIFT * rounded.astype(jnp.float32)
    return value + RELAX_WEIGHT * (target.astype(jnp.float32) - image)


def gather_kernel(pieces, operator, *refs):
    parts, (rhs_mine, rhs_pair, start_pair, message, part_mine) = refs[: 2 * pieces], refs[2 * pieces :]
    extent = operator.shape[2:5]
    position = lax.axis_index("xy")
    even, _ = time_sides(True)
    for whole, held in ((rhs_mine, parts[:pieces]), (rhs_pair, parts[pieces:])):
        for y in range(extent[0]):
            for z in range(extent[1]):
                for x in range(extent[2]):
                    if pieces == 1:
                        whole[y, z, x] = held[0][x, y * extent[1] + z]
                    else:
                        whole[y, z, lax.rem(position + x, pieces)] = held[x][y * extent[1] + z]

    def begin(site):
        message[(0,) + site] = (RELAX_WEIGHT * rhs_mine[site].astype(jnp.float32)).astype(jnp.bfloat16)
        start_pair[site] = (RELAX_WEIGHT * rhs_pair[site].astype(jnp.float32)).astype(jnp.bfloat16)

    for_sites(extent, begin)
    here = message.at[0]

    def step(site):
        sums = stencil(operator, site, here, [(even, start_pair)])
        value = RELAX_WEIGHT * rhs_mine[site].astype(jnp.float32)
        part = relaxed(value, here[site], rhs_mine[site], sums)
        part_mine[site] = part
        message[(1,) + site] = part.astype(jnp.bfloat16)

    for_sites(extent, step)


def pair_kernel(scaled, operator, rhs_pair, held, here, sent, part_pair, passed=None):
    even, _ = time_sides(False)
    other = sent.at[0]

    def step(site):
        sums = stencil(operator, site, here, [(even, other)])
        if scaled:
            value = RELAX_WEIGHT * rhs_pair[site].astype(jnp.float32)
        else:
            value = held[site]
        part_pair[site] = relaxed(value, here[site], rhs_pair[site], sums)
        if scaled:
            passed[site] = held[site]

    for_sites(operator.shape[2:5], step)


def second_kernel(
    op_mine, op_pair, back_near, back_far, rhs_mine, rhs_pair, sent, start_pair, part_mine, part_pair, near, far,
    message, field_mine, part_next, value_pair, field_pair, one_mine, one_pair, one_near, one_far, x_mine, x_pair,
):
    extent = op_mine.shape[2:5]
    even, odd = time_sides(True)
    pair_even, pair_odd = time_sides(False)

    def first(site):
        value = part_mine[site] - RELAX_WEIGHT * products([(op_mine[(0, odd) + site], near[(0,) + site])])
        x_mine[site] = value
        one_mine[site] = value.astype(jnp.bfloat16)
        value = part_pair[site] - RELAX_WEIGHT * products([(op_pair[(0, pair_odd) + site], far[(0,) + site])])
        x_pair[site] = value
        one_pair[site] = value.astype(jnp.bfloat16)
        value = near[(1,) + site].astype(jnp.float32) - RELAX_WEIGHT * products([(back_near[site], sent[(0,) + site])])
        one_near[site] = value.astype(jnp.bfloat16)
        value = far[(1,) + site].astype(jnp.float32) - RELAX_WEIGHT * products([(back_far[site], start_pair[site])])
        one_far[site] = value.astype(jnp.bfloat16)

    for_sites(extent, first)

    def second(site):
        sums = stencil(op_mine, site, one_mine, [(even, one_pair), (odd, one_near)])
        value = relaxed(x_mine[site], one_mine[site], rhs_mine[site], sums)
        x_mine[site] = value
        message[(0,) + site] = value.astype(jnp.bfloat16)
        field_mine[site] = value.astype(jnp.bfloat16)
        sums = stencil(op_pair, site, one_pair, [(pair_even, one_mine), (pair_odd, one_far)])
        value = relaxed(x_pair[site], one_pair[site], rhs_pair[site], sums)
        value_pair[site] = value
        field_pair[site] = value.astype(jnp.bfloat16)

    for_sites(extent, second)
    here = message.at[0]

    def third(site):
        sums = stencil(op_mine, site, here, [(even, field_pair)])
        part = relaxed(x_mine[site], here[site], rhs_mine[site], sums)
        part_next[site] = part
        message[(1,) + site] = part.astype(jnp.bfloat16)

    for_sites(extent, third)


def last_kernel(
    op_mine, op_pair, back_near, rhs_mine, sent, part_mine, part_pair, near, far,
    result, column, one_mine, one_pair, one_near, x_mine,
):
    extent = op_mine.shape[2:5]
    even, odd = time_sides(True)
    _, pair_odd = time_sides(False)

    def first(site):
        value = part_mine[site] - RELAX_WEIGHT * products([(op_mine[(0, odd) + site], near[(0,) + site])])
        x_mine[site] = value
        one_mine[site] = value.astype(jnp.bfloat16)
        value = part_pair[site] - RELAX_WEIGHT * products([(op_pair[(0, pair_odd) + site], far[site])])
        one_pair[site] = value.astype(jnp.bfloat16)
        value = near[(1,) + site].astype(jnp.float32) - RELAX_WEIGHT * products([(back_near[site], sent[(0,) + site])])
        one_near[site] = value.astype(jnp.bfloat16)

    for_sites(extent, first)

    def second(site):
        sums = stencil(op_mine, site, one_mine, [(even, one_pair), (odd, one_near)])
        value = relaxed(x_mine[site], one_mine[site], rhs_mine[site], sums)
        result[(0,) + site] = value.astype(jnp.bfloat16)

    for_sites(extent, second)
    position = lax.axis_index("xy")
    for y in range(extent[0]):
        for z in range(extent[1]):
            column[y * extent[1] + z] = result[0, y, z, position]


def in_hbm(array):
    return pltpu.with_memory_space_constraint(array, pltpu.HBM)


def in_vmem(array):
    return pltpu.with_memory_space_constraint(array, pltpu.VMEM)


def kernel_call(kernel, name, outs, scratch, *operands):
    return pl.pallas_call(
        kernel,
        in_specs=[pl.BlockSpec(memory_space=pltpu.VMEM)] * len(operands),
        out_specs=[pl.BlockSpec(memory_space=pltpu.VMEM)] * len(outs),
        out_shape=[pltpu.VMEM(shape, dtype) for shape, dtype in outs],
        scratch_shapes=[pltpu.VMEM(shape, dtype) for shape, dtype in scratch],
        compiler_params=pltpu.CompilerParams(vmem_limit_bytes=KERNEL_VMEM),
        name=name,
    )(*[in_vmem(operand) for operand in operands])


def exchange_plan():
    slices, columns = lax.axis_size("zt"), lax.axis_size("xy")
    other = [i ^ 1 for i in range(slices)]
    across = [(i + 1 if i % 2 else i - 1) % slices for i in range(slices)]

    def permutation(target, turn=0):
        return [
            (i * columns + j, target[i] * columns + (j + turn) % columns) for i in range(slices) for j in range(columns)
        ]

    def send(array, target, turn=0):
        return lax.ppermute(array, ("zt", "xy"), permutation(target, turn))

    far = [other[across[i]] for i in range(slices)]
    return send, list(range(slices)), other, across, far


def per_device(fine_vectors, null_vectors, coarse_operator):
    send, same, other, across, far = exchange_plan()
    columns = lax.axis_size("xy")
    extent = coarse_operator.shape[2:5]
    bf16, f32 = jnp.bfloat16, jnp.float32
    own, null_kept, block = restrict(fine_vectors, null_vectors, coarse_operator)
    full = extent + own.shape[1:]
    if columns == 2:
        parts = [own, send(own, same, 1), send(own, other), send(own, other, 1)]
    else:
        every = lax.all_gather(own, "xy")
        parts = [every, send(every, other)]
    back_near = send(block, across)
    op_pair = send(coarse_operator, other)
    rhs_mine, rhs_pair, start_pair, sent, part_mine = kernel_call(
        functools.partial(gather_kernel, len(parts) // 2),
        "gather",
        [(full, bf16), (full, bf16), (full, bf16), ((2,) + full, bf16), (full, f32)],
        [],
        coarse_operator,
        *parts,
    )
    near_message, far_message = send(sent, across), send(sent, far)
    part_pair, back_far = kernel_call(
        functools.partial(pair_kernel, True), "pair_one", [(full, f32), (block.shape, bf16)], [],
        op_pair, rhs_pair, back_near, start_pair, sent,
    )
    back_far = send(back_far, other)
    sent_next, field_mine, part_mine, value_pair, field_pair = kernel_call(
        second_kernel,
        "second",
        [((2,) + full, bf16), (full, bf16), (full, f32), (full, f32), (full, bf16)],
        [(full, bf16)] * 4 + [(full, f32)] * 2,
        coarse_operator, op_pair, back_near, back_far, rhs_mine, rhs_pair, sent, start_pair, part_mine, part_pair,
        near_message, far_message,
    )
    near_message, far_field = send(sent_next, across), send(field_mine, far)
    (part_pair,) = kernel_call(
        functools.partial(pair_kernel, False), "pair_two", [(full, f32)], [],
        op_pair, rhs_pair, value_pair, field_pair, sent_next,
    )
    coarse_iterate, column = kernel_call(
        last_kernel,
        "last",
        [((1,) + full, bf16), (own.shape, bf16)],
        [(full, bf16)] * 3 + [(full, f32)],
        coarse_operator, op_pair, back_near, rhs_mine, sent_next, part_mine, part_pair, near_message, far_field,
    )
    return (prolong(column, null_kept), coarse_iterate)


def solution(mesh):
    return jax.shard_map(
        per_device,
        mesh=mesh,
        in_specs=(
            P("zt", None, None, None, "xy"),
            P("zt", None, None, None, "xy"),
            P("zt", None, None, None, None, None, None),
        ),
        out_specs=(P("zt", None, None, None, "xy"), P("zt", None, None, None, None, None)),
        check_vma=False,
    )
```

time: 47 us -> 35.2 us (0.75)
  waiting for transfers between devices: 22.7 us -> 10 us
  starting transfers between devices: 4.99 us -> 14.9 us
  blocking collectives: 5.6 us -> 0 us
  matrix products: 3.12 us -> 0 us
    ppermute x8 -> x10, waiting for transfers between devices: 22.7 us -> 10 us  [send(): return lax.ppermute(array, ('zt', 'xy'), permutation(target, turn))]
    ppermute x8 -> x10, starting transfers between devices: 4.99 us -> 14.9 us  [send(): return lax.ppermute(array, ('zt', 'xy'), permutation(target, turn))]
    all_gather x1 -> x0, blocking collectives: 5.6 us -> none  [per_device(): whole_rhs = lax.all_gather(coarse_rhs, 'xy', axis=3, tiled=True)]
    dot_general x4 -> x0, matrix products: 3.12 us -> none  [stencil_product(): jnp.einsum('tdyzxij,tdyzxrj->tyzxri', operator_block, stacked, preferred_...]
    dynamic_slice x1 -> x0, local copies, waits for them, and re-layouts: 0.61 us -> none  [per_device(): column = lax.dynamic_slice_in_dim(coarse_iterate, position, 1, 3)]
    unnamed x12 -> x3, local copies, waits for them, and re-layouts: 0.09 us -> 0.64 us
    pallas_call x2 -> x7, Pallas kernels: 8.44 us -> 8.78 us  [the longest x5 4.37 us: kernel_call(): pl.pallas_call(kernel, in_specs=[pl.BlockSpec(memory_space=pltpu.VMEM)] *...]
  transfers between devices with their start and end apart: 8 -> 10, of which waited for: 8 -> 6; matrix products, arithmetic and copies ran while one was open for 0% -> 0% of each run, Pallas kernels for 0% -> 11%
where the time goes in v2:
time: 35.2 us; the launch traced here: 35 us
  starting transfers between devices  14.9 us (42%)
  waiting for transfers between devices  10 us (28%)
  Pallas kernels  8.78 us (25%)
  between operations  0.67 us (2%)
  local copies, waits for them, and re-layouts  0.64 us (2%)
    ppermute x10, starting transfers between devices, send(): return lax.ppermute(array, ('zt', 'xy'), permutation(target, turn))  14.9 us
    ppermute x10, waiting for transfers between devices, send(): return lax.ppermute(array, ('zt', 'xy'), permutation(target, turn))  10 us
    pallas_call x5, Pallas kernels, kernel_call(): pl.pallas_call(kernel, in_specs=[pl.BlockSpec(memory_space=pltpu.VMEM)] *...  4.37 us
    pallas_call x1, Pallas kernels, restrict(): pl.pallas_call(functools.partial(restrict_kernel, coarse_y), in_specs=[pl...  2.68 us
    pallas_call x1, Pallas kernels, prolong(): pl.pallas_call(functools.partial(prolong_kernel, aggregates // CZ), in_sp...  1.73 us
  transfers between devices with their start and end apart: 10, of which 6 were waited for; matrix products, arithmetic and copies ran while one was open for 0% of the time, Pallas kernels for 11%

profile of v2, /device:TPU:0, one launch (start us, length us, event | category | flops | bytes accessed | tf_op | source)
XLA Modules:
  0.0 35.0 jit_solution(6100203572791191612)
XLA Ops:
  0.6 0.0 copy-start
  0.6 0.5 %collective-permute-start = (bf16[1,9,2,2,2,128,128]{6,5,4,3,2,1,0:T(8,128)(2,1)}, bf16[1,9,2,2,2,128,128]{6,5,4,3,2,1,0:T(8,128)(2,1)S(1)}, u32[]{:S(2)}, u32[]{:S(2)}) collective-permute-start(bf16[1,9,2,2,2,128,128]{6,5,4,3,2,1,0:T(8,128)(2,1)} %op_mine.3), channel_id=1, source_target_pairs={{0,2},{1,3},{2,0},{3,1},{4,6},{5,7},{6,4},{7,5},{8,10},{9,11},{10,... | collective-permute-start | bytes 7077896 | tf_op jit(solution)/shard_map/ppermute | solution.py:344
  1.2 2.7 %restrict.1 = (bf16[4,16,128]{2,1,0:T(8,128)(2,1)S(1)}, bf16[4,2,12,32,256]{4,3,2,1,0:T(8,128)(2,1)S(1)}, bf16[2,2,2,128,128]{4,3,2,1,0:T(8,128)(2,1)S(1)}) custom-call(bf16[4,2,12,16,256]{4,3,2,1,0:T(8,128)(2,1)} %fine_hbm.1, bf16[4,2,12,32,256]{4,3,2,1,0:T(8,128)(2,1)} %null_hbm.1, bf16[1,9,2,2,2,128,128]{6,5,4,3,2,1,0:T(8,128)(2,1)} %op_mine.3), custom_call_target="tpu_custom_call" | custom-call | tf_op jit(solution)/shard_map/restrict/pallas_call | solution.py:71
  3.8 5.5 %collective-permute-start.1 = (bf16[2,2,2,128,128]{4,3,2,1,0:T(8,128)(2,1)S(1)}, bf16[2,2,2,128,128]{4,3,2,1,0:T(8,128)(2,1)S(1)}, u32[]{:S(2)}, u32[]{:S(2)}) collective-permute-start(bf16[2,2,2,128,128]{4,3,2,1,0:T(8,128)(2,1)S(1)} %get-tuple-element.19), channel_id=1, source_target_pairs={{0,30},{1,31},{2,4},{3,5},{4,2},{5,3},{6,8},{7,9},{8,6},{9,7},{10,... | collective-permute-start | bytes 786440 | tf_op jit(solution)/shard_map/ppermute | solution.py:344
  9.4 1.5 %collective-permute-start.2 = (bf16[4,16,128]{2,1,0:T(8,128)(2,1)S(1)}, bf16[4,16,128]{2,1,0:T(8,128)(2,1)S(1)}, u32[]{:S(2)}, u32[]{:S(2)}) collective-permute-start(bf16[4,16,128]{2,1,0:T(8,128)(2,1)S(1)} %get-tuple-element.20.refs_0_), channel_id=1, source_target_pairs={{0,1},{1,0},{2,3},{3,2},{4,5},{5,4},{6,7},{7,6},{8,9},{9,8},{10,11... | collective-permute-start | bytes 49160 | tf_op jit(solution)/shard_map/ppermute | solution.py:344
  10.9 0.0 collective-permute-start.3
  10.9 0.6 %collective-permute-start.4 = (bf16[4,16,128]{2,1,0:T(8,128)(2,1)S(1)}, bf16[4,16,128]{2,1,0:T(8,128)(2,1)S(1)}, u32[]{:S(2)}, u32[]{:S(2)}) collective-permute-start(bf16[4,16,128]{2,1,0:T(8,128)(2,1)S(1)} %get-tuple-element.20.refs_0_), channel_id=1, source_target_pairs={{0,3},{1,2},{2,1},{3,0},{4,7},{5,6},{6,5},{7,4},{8,11},{9,10},{10,... | collective-permute-start | bytes 49160 | tf_op jit(solution)/shard_map/ppermute | solution.py:344
  11.5 1.6 %collective-permute-done.2.refs_1_ = bf16[4,16,128]{2,1,0:T(8,128)(2,1)S(1)} collective-permute-done((bf16[4,16,128]{2,1,0:T(8,128)(2,1)S(1)}, bf16[4,16,128]{2,1,0:T(8,128)(2,1)S(1)}, u32[]{:S(2)}, u32[]{:S(2)}) %collective-permute-start.2) | collective-permute-done | bytes 16416 | tf_op jit(solution)/shard_map/ppermute | solution.py:344
  13.1 0.0 collective-permute-done.3.refs_2_
  13.1 0.9 %collective-permute-done.4.refs_3_ = bf16[4,16,128]{2,1,0:T(8,128)(2,1)S(1)} collective-permute-done((bf16[4,16,128]{2,1,0:T(8,128)(2,1)S(1)}, bf16[4,16,128]{2,1,0:T(8,128)(2,1)S(1)}, u32[]{:S(2)}, u32[]{:S(2)}) %collective-permute-start.4) | collective-permute-done | bytes 16416 | tf_op jit(solution)/shard_map/ppermute | solution.py:344
  14.1 0.0 copy-done
  14.1 0.5 %gather.1 = (bf16[2,2,2,16,128]{4,3,2,1,0:T(8,128)(2,1)S(1)}, bf16[2,2,2,16,128]{4,3,2,1,0:T(8,128)(2,1)S(1)}, bf16[2,2,2,16,128]{4,3,2,1,0:T(8,128)(2,1)S(1)}, ...) custom-call(bf16[1,9,2,2,2,128,128]{6,5,4,3,2,1,0:T(8,128)(2,1)S(1)} %copy-done, ...), custom_call_target="tpu_custom_call" | custom-call | tf_op jit(solution)/shard_map/gather/pallas_call | solution.py:322
  14.6 0.0 collective-permute-done.1.held.back_near
  14.6 0.0 collective-permute-done.operator.op_pair
  14.6 0.5 %pair_one.1 = (f32[2,2,2,16,128]{4,3,2,1,0:T(8,128)S(1)}, bf16[2,2,2,128,128]{4,3,2,1,0:T(8,128)(2,1)S(1)}) custom-call(bf16[1,9,2,2,2,128,128]{6,5,4,3,2,1,0:T(8,128)(2,1)S(1)} %collective-permute-done.operator.op_pair, bf16[2,2,2,16,128]{4,3,2,1,0:T(8,128)(2,1)S(1)} %get-tuple-element.22.rhs_pair, ...), custom_call_target="tpu_custom_call" | custom-call | tf_op jit(solution)/shard_map/pair_one/pallas_call | solution.py:322
  15.1 0.5 %collective-permute-start.5 = (bf16[2,2,2,128,128]{4,3,2,1,0:T(8,128)(2,1)S(1)}, bf16[2,2,2,128,128]{4,3,2,1,0:T(8,128)(2,1)S(1)}, u32[]{:S(2)}, u32[]{:S(2)}) collective-permute-start(bf16[2,2,2,128,128]{4,3,2,1,0:T(8,128)(2,1)S(1)} %get-tuple-element.25), channel_id=1, source_target_pairs={{0,2},{1,3},{2,0},{3,1},{4,6},{5,7},{6,4},{7,5},{8,10},{9,11},{10,... | collective-permute-start | bytes 786440 | tf_op jit(solution)/shard_map/ppermute | solution.py:344
  15.7 2.8 %collective-permute-start.6 = (bf16[2,2,2,2,16,128]{5,4,3,2,1,0:T(8,128)(2,1)S(1)}, bf16[2,2,2,2,16,128]{5,4,3,2,1,0:T(8,128)(2,1)S(1)}, u32[]{:S(2)}, u32[]{:S(2)}) collective-permute-start(bf16[2,2,2,2,16,128]{5,4,3,2,1,0:T(8,128)(2,1)S(1)} %get-tuple-element.24.sent), channel_id=1, source_target_pairs={{0,30},{1,31},{2,4},{3,5},{4,2},{5,3},{6,8},{7,9},{8,6},{9,7},{10,... | collective-permute-start | bytes 196616 | tf_op jit(solution)/shard_map/ppermute | solution.py:344
  18.5 0.7 %collective-permute-start.7 = (bf16[2,2,2,2,16,128]{5,4,3,2,1,0:T(8,128)(2,1)S(1)}, bf16[2,2,2,2,16,128]{5,4,3,2,1,0:T(8,128)(2,1)S(1)}, u32[]{:S(2)}, u32[]{:S(2)}) collective-permute-start(bf16[2,2,2,2,16,128]{5,4,3,2,1,0:T(8,128)(2,1)S(1)} %get-tuple-element.24.sent), channel_id=1, source_target_pairs={{0,28},{1,29},{2,6},{3,7},{4,0},{5,1},{6,10},{7,11},{8,4},{9,5},{1... | collective-permute-start | bytes 196616 | tf_op jit(solution)/shard_map/ppermute | solution.py:344
  19.1 2.9 %collective-permute-done.6.near = bf16[2,2,2,2,16,128]{5,4,3,2,1,0:T(8,128)(2,1)S(1)} collective-permute-done((bf16[2,2,2,2,16,128]{5,4,3,2,1,0:T(8,128)(2,1)S(1)}, bf16[2,2,2,2,16,128]{5,4,3,2,1,0:T(8,128)(2,1)S(1)}, u32[]{:S(2)}, u32[]{:S(2)}) %collective-permute-start.6) | collective-permute-done | bytes 65568 | tf_op jit(solution)/shard_map/ppermute | solution.py:344
  22.0 1.4 %collective-permute-done.7.far = bf16[2,2,2,2,16,128]{5,4,3,2,1,0:T(8,128)(2,1)S(1)} collective-permute-done((bf16[2,2,2,2,16,128]{5,4,3,2,1,0:T(8,128)(2,1)S(1)}, bf16[2,2,2,2,16,128]{5,4,3,2,1,0:T(8,128)(2,1)S(1)}, u32[]{:S(2)}, u32[]{:S(2)}) %collective-permute-start.7) | collective-permute-done | bytes 65568 | tf_op jit(solution)/shard_map/ppermute | solution.py:344
  23.4 0.0 collective-permute-done.5.back_far
  23.5 1.9 %second.1 = (bf16[2,2,2,2,16,128]{5,4,3,2,1,0:T(8,128)(2,1)S(1)}, bf16[2,2,2,16,128]{4,3,2,1,0:T(8,128)(2,1)S(1)}, f32[2,2,2,16,128]{4,3,2,1,0:T(8,128)S(1)}, f3...) custom-call(bf16[1,9,2,2,2,128,128]{6,5,4,3,2,1,0:T(8,128)(2,1)S(1)} %copy-done, ...), custom_call_target="tpu_custom_call" | custom-call | tf_op jit(solution)/shard_map/second/pallas_call | solution.py:322
  25.3 1.4 %collective-permute-start.8 = (bf16[2,2,2,2,16,128]{5,4,3,2,1,0:T(8,128)(2,1)S(1)}, bf16[2,2,2,2,16,128]{5,4,3,2,1,0:T(8,128)(2,1)S(1)}, u32[]{:S(2)}, u32[]{:S(2)}) collective-permute-start(bf16[2,2,2,2,16,128]{5,4,3,2,1,0:T(8,128)(2,1)S(1)} %get-tuple-element.28.sent), channel_id=1, source_target_pairs={{0,30},{1,31},{2,4},{3,5},{4,2},{5,3},{6,8},{7,9},{8,6},{9,7},{10,... | collective-permute-start | bytes 196616 | tf_op jit(solution)/shard_map/ppermute | solution.py:344
  26.8 1.3 %collective-permute-start.9 = (bf16[2,2,2,16,128]{4,3,2,1,0:T(8,128)(2,1)S(1)}, bf16[2,2,2,16,128]{4,3,2,1,0:T(8,128)(2,1)S(1)}, u32[]{:S(2)}, u32[]{:S(2)}) collective-permute-start(bf16[2,2,2,16,128]{4,3,2,1,0:T(8,128)(2,1)S(1)} %get-tuple-element.32), channel_id=1, source_target_pairs={{0,28},{1,29},{2,6},{3,7},{4,0},{5,1},{6,10},{7,11},{8,4},{9,5},{1... | collective-permute-start | bytes 98312 | tf_op jit(solution)/shard_map/ppermute | solution.py:344
  28.1 0.5 %pair_two.1.part_pair = f32[2,2,2,16,128]{4,3,2,1,0:T(8,128)S(1)} custom-call(bf16[1,9,2,2,2,128,128]{6,5,4,3,2,1,0:T(8,128)(2,1)S(1)} %collective-permute-done.operator.op_pair, bf16[2,2,2,16,128]{4,3,2,1,0:T(8,128)(2,1)S(1)} %get-tuple-element.22.rhs_pair, f32[2,2,2,16,128]{4,3,2,1,0:T(8,128)S(1)} %get-tuple-element.30.held, ...), custom_call_target="tpu_custom_call" | custom-call | tf_op jit(solution)/shard_map/pair_two/pallas_call | solution.py:322
  28.6 2.1 %collective-permute-done.9.far = bf16[2,2,2,16,128]{4,3,2,1,0:T(8,128)(2,1)S(1)} collective-permute-done((bf16[2,2,2,16,128]{4,3,2,1,0:T(8,128)(2,1)S(1)}, bf16[2,2,2,16,128]{4,3,2,1,0:T(8,128)(2,1)S(1)}, u32[]{:S(2)}, u32[]{:S(2)}) %collective-permute-start.9) | collective-permute-done | bytes 32800 | tf_op jit(solution)/shard_map/ppermute | solution.py:344
  30.7 1.1 %collective-permute-done.8.near = bf16[2,2,2,2,16,128]{5,4,3,2,1,0:T(8,128)(2,1)S(1)} collective-permute-done((bf16[2,2,2,2,16,128]{5,4,3,2,1,0:T(8,128)(2,1)S(1)}, bf16[2,2,2,2,16,128]{5,4,3,2,1,0:T(8,128)(2,1)S(1)}, u32[]{:S(2)}, u32[]{:S(2)}) %collective-permute-start.8) | collective-permute-done | bytes 65568 | tf_op jit(solution)/shard_map/ppermute | solution.py:344
  31.7 0.9 %last.1 = (bf16[1,2,2,2,16,128]{5,4,3,2,1,0:T(8,128)(2,1)S(1)}, bf16[4,16,128]{2,1,0:T(8,128)(2,1)S(1)}) custom-call(bf16[1,9,2,2,2,128,128]{6,5,4,3,2,1,0:T(8,128)(2,1)S(1)} %copy-done, bf16[1,9,2,2,2,128,128]{6,5,4,3,2,1,0:T(8,128)(2,1)S(1)} %collective-permute-done.operator.op_pair, ...), custom_call_target="tpu_custom_call" | custom-call | tf_op jit(solution)/shard_map/last/pallas_call | solution.py:322
  32.7 0.6 %copy.5 = bf16[1,2,2,2,16,128]{5,4,3,2,1,0:T(8,128)(2,1)} copy(bf16[1,2,2,2,16,128]{5,4,3,2,1,0:T(8,128)(2,1)S(1)} %get-tuple-element.37) | data formatting | bytes 65536
  33.3 1.7 %prolong.1 = bf16[4,2,12,16,256]{4,3,2,1,0:T(8,128)(2,1)} custom-call(bf16[4,16,128]{2,1,0:T(8,128)(2,1)S(1)} %get-tuple-element.33.coarse_ref, bf16[4,2,12,32,256]{4,3,2,1,0:T(8,128)(2,1)S(1)} %get-tuple-element.34.null_ref), custom_call_target="tpu_custom_call" | custom-call | tf_op jit(solution)/shard_map/prolong/pallas_call | solution.py:123
Async XLA Ops:
  0.6 13.4 %copy-start = (bf16[1,9,2,2,2,128,128]{6,5,4,3,2,1,0:T(8,128)(2,1)S(1)}, bf16[1,9,2,2,2,128,128]{6,5,4,3,2,1,0:T(8,128)(2,1)}, u32[]{:S(2)}) copy-start(bf16[1,9,2,2,2,128,128]{6,5,4,3,2,1,0:T(8,128)(2,1)} %op_mine.3) | copy-start | bytes 7077892
  0.6 14.0 %collective-permute-start = (bf16[1,9,2,2,2,128,128]{6,5,4,3,2,1,0:T(8,128)(2,1)}, bf16[1,9,2,2,2,128,128]{6,5,4,3,2,1,0:T(8,128)(2,1)S(1)}, u32[]{:S(2)}, u32[]{:S(2)}) collective-permute-start(bf16[1,9,2,2,2,128,128]{6,5,4,3,2,1,0:T(8,128)(2,1)} %op_mine.3), channel_id=1, source_target_pairs={{0,2},{1,3},{2,0},{3,1},{4,6},{5,7},{6,4},{7,5},{8,10},{9,11},{10,... | collective-permute-start | bytes 7077896 | tf_op jit(solution)/shard_map/ppermute | solution.py:344
  3.8 10.7 %collective-permute-start.1 = (bf16[2,2,2,128,128]{4,3,2,1,0:T(8,128)(2,1)S(1)}, bf16[2,2,2,128,128]{4,3,2,1,0:T(8,128)(2,1)S(1)}, u32[]{:S(2)}, u32[]{:S(2)}) collective-permute-start(bf16[2,2,2,128,128]{4,3,2,1,0:T(8,128)(2,1)S(1)} %get-tuple-element.19), channel_id=1, source_target_pairs={{0,30},{1,31},{2,4},{3,5},{4,2},{5,3},{6,8},{7,9},{8,6},{9,7},{10,... | collective-permute-start | bytes 786440 | tf_op jit(solution)/shard_map/ppermute | solution.py:344
  9.4 3.7 %collective-permute-start.2 = (bf16[4,16,128]{2,1,0:T(8,128)(2,1)S(1)}, bf16[4,16,128]{2,1,0:T(8,128)(2,1)S(1)}, u32[]{:S(2)}, u32[]{:S(2)}) collective-permute-start(bf16[4,16,128]{2,1,0:T(8,128)(2,1)S(1)} %get-tuple-element.20.refs_0_), channel_id=1, source_target_pairs={{0,1},{1,0},{2,3},{3,2},{4,5},{5,4},{6,7},{7,6},{8,9},{9,8},{10,11... | collective-permute-start | bytes 49160 | tf_op jit(solution)/shard_map/ppermute | solution.py:344
  10.9 2.2 %collective-permute-start.3 = (bf16[4,16,128]{2,1,0:T(8,128)(2,1)S(1)}, bf16[4,16,128]{2,1,0:T(8,128)(2,1)S(1)}, u32[]{:S(2)}, u32[]{:S(2)}) collective-permute-start(bf16[4,16,128]{2,1,0:T(8,128)(2,1)S(1)} %get-tuple-element.20.refs_0_), channel_id=1, source_target_pairs={{0,2},{1,3},{2,0},{3,1},{4,6},{5,7},{6,4},{7,5},{8,10},{9,11},{10,... | collective-permute-start | bytes 49160 | tf_op jit(solution)/shard_map/ppermute | solution.py:344
  10.9 3.2 %collective-permute-start.4 = (bf16[4,16,128]{2,1,0:T(8,128)(2,1)S(1)}, bf16[4,16,128]{2,1,0:T(8,128)(2,1)S(1)}, u32[]{:S(2)}, u32[]{:S(2)}) collective-permute-start(bf16[4,16,128]{2,1,0:T(8,128)(2,1)S(1)} %get-tuple-element.20.refs_0_), channel_id=1, source_target_pairs={{0,3},{1,2},{2,1},{3,0},{4,7},{5,6},{6,5},{7,4},{8,11},{9,10},{10,... | collective-permute-start | bytes 49160 | tf_op jit(solution)/shard_map/ppermute | solution.py:344
  15.1 8.3 %collective-permute-start.5 = (bf16[2,2,2,128,128]{4,3,2,1,0:T(8,128)(2,1)S(1)}, bf16[2,2,2,128,128]{4,3,2,1,0:T(8,128)(2,1)S(1)}, u32[]{:S(2)}, u32[]{:S(2)}) collective-permute-start(bf16[2,2,2,128,128]{4,3,2,1,0:T(8,128)(2,1)S(1)} %get-tuple-element.25), channel_id=1, source_target_pairs={{0,2},{1,3},{2,0},{3,1},{4,6},{5,7},{6,4},{7,5},{8,10},{9,11},{10,... | collective-permute-start | bytes 786440 | tf_op jit(solution)/shard_map/ppermute | solution.py:344
  15.7 6.4 %collective-permute-start.6 = (bf16[2,2,2,2,16,128]{5,4,3,2,1,0:T(8,128)(2,1)S(1)}, bf16[2,2,2,2,16,128]{5,4,3,2,1,0:T(8,128)(2,1)S(1)}, u32[]{:S(2)}, u32[]{:S(2)}) collective-permute-start(bf16[2,2,2,2,16,128]{5,4,3,2,1,0:T(8,128)(2,1)S(1)} %get-tuple-element.24.sent), channel_id=1, source_target_pairs={{0,30},{1,31},{2,4},{3,5},{4,2},{5,3},{6,8},{7,9},{8,6},{9,7},{10,... | collective-permute-start | bytes 196616 | tf_op jit(solution)/shard_map/ppermute | solution.py:344
  18.5 5.0 %collective-permute-start.7 = (bf16[2,2,2,2,16,128]{5,4,3,2,1,0:T(8,128)(2,1)S(1)}, bf16[2,2,2,2,16,128]{5,4,3,2,1,0:T(8,128)(2,1)S(1)}, u32[]{:S(2)}, u32[]{:S(2)}) collective-permute-start(bf16[2,2,2,2,16,128]{5,4,3,2,1,0:T(8,128)(2,1)S(1)} %get-tuple-element.24.sent), channel_id=1, source_target_pairs={{0,28},{1,29},{2,6},{3,7},{4,0},{5,1},{6,10},{7,11},{8,4},{9,5},{1... | collective-permute-start | bytes 196616 | tf_op jit(solution)/shard_map/ppermute | solution.py:344
  25.3 6.4 %collective-permute-start.8 = (bf16[2,2,2,2,16,128]{5,4,3,2,1,0:T(8,128)(2,1)S(1)}, bf16[2,2,2,2,16,128]{5,4,3,2,1,0:T(8,128)(2,1)S(1)}, u32[]{:S(2)}, u32[]{:S(2)}) collective-permute-start(bf16[2,2,2,2,16,128]{5,4,3,2,1,0:T(8,128)(2,1)S(1)} %get-tuple-element.28.sent), channel_id=1, source_target_pairs={{0,30},{1,31},{2,4},{3,5},{4,2},{5,3},{6,8},{7,9},{8,6},{9,7},{10,... | collective-permute-start | bytes 196616 | tf_op jit(solution)/shard_map/ppermute | solution.py:344
  26.8 3.9 %collective-permute-start.9 = (bf16[2,2,2,16,128]{4,3,2,1,0:T(8,128)(2,1)S(1)}, bf16[2,2,2,16,128]{4,3,2,1,0:T(8,128)(2,1)S(1)}, u32[]{:S(2)}, u32[]{:S(2)}) collective-permute-start(bf16[2,2,2,16,128]{4,3,2,1,0:T(8,128)(2,1)S(1)} %get-tuple-element.32), channel_id=1, source_target_pairs={{0,28},{1,29},{2,6},{3,7},{4,0},{5,1},{6,10},{7,11},{8,4},{9,5},{1... | collective-permute-start | bytes 98312 | tf_op jit(solution)/shard_map/ppermute | solution.py:344

commit v3 on v2

--- a/solution.py
+++ b/solution.py
@@ -13,6 +13,7 @@
 DIAGONAL_SHIFT = 3.0
 LANES = (((1,), (1,)), ((), ()))
 KERNEL_VMEM = 16 * 1024 * 1024
+GATHER_FLOPS = 10**10
 
 
 def aggregate_ids(shape, coarse_y):
@@ -23,7 +24,7 @@
     return y * CZ + z
 
 
-def restrict_kernel(coarse_y, fine_hbm, null_hbm, operator, out_ref, null_ref, block, fine_ref, loaded):
+def restrict_kernel(coarse_y, fine_hbm, null_hbm, operator_hbm, out_ref, null_ref, operator, block, fine_ref, loaded):
     aggregates = coarse_y * CZ
     times, _, _, rhs, sites = fine_ref.shape
     vectors = null_ref.shape[3]
@@ -32,7 +33,8 @@
     for t in range(times):
         loads.append(pltpu.make_async_copy(fine_hbm.at[t], fine_ref.at[t], loaded.at[2 * t]))
         loads.append(pltpu.make_async_copy(null_hbm.at[t], null_ref.at[t], loaded.at[2 * t + 1]))
-    loads.append(pltpu.make_async_copy(operator.at[0, odd], block, loaded.at[2 * times]))
+    loads.append(pltpu.make_async_copy(operator_hbm.at[0, odd], block, loaded.at[2 * times]))
+    loads.append(pltpu.make_async_copy(operator_hbm, operator, loaded.at[2 * times + 1]))
     for load in loads:
         load.start()
     ids = aggregate_ids((2 * rhs, sites), coarse_y)
@@ -62,6 +64,7 @@
             real.append(top[:, :vectors] + low[:, vectors:])
             imag.append(low[:, :vectors] - top[:, vectors:])
         out_ref[a] = jnp.concatenate(real + imag, axis=1).astype(out_ref.dtype)
+    loads[-2].wait()
     loads[-1].wait()
 
 
@@ -71,20 +74,22 @@
     return pl.pallas_call(
         functools.partial(restrict_kernel, coarse_y),
         in_specs=[pl.BlockSpec(memory_space=pl.ANY)] * 3,
-        out_specs=[pl.BlockSpec(memory_space=pltpu.VMEM)] * 3,
+        out_specs=[pl.BlockSpec(memory_space=pltpu.VMEM)] * 4,
         out_shape=[
             pltpu.VMEM((coarse_y * CZ, rhs, 4 * null.shape[3]), jnp.bfloat16),
             pltpu.VMEM(null.shape, null.dtype),
+            pltpu.VMEM(operator.shape, operator.dtype),
             pltpu.VMEM(operator.shape[2:], operator.dtype),
         ],
-        scratch_shapes=[pltpu.VMEM(fine.shape, fine.dtype), pltpu.SemaphoreType.DMA((2 * times + 1,))],
+        scratch_shapes=[pltpu.VMEM(fine.shape, fine.dtype), pltpu.SemaphoreType.DMA((2 * times + 2,))],
         compiler_params=pltpu.CompilerParams(vmem_limit_bytes=KERNEL_VMEM),
         name="restrict",
     )(in_hbm(fine), in_hbm(null), in_hbm(operator))
 
 
-def prolong_kernel(coarse_y, coarse_ref, null_ref, out_ref, held, done):
-    aggregates = coarse_y * CZ
+def prolong(column, null_ref, out_ref, held, done):
+    aggregates = len(column)
+    coarse_y = aggregates // CZ
     times, _, _, rhs, sites = held.shape
     vectors = null_ref.shape[3]
     ids = aggregate_ids((2 * rhs, sites), coarse_y)
@@ -93,7 +98,7 @@
     for h in range(2):
         mixer = []
         for a in range(aggregates):
-            weights = coarse_ref[a]
+            weights = column[a]
             real = weights[:, h * vectors : (h + 1) * vectors]
             imag = weights[:, (2 + h) * vectors : (3 + h) * vectors]
             mixer.append(jnp.concatenate([real, -imag], axis=1))
@@ -116,21 +121,6 @@
         copy.wait()
 
 
-def prolong(coarse, null):
-    aggregates, rhs, _ = coarse.shape
-    times, _, _, _, sites = null.shape
-    shape = (times, 2, 12, rhs, sites)
-    return pl.pallas_call(
-        functools.partial(prolong_kernel, aggregates // CZ),
-        in_specs=[pl.BlockSpec(memory_space=pltpu.VMEM)] * 2,
-        out_specs=pl.BlockSpec(memory_space=pl.ANY),
-        out_shape=jax.ShapeDtypeStruct(shape, jnp.bfloat16),
-        scratch_shapes=[pltpu.VMEM(shape, jnp.bfloat16), pltpu.SemaphoreType.DMA((times,))],
-        compiler_params=pltpu.CompilerParams(vmem_limit_bytes=KERNEL_VMEM),
-        name="prolong",
-    )(in_vmem(coarse), in_vmem(null))
-
-
 def time_sides(even_slice):
     parity = lax.rem(lax.axis_index("zt"), 2)
     if not even_slice:
@@ -187,7 +177,7 @@
 
 
 def gather_kernel(pieces, operator, *refs):
-    parts, (rhs_mine, rhs_pair, start_pair, message, part_mine) = refs[: 2 * pieces], refs[2 * pieces :]
+    parts, (rhs_mine, rhs_pair, start_mine, start_pair, message, part_mine) = refs[: 2 * pieces], refs[2 * pieces :]
     extent = operator.shape[2:5]
     position = lax.axis_index("xy")
     even, _ = time_sides(True)
@@ -201,11 +191,12 @@
                         whole[y, z, lax.rem(position + x, pieces)] = held[x][y * extent[1] + z]
 
     def begin(site):
-        message[(0,) + site] = (RELAX_WEIGHT * rhs_mine[site].astype(jnp.float32)).astype(jnp.bfloat16)
+        start_mine[site] = (RELAX_WEIGHT * rhs_mine[site].astype(jnp.float32)).astype(jnp.bfloat16)
+        message[(0,) + site] = start_mine[site]
         start_pair[site] = (RELAX_WEIGHT * rhs_pair[site].astype(jnp.float32)).astype(jnp.bfloat16)
 
     for_sites(extent, begin)
-    here = message.at[0]
+    here = start_mine
 
     def step(site):
         sums = stencil(operator, site, here, [(even, start_pair)])
@@ -217,74 +208,36 @@
     for_sites(extent, step)
 
 
-def pair_kernel(scaled, operator, rhs_pair, held, here, sent, part_pair, passed=None):
+def pair_kernel(scaled, operator, rhs_pair, here, other, part_pair):
     even, _ = time_sides(False)
-    other = sent.at[0]
 
     def step(site):
         sums = stencil(operator, site, here, [(even, other)])
         if scaled:
             value = RELAX_WEIGHT * rhs_pair[site].astype(jnp.float32)
         else:
-            value = held[site]
+            value = here[site].astype(jnp.float32)
         part_pair[site] = relaxed(value, here[site], rhs_pair[site], sums)
-        if scaled:
-            passed[site] = held[site]
 
     for_sites(operator.shape[2:5], step)
 
 
 def second_kernel(
-    op_mine, op_pair, back_near, back_far, rhs_mine, rhs_pair, sent, start_pair, part_mine, part_pair, near, far,
-    message, field_mine, part_next, value_pair, field_pair, one_mine, one_pair, one_near, one_far, x_mine, x_pair,
+    op_mine, op_pair, back_near, rhs_mine, sent, part_mine, part_pair, near, far,
+    field_mine, value_mine, one_mine, one_pair, one_near, x_mine,
 ):
-    extent = op_mine.shape[2:5]
-    even, odd = time_sides(True)
-    pair_even, pair_odd = time_sides(False)
-
-    def first(site):
-        value = part_mine[site] - RELAX_WEIGHT * products([(op_mine[(0, odd) + site], near[(0,) + site])])
-        x_mine[site] = value
-        one_mine[site] = value.astype(jnp.bfloat16)
-        value = part_pair[site] - RELAX_WEIGHT * products([(op_pair[(0, pair_odd) + site], far[(0,) + site])])
-        x_pair[site] = value
-        one_pair[site] = value.astype(jnp.bfloat16)
-        value = near[(1,) + site].astype(jnp.float32) - RELAX_WEIGHT * products([(back_near[site], sent[(0,) + site])])
-        one_near[site] = value.astype(jnp.bfloat16)
-        value = far[(1,) + site].astype(jnp.float32) - RELAX_WEIGHT * products([(back_far[site], start_pair[site])])
-        one_far[site] = value.astype(jnp.bfloat16)
-
-    for_sites(extent, first)
+    halfway(op_mine, op_pair, back_near, sent, part_mine, part_pair, near, far, one_mine, one_pair, one_near, x_mine)
 
     def second(site):
-        sums = stencil(op_mine, site, one_mine, [(even, one_pair), (odd, one_near)])
-        value = relaxed(x_mine[site], one_mine[site], rhs_mine[site], sums)
-        x_mine[site] = value
-        message[(0,) + site] = value.astype(jnp.bfloat16)
+        value = second_step(op_mine, rhs_mine, one_mine, one_pair, one_near, x_mine, site)
+        value_mine[site] = value
         field_mine[site] = value.astype(jnp.bfloat16)
-        sums = stencil(op_pair, site, one_pair, [(pair_even, one_mine), (pair_odd, one_far)])
-        value = relaxed(x_pair[site], one_pair[site], rhs_pair[site], sums)
-        value_pair[site] = value
-        field_pair[site] = value.astype(jnp.bfloat16)
-
-    for_sites(extent, second)
-    here = message.at[0]
-
-    def third(site):
-        sums = stencil(op_mine, site, here, [(even, field_pair)])
-        part = relaxed(x_mine[site], here[site], rhs_mine[site], sums)
-        part_next[site] = part
-        message[(1,) + site] = part.astype(jnp.bfloat16)
-
-    for_sites(extent, third)
-
-
-def last_kernel(
-    op_mine, op_pair, back_near, rhs_mine, sent, part_mine, part_pair, near, far,
-    result, column, one_mine, one_pair, one_near, x_mine,
-):
-    extent = op_mine.shape[2:5]
-    even, odd = time_sides(True)
+
+    for_sites(op_mine.shape[2:5], second)
+
+
+def halfway(op_mine, op_pair, back_near, sent, part_mine, part_pair, near, far, one_mine, one_pair, one_near, x_mine):
+    _, odd = time_sides(True)
     _, pair_odd = time_sides(False)
 
     def first(site):
@@ -296,18 +249,69 @@
         value = near[(1,) + site].astype(jnp.float32) - RELAX_WEIGHT * products([(back_near[site], sent[(0,) + site])])
         one_near[site] = value.astype(jnp.bfloat16)
 
-    for_sites(extent, first)
+    for_sites(op_mine.shape[2:5], first)
+
+
+def second_step(op_mine, rhs_mine, one_mine, one_pair, one_near, x_mine, site):
+    even, odd = time_sides(True)
+    sums = stencil(op_mine, site, one_mine, [(even, one_pair), (odd, one_near)])
+    return relaxed(x_mine[site], one_mine[site], rhs_mine[site], sums)
+
+
+def third_kernel(op_mine, rhs_mine, field_mine, value_mine, field_pair, message, part_next):
+    even, _ = time_sides(True)
+
+    def third(site):
+        sums = stencil(op_mine, site, field_mine, [(even, field_pair)])
+        part = relaxed(value_mine[site], field_mine[site], rhs_mine[site], sums)
+        part_next[site] = part
+        message[(0,) + site] = field_mine[site]
+        message[(1,) + site] = part.astype(jnp.bfloat16)
+
+    for_sites(op_mine.shape[2:5], third)
+
+
+def last_kernel(
+    op_mine, op_pair, back_near, rhs_mine, sent, part_mine, part_pair, near, far, null,
+    fine_out, coarse_out, one_mine, one_pair, one_near, x_mine, result, held, done,
+):
+    extent = op_mine.shape[2:5]
+    halfway(op_mine, op_pair, back_near, sent, part_mine, part_pair, near, far, one_mine, one_pair, one_near, x_mine)
 
     def second(site):
-        sums = stencil(op_mine, site, one_mine, [(even, one_pair), (odd, one_near)])
-        value = relaxed(x_mine[site], one_mine[site], rhs_mine[site], sums)
+        value = second_step(op_mine, rhs_mine, one_mine, one_pair, one_near, x_mine, site)
         result[(0,) + site] = value.astype(jnp.bfloat16)
 
     for_sites(extent, second)
+    times = held.shape[0]
+    copy = pltpu.make_async_copy(result, coarse_out, done.at[times])
+    copy.start()
     position = lax.axis_index("xy")
-    for y in range(extent[0]):
-        for z in range(extent[1]):
-            column[y * extent[1] + z] = result[0, y, z, position]
+    column = [result[0, y, z, position] for y in range(extent[0]) for z in range(extent[1])]
+    prolong(column, null, fine_out, held, done)
+    copy.wait()
+
+
+def last(shape, *operands):
+    full, times = operands[5].shape, shape[0]
+    return pl.pallas_call(
+        last_kernel,
+        in_specs=[pl.BlockSpec(memory_space=pltpu.VMEM)] * len(operands),
+        out_specs=[pl.BlockSpec(memory_space=pl.ANY)] * 2,
+        out_shape=[
+            jax.ShapeDtypeStruct(shape, jnp.bfloat16),
+            jax.ShapeDtypeStruct((1,) + full, jnp.bfloat16),
+        ],
+        scratch_shapes=[pltpu.VMEM(full, jnp.bfloat16)] * 3
+        + [
+            pltpu.VMEM(full, jnp.float32),
+            pltpu.VMEM((1,) + full, jnp.bfloat16),
+            pltpu.VMEM(shape, jnp.bfloat16),
+            pltpu.SemaphoreType.DMA((times + 1,)),
+        ],
+        compiler_params=pltpu.CompilerParams(vmem_limit_bytes=KERNEL_VMEM),
+        name="last",
+    )(*[in_vmem(operand) for operand in operands])
 
 
 def in_hbm(array):
@@ -318,7 +322,7 @@
     return pltpu.with_memory_space_constraint(array, pltpu.VMEM)
 
 
-def kernel_call(kernel, name, outs, scratch, *operands):
+def kernel_call(kernel, name, outs, scratch, *operands, flops=0):
     return pl.pallas_call(
         kernel,
         in_specs=[pl.BlockSpec(memory_space=pltpu.VMEM)] * len(operands),
@@ -326,6 +330,7 @@
         out_shape=[pltpu.VMEM(shape, dtype) for shape, dtype in outs],
         scratch_shapes=[pltpu.VMEM(shape, dtype) for shape, dtype in scratch],
         compiler_params=pltpu.CompilerParams(vmem_limit_bytes=KERNEL_VMEM),
+        cost_estimate=pl.CostEstimate(flops=flops, bytes_accessed=0, transcendentals=0) if flops else None,
         name=name,
     )(*[in_vmem(operand) for operand in operands])
 
@@ -352,7 +357,7 @@
     columns = lax.axis_size("xy")
     extent = coarse_operator.shape[2:5]
     bf16, f32 = jnp.bfloat16, jnp.float32
-    own, null_kept, block = restrict(fine_vectors, null_vectors, coarse_operator)
+    own, null_kept, operator, block = restrict(fine_vectors, null_vectors, coarse_operator)
     full = extent + own.shape[1:]
     if columns == 2:
         parts = [own, send(own, same, 1), send(own, other), send(own, other, 1)]
@@ -360,42 +365,43 @@
         every = lax.all_gather(own, "xy")
         parts = [every, send(every, other)]
     back_near = send(block, across)
-    op_pair = send(coarse_operator, other)
-    rhs_mine, rhs_pair, start_pair, sent, part_mine = kernel_call(
+    op_pair = send(operator, other)
+    rhs_mine, rhs_pair, start_mine, start_pair, sent, part_mine = kernel_call(
         functools.partial(gather_kernel, len(parts) // 2),
         "gather",
-        [(full, bf16), (full, bf16), (full, bf16), ((2,) + full, bf16), (full, f32)],
+        [(full, bf16)] * 4 + [((2,) + full, bf16), (full, f32)],
         [],
-        coarse_operator,
+        operator,
         *parts,
-    )
-    near_message, far_message = send(sent, across), send(sent, far)
-    part_pair, back_far = kernel_call(
-        functools.partial(pair_kernel, True), "pair_one", [(full, f32), (block.shape, bf16)], [],
-        op_pair, rhs_pair, back_near, start_pair, sent,
-    )
-    back_far = send(back_far, other)
-    sent_next, field_mine, part_mine, value_pair, field_pair = kernel_call(
+        flops=GATHER_FLOPS,
+    )
+    near_message, far_field = send(sent, across), send(start_mine, far)
+    (part_pair,) = kernel_call(
+        functools.partial(pair_kernel, True), "pair_one", [(full, f32)], [],
+        op_pair, rhs_pair, start_pair, start_mine,
+    )
+    field_mine, value_mine = kernel_call(
         second_kernel,
         "second",
-        [((2,) + full, bf16), (full, bf16), (full, f32), (full, f32), (full, bf16)],
-        [(full, bf16)] * 4 + [(full, f32)] * 2,
-        coarse_operator, op_pair, back_near, back_far, rhs_mine, rhs_pair, sent, start_pair, part_mine, part_pair,
-        near_message, far_message,
-    )
-    near_message, far_field = send(sent_next, across), send(field_mine, far)
+        [(full, bf16), (full, f32)],
+        [(full, bf16)] * 3 + [(full, f32)],
+        operator, op_pair, back_near, rhs_mine, sent, part_mine, part_pair, near_message, far_field,
+    )
+    field_pair = send(field_mine, other)
+    sent, part_mine = kernel_call(
+        third_kernel, "third", [((2,) + full, bf16), (full, f32)], [],
+        operator, rhs_mine, field_mine, value_mine, field_pair,
+    )
+    near_message, far_field = send(sent, across), send(field_mine, far)
     (part_pair,) = kernel_call(
         functools.partial(pair_kernel, False), "pair_two", [(full, f32)], [],
-        op_pair, rhs_pair, value_pair, field_pair, sent_next,
-    )
-    coarse_iterate, column = kernel_call(
-        last_kernel,
-        "last",
-        [((1,) + full, bf16), (own.shape, bf16)],
-        [(full, bf16)] * 3 + [(full, f32)],
-        coarse_operator, op_pair, back_near, rhs_mine, sent_next, part_mine, part_pair, near_message, far_field,
-    )
-    return (prolong(column, null_kept), coarse_iterate)
+        op_pair, rhs_pair, field_pair, field_mine,
+    )
+    fine_correction, coarse_iterate = last(
+        fine_vectors.shape,
+        operator, op_pair, back_near, rhs_mine, sent, part_mine, part_pair, near_message, far_field, null_kept,
+    )
+    return (fine_correction, coarse_iterate)
 
 
 def solution(mesh):

time: 35.2 us -> 31.5 us (0.89)
  waiting for transfers between devices: 10 us -> 6.92 us
  local copies, waits for them, and re-layouts: 0.64 us -> 0 us
  starting transfers between devices: 14.9 us -> 15.5 us
  Pallas kernels: 8.78 us -> 8.28 us
    ppermute x10, waiting for transfers between devices: 10 us -> 6.92 us  [send(): return lax.ppermute(array, ('zt', 'xy'), permutation(target, turn))]
    pallas_call x5, Pallas kernels: 4.37 us -> 3 us  [kernel_call(): pl.pallas_call(kernel, in_specs=[pl.BlockSpec(memory_space=pltpu.VMEM)] *...]
    pallas_call x1, Pallas kernels: 1.73 us -> 2.68 us  [last(): pl.pallas_call(last_kernel, in_specs=[pl.BlockSpec(memory_space=pltpu.VME...]
    unnamed x3 -> x0, local copies, waits for them, and re-layouts: 0.64 us -> none
    ppermute x10, starting transfers between devices: 14.9 us -> 15.5 us  [send(): return lax.ppermute(array, ('zt', 'xy'), permutation(target, turn))]
  transfers between devices with their start and end apart: 10 -> 10, of which waited for: 6 -> 3; matrix products, arithmetic and copies ran while one was open for 0% -> 0% of each run, Pallas kernels for 11% -> 5%
where the time goes in v3:
time: 31.5 us; the launch traced here: 31.4 us
  starting transfers between devices  15.5 us (49%)
  Pallas kernels  8.28 us (26%)
  waiting for transfers between devices  6.92 us (22%)
  between operations  0.66 us (2%)
    ppermute x10, starting transfers between devices, send(): return lax.ppermute(array, ('zt', 'xy'), permutation(target, turn))  15.5 us
    ppermute x10, waiting for transfers between devices, send(): return lax.ppermute(array, ('zt', 'xy'), permutation(target, turn))  6.92 us
    pallas_call x5, Pallas kernels, kernel_call(): pl.pallas_call(kernel, in_specs=[pl.BlockSpec(memory_space=pltpu.VMEM)] *...  3 us
    pallas_call x1, Pallas kernels, last(): pl.pallas_call(last_kernel, in_specs=[pl.BlockSpec(memory_space=pltpu.VME...  2.68 us
    pallas_call x1, Pallas kernels, restrict(): pl.pallas_call(functools.partial(restrict_kernel, coarse_y), in_specs=[pl...  2.6 us
  transfers between devices with their start and end apart: 10, of which 3 were waited for; matrix products, arithmetic and copies ran while one was open for 0% of the time, Pallas kernels for 5%

profile of v3, /device:TPU:0, one launch (start us, length us, event | category | flops | bytes accessed | tf_op | source)
XLA Modules:
  0.0 31.4 jit_solution(3127342135089804409)
XLA Ops:
  0.6 2.6 %restrict.1 = (bf16[4,16,128]{2,1,0:T(8,128)(2,1)S(1)}, bf16[4,2,12,32,256]{4,3,2,1,0:T(8,128)(2,1)S(1)}, bf16[1,9,2,2,2,128,128]{6,5,4,3,2,1,0:T(8,128)(2,1)S(1)}, bf16[2,2,2,128,128]{4,3,2,1,0:T(8,128)(2,1)S(1)}) custom-call(bf16[4,2,12,16,256]{4,3,2,1,0:T(8,128)(2,1)} %fine_hbm.1, bf16[4,2,12,32,256]{4,3,2,1,0:T(8,128)(2,1)} %null_hbm.1, ...), custom_call_target="tpu_custom_call" | custom-call | tf_op jit(solution)/shard_map/restrict/pallas_call | solution.py:74
  3.2 0.5 %collective-permute-start = (bf16[1,9,2,2,2,128,128]{6,5,4,3,2,1,0:T(8,128)(2,1)S(1)}, bf16[1,9,2,2,2,128,128]{6,5,4,3,2,1,0:T(8,128)(2,1)S(1)}, u32[]{:S(2)}, u32[]{:S(2)}) collective-permute-start(bf16[1,9,2,2,2,128,128]{6,5,4,3,2,1,0:T(8,128)(2,1)S(1)} %get-tuple-element.16.operator.op_mine), channel_id=1, source_target_pairs={{0,2},{1,3},{2,0},{3,1},{4,6},{5,7},{6,4},{7,5},{8,10},{9,11},{10,... | collective-permute-start | bytes 7077896 | tf_op jit(solution)/shard_map/ppermute | solution.py:349
  3.8 2.6 %collective-permute-start.4 = (bf16[4,16,128]{2,1,0:T(8,128)(2,1)S(1)}, bf16[4,16,128]{2,1,0:T(8,128)(2,1)S(1)}, u32[]{:S(2)}, u32[]{:S(2)}) collective-permute-start(bf16[4,16,128]{2,1,0:T(8,128)(2,1)S(1)} %get-tuple-element.18.refs_0_), channel_id=1, source_target_pairs={{0,3},{1,2},{2,1},{3,0},{4,7},{5,6},{6,5},{7,4},{8,11},{9,10},{10,... | collective-permute-start | bytes 49160 | tf_op jit(solution)/shard_map/ppermute | solution.py:349
  6.4 0.1 collective-permute-start.3
  6.5 0.3 %collective-permute-start.2 = (bf16[4,16,128]{2,1,0:T(8,128)(2,1)S(1)}, bf16[4,16,128]{2,1,0:T(8,128)(2,1)S(1)}, u32[]{:S(2)}, u32[]{:S(2)}) collective-permute-start(bf16[4,16,128]{2,1,0:T(8,128)(2,1)S(1)} %get-tuple-element.18.refs_0_), channel_id=1, source_target_pairs={{0,1},{1,0},{2,3},{3,2},{4,5},{5,4},{6,7},{7,6},{8,9},{9,8},{10,11... | collective-permute-start | bytes 49160 | tf_op jit(solution)/shard_map/ppermute | solution.py:349
  6.8 4.5 %collective-permute-start.1 = (bf16[2,2,2,128,128]{4,3,2,1,0:T(8,128)(2,1)S(1)}, bf16[2,2,2,128,128]{4,3,2,1,0:T(8,128)(2,1)S(1)}, u32[]{:S(2)}, u32[]{:S(2)}) collective-permute-start(bf16[2,2,2,128,128]{4,3,2,1,0:T(8,128)(2,1)S(1)} %get-tuple-element.17), channel_id=1, source_target_pairs={{0,30},{1,31},{2,4},{3,5},{4,2},{5,3},{6,8},{7,9},{8,6},{9,7},{10,... | collective-permute-start | bytes 786440 | tf_op jit(solution)/shard_map/ppermute | solution.py:349
  11.3 0.0 collective-permute-done.4.refs_3_
  11.3 0.0 collective-permute-done.3.refs_2_
  11.3 0.0 collective-permute-done.2.refs_1_
  11.3 0.5 %gather.1 = (bf16[2,2,2,16,128]{4,3,2,1,0:T(8,128)(2,1)S(1)}, bf16[2,2,2,16,128]{4,3,2,1,0:T(8,128)(2,1)S(1)}, bf16[2,2,2,16,128]{4,3,2,1,0:T(8,128)(2,1)S(1)}, ...) custom-call(bf16[1,9,2,2,2,128,128]{6,5,4,3,2,1,0:T(8,128)(2,1)S(1)}, ...), custom_call_target="tpu_custom_call" | custom-call | flops 10000000000 | tf_op jit(solution)/shard_map/gather/pallas_call | solution.py:326
  11.8 2.4 %collective-permute-start.5 = (bf16[2,2,2,2,16,128]{5,4,3,2,1,0:T(8,128)(2,1)S(1)}, bf16[2,2,2,2,16,128]{5,4,3,2,1,0:T(8,128)(2,1)S(1)}, u32[]{:S(2)}, u32[]{:S(2)}) collective-permute-start(bf16[2,2,2,2,16,128]{5,4,3,2,1,0:T(8,128)(2,1)S(1)} %get-tuple-element.20.sent), channel_id=1, source_target_pairs={{0,30},{1,31},{2,4},{3,5},{4,2},{5,3},{6,8},{7,9},{8,6},{9,7},{10,... | collective-permute-start | bytes 196616 | tf_op jit(solution)/shard_map/ppermute | solution.py:349
  14.2 1.1 %collective-permute-start.6 = (bf16[2,2,2,16,128]{4,3,2,1,0:T(8,128)(2,1)S(1)}, bf16[2,2,2,16,128]{4,3,2,1,0:T(8,128)(2,1)S(1)}, u32[]{:S(2)}, u32[]{:S(2)}) collective-permute-start(bf16[2,2,2,16,128]{4,3,2,1,0:T(8,128)(2,1)S(1)} %get-tuple-element.24.other), channel_id=1, source_target_pairs={{0,28},{1,29},{2,6},{3,7},{4,0},{5,1},{6,10},{7,11},{8,4},{9,5},{1... | collective-permute-start | bytes 98312 | tf_op jit(solution)/shard_map/ppermute | solution.py:349
  15.3 0.0 collective-permute-done.operator.op_pair
  15.3 0.5 %pair_one.1.part_pair = f32[2,2,2,16,128]{4,3,2,1,0:T(8,128)S(1)} custom-call(bf16[1,9,2,2,2,128,128]{6,5,4,3,2,1,0:T(8,128)(2,1)S(1)} %collective-permute-done.operator.op_pair, bf16[2,2,2,16,128]{4,3,2,1,0:T(8,128)(2,1)S(1)} %get-tuple-element.22.rhs_pair, bf16[2,2,2,16,128]{4,3,2,1,0:T(8,128)(2,1)S(1)} %get-tuple-element.23.here, ...), custom_call_target="tpu_custom_call" | custom-call | tf_op jit(solution)/shard_map/pair_one/pallas_call | solution.py:326
  15.8 3.1 %collective-permute-done.6.far = bf16[2,2,2,16,128]{4,3,2,1,0:T(8,128)(2,1)S(1)} collective-permute-done((bf16[2,2,2,16,128]{4,3,2,1,0:T(8,128)(2,1)S(1)}, bf16[2,2,2,16,128]{4,3,2,1,0:T(8,128)(2,1)S(1)}, u32[]{:S(2)}, u32[]{:S(2)}) %collective-permute-start.6) | collective-permute-done | bytes 32800 | tf_op jit(solution)/shard_map/ppermute | solution.py:349
  18.9 0.0 collective-permute-done.5.near
  18.9 0.0 collective-permute-done.1.back_near
  18.9 0.9 %second.1 = (bf16[2,2,2,16,128]{4,3,2,1,0:T(8,128)(2,1)S(1)}, f32[2,2,2,16,128]{4,3,2,1,0:T(8,128)S(1)}) custom-call(bf16[1,9,2,2,2,128,128]{6,5,4,3,2,1,0:T(8,128)(2,1)S(1)} %get-tuple-element.16.operator.op_mine, bf16[1,9,2,2,2,128,128]{6,5,4,3,2,1,0:T(8,128)(2,1)S(1)} %collective-permute-done.operator.op_pair, ...), custom_call_target="tpu_custom_call" | custom-call | tf_op jit(solution)/shard_map/second/pallas_call | solution.py:326
  19.9 0.0 collective-permute-start.7
  19.9 1.2 %collective-permute-done.7.field_pair.here = bf16[2,2,2,16,128]{4,3,2,1,0:T(8,128)(2,1)S(1)} collective-permute-done((bf16[2,2,2,16,128]{4,3,2,1,0:T(8,128)(2,1)S(1)}, bf16[2,2,2,16,128]{4,3,2,1,0:T(8,128)(2,1)S(1)}, u32[]{:S(2)}, u32[]{:S(2)}) %collective-permute-start.7) | collective-permute-done | bytes 32800 | tf_op jit(solution)/shard_map/ppermute | solution.py:349
  21.1 0.5 %third.1 = (bf16[2,2,2,2,16,128]{5,4,3,2,1,0:T(8,128)(2,1)S(1)}, f32[2,2,2,16,128]{4,3,2,1,0:T(8,128)S(1)}) custom-call(bf16[1,9,2,2,2,128,128]{6,5,4,3,2,1,0:T(8,128)(2,1)S(1)} %get-tuple-element.16.operator.op_mine, bf16[2,2,2,16,128]{4,3,2,1,0:T(8,128)(2,1)S(1)} %get-tuple-element.19.rhs_mine, ...), custom_call_target="tpu_custom_call" | custom-call | tf_op jit(solution)/shard_map/third/pallas_call | solution.py:326
  21.6 3.0 %collective-permute-start.8 = (bf16[2,2,2,2,16,128]{5,4,3,2,1,0:T(8,128)(2,1)S(1)}, bf16[2,2,2,2,16,128]{5,4,3,2,1,0:T(8,128)(2,1)S(1)}, u32[]{:S(2)}, u32[]{:S(2)}) collective-permute-start(bf16[2,2,2,2,16,128]{5,4,3,2,1,0:T(8,128)(2,1)S(1)} %get-tuple-element.27.sent), channel_id=1, source_target_pairs={{0,30},{1,31},{2,4},{3,5},{4,2},{5,3},{6,8},{7,9},{8,6},{9,7},{10,... | collective-permute-start | bytes 196616 | tf_op jit(solution)/shard_map/ppermute | solution.py:349
  24.6 1.0 %collective-permute-start.9 = (bf16[2,2,2,16,128]{4,3,2,1,0:T(8,128)(2,1)S(1)}, bf16[2,2,2,16,128]{4,3,2,1,0:T(8,128)(2,1)S(1)}, u32[]{:S(2)}, u32[]{:S(2)}) collective-permute-start(bf16[2,2,2,16,128]{4,3,2,1,0:T(8,128)(2,1)S(1)} %get-tuple-element.25.field_mine.other), channel_id=1, source_target_pairs={{0,28},{1,29},{2,6},{3,7},{4,0},{5,1},{6,10},{7,11},{8,4},{9,5},{1... | collective-permute-start | bytes 98312 | tf_op jit(solution)/shard_map/ppermute | solution.py:349
  25.6 0.5 %pair_two.1.part_pair = f32[2,2,2,16,128]{4,3,2,1,0:T(8,128)S(1)} custom-call(bf16[1,9,2,2,2,128,128]{6,5,4,3,2,1,0:T(8,128)(2,1)S(1)} %collective-permute-done.operator.op_pair, bf16[2,2,2,16,128]{4,3,2,1,0:T(8,128)(2,1)S(1)} %get-tuple-element.22.rhs_pair, bf16[2,2,2,16,128]{4,3,2,1,0:T(8,128)(2,1)S(1)} %collective-permute-done.7.field_pair.here, ...), custom_call_target="tpu_custom_call" | custom-call | tf_op jit(solution)/shard_map/pair_two/pallas_call | solution.py:326
  26.1 2.6 %collective-permute-done.9.far = bf16[2,2,2,16,128]{4,3,2,1,0:T(8,128)(2,1)S(1)} collective-permute-done((bf16[2,2,2,16,128]{4,3,2,1,0:T(8,128)(2,1)S(1)}, bf16[2,2,2,16,128]{4,3,2,1,0:T(8,128)(2,1)S(1)}, u32[]{:S(2)}, u32[]{:S(2)}) %collective-permute-start.9) | collective-permute-done | bytes 32800 | tf_op jit(solution)/shard_map/ppermute | solution.py:349
  28.7 0.0 collective-permute-done.8.near
  28.7 2.7 %last.1 = (bf16[4,2,12,16,256]{4,3,2,1,0:T(8,128)(2,1)}, bf16[1,2,2,2,16,128]{5,4,3,2,1,0:T(8,128)(2,1)}) custom-call(bf16[1,9,2,2,2,128,128]{6,5,4,3,2,1,0:T(8,128)(2,1)S(1)} %get-tuple-element.16.operator.op_mine, bf16[1,9,2,2,2,128,128]{6,5,4,3,2,1,0:T(8,128)(2,1)S(1)} %collective-permute-done.operator.op_pair, ...), custom_call_target="tpu_custom_call" | custom-call | tf_op jit(solution)/shard_map/last/pallas_call | solution.py:297
Async XLA Ops:
  3.2 12.1 %collective-permute-start = (bf16[1,9,2,2,2,128,128]{6,5,4,3,2,1,0:T(8,128)(2,1)S(1)}, bf16[1,9,2,2,2,128,128]{6,5,4,3,2,1,0:T(8,128)(2,1)S(1)}, u32[]{:S(2)}, u32[]{:S(2)}) collective-permute-start(bf16[1,9,2,2,2,128,128]{6,5,4,3,2,1,0:T(8,128)(2,1)S(1)} %get-tuple-element.16.operator.op_mine), channel_id=1, source_target_pairs={{0,2},{1,3},{2,0},{3,1},{4,6},{5,7},{6,4},{7,5},{8,10},{9,11},{10,... | collective-permute-start | bytes 7077896 | tf_op jit(solution)/shard_map/ppermute | solution.py:349
  3.8 7.5 %collective-permute-start.4 = (bf16[4,16,128]{2,1,0:T(8,128)(2,1)S(1)}, bf16[4,16,128]{2,1,0:T(8,128)(2,1)S(1)}, u32[]{:S(2)}, u32[]{:S(2)}) collective-permute-start(bf16[4,16,128]{2,1,0:T(8,128)(2,1)S(1)} %get-tuple-element.18.refs_0_), channel_id=1, source_target_pairs={{0,3},{1,2},{2,1},{3,0},{4,7},{5,6},{6,5},{7,4},{8,11},{9,10},{10,... | collective-permute-start | bytes 49160 | tf_op jit(solution)/shard_map/ppermute | solution.py:349
  6.4 4.9 %collective-permute-start.3 = (bf16[4,16,128]{2,1,0:T(8,128)(2,1)S(1)}, bf16[4,16,128]{2,1,0:T(8,128)(2,1)S(1)}, u32[]{:S(2)}, u32[]{:S(2)}) collective-permute-start(bf16[4,16,128]{2,1,0:T(8,128)(2,1)S(1)} %get-tuple-element.18.refs_0_), channel_id=1, source_target_pairs={{0,2},{1,3},{2,0},{3,1},{4,6},{5,7},{6,4},{7,5},{8,10},{9,11},{10,... | collective-permute-start | bytes 49160 | tf_op jit(solution)/shard_map/ppermute | solution.py:349
  6.5 4.8 %collective-permute-start.2 = (bf16[4,16,128]{2,1,0:T(8,128)(2,1)S(1)}, bf16[4,16,128]{2,1,0:T(8,128)(2,1)S(1)}, u32[]{:S(2)}, u32[]{:S(2)}) collective-permute-start(bf16[4,16,128]{2,1,0:T(8,128)(2,1)S(1)} %get-tuple-element.18.refs_0_), channel_id=1, source_target_pairs={{0,1},{1,0},{2,3},{3,2},{4,5},{5,4},{6,7},{7,6},{8,9},{9,8},{10,11... | collective-permute-start | bytes 49160 | tf_op jit(solution)/shard_map/ppermute | solution.py:349
  6.8 12.1 %collective-permute-start.1 = (bf16[2,2,2,128,128]{4,3,2,1,0:T(8,128)(2,1)S(1)}, bf16[2,2,2,128,128]{4,3,2,1,0:T(8,128)(2,1)S(1)}, u32[]{:S(2)}, u32[]{:S(2)}) collective-permute-start(bf16[2,2,2,128,128]{4,3,2,1,0:T(8,128)(2,1)S(1)} %get-tuple-element.17), channel_id=1, source_target_pairs={{0,30},{1,31},{2,4},{3,5},{4,2},{5,3},{6,8},{7,9},{8,6},{9,7},{10,... | collective-permute-start | bytes 786440 | tf_op jit(solution)/shard_map/ppermute | solution.py:349
  11.8 7.1 %collective-permute-start.5 = (bf16[2,2,2,2,16,128]{5,4,3,2,1,0:T(8,128)(2,1)S(1)}, bf16[2,2,2,2,16,128]{5,4,3,2,1,0:T(8,128)(2,1)S(1)}, u32[]{:S(2)}, u32[]{:S(2)}) collective-permute-start(bf16[2,2,2,2,16,128]{5,4,3,2,1,0:T(8,128)(2,1)S(1)} %get-tuple-element.20.sent), channel_id=1, source_target_pairs={{0,30},{1,31},{2,4},{3,5},{4,2},{5,3},{6,8},{7,9},{8,6},{9,7},{10,... | collective-permute-start | bytes 196616 | tf_op jit(solution)/shard_map/ppermute | solution.py:349
  14.2 4.7 %collective-permute-start.6 = (bf16[2,2,2,16,128]{4,3,2,1,0:T(8,128)(2,1)S(1)}, bf16[2,2,2,16,128]{4,3,2,1,0:T(8,128)(2,1)S(1)}, u32[]{:S(2)}, u32[]{:S(2)}) collective-permute-start(bf16[2,2,2,16,128]{4,3,2,1,0:T(8,128)(2,1)S(1)} %get-tuple-element.24.other), channel_id=1, source_target_pairs={{0,28},{1,29},{2,6},{3,7},{4,0},{5,1},{6,10},{7,11},{8,4},{9,5},{1... | collective-permute-start | bytes 98312 | tf_op jit(solution)/shard_map/ppermute | solution.py:349
  19.9 1.2 %collective-permute-start.7 = (bf16[2,2,2,16,128]{4,3,2,1,0:T(8,128)(2,1)S(1)}, bf16[2,2,2,16,128]{4,3,2,1,0:T(8,128)(2,1)S(1)}, u32[]{:S(2)}, u32[]{:S(2)}) collective-permute-start(bf16[2,2,2,16,128]{4,3,2,1,0:T(8,128)(2,1)S(1)} %get-tuple-element.25.field_mine.other), channel_id=1, source_target_pairs={{0,2},{1,3},{2,0},{3,1},{4,6},{5,7},{6,4},{7,5},{8,10},{9,11},{10,... | collective-permute-start | bytes 98312 | tf_op jit(solution)/shard_map/ppermute | solution.py:349
  21.6 7.1 %collective-permute-start.8 = (bf16[2,2,2,2,16,128]{5,4,3,2,1,0:T(8,128)(2,1)S(1)}, bf16[2,2,2,2,16,128]{5,4,3,2,1,0:T(8,128)(2,1)S(1)}, u32[]{:S(2)}, u32[]{:S(2)}) collective-permute-start(bf16[2,2,2,2,16,128]{5,4,3,2,1,0:T(8,128)(2,1)S(1)} %get-tuple-element.27.sent), channel_id=1, source_target_pairs={{0,30},{1,31},{2,4},{3,5},{4,2},{5,3},{6,8},{7,9},{8,6},{9,7},{10,... | collective-permute-start | bytes 196616 | tf_op jit(solution)/shard_map/ppermute | solution.py:349
  24.6 4.1 %collective-permute-start.9 = (bf16[2,2,2,16,128]{4,3,2,1,0:T(8,128)(2,1)S(1)}, bf16[2,2,2,16,128]{4,3,2,1,0:T(8,128)(2,1)S(1)}, u32[]{:S(2)}, u32[]{:S(2)}) collective-permute-start(bf16[2,2,2,16,128]{4,3,2,1,0:T(8,128)(2,1)S(1)} %get-tuple-element.25.field_mine.other), channel_id=1, source_target_pairs={{0,28},{1,29},{2,6},{3,7},{4,0},{5,1},{6,10},{7,11},{8,4},{9,5},{1... | collective-permute-start | bytes 98312 | tf_op jit(solution)/shard_map/ppermute | solution.py:349

commit v4 on v3

--- a/solution.py
+++ b/solution.py
@@ -88,30 +88,30 @@
 
 
 def prolong(column, null_ref, out_ref, held, done):
-    aggregates = len(column)
-    coarse_y = aggregates // CZ
+    coarse_y = len(column) // CZ
     times, _, _, rhs, sites = held.shape
     vectors = null_ref.shape[3]
-    ids = aggregate_ids((2 * rhs, sites), coarse_y)
-    masks = [ids == a for a in range(aggregates)]
+    ids = aggregate_ids((2 * vectors, sites), coarse_y)
+    masks = [(lax.rem(ids, CZ) == z).astype(jnp.float32).astype(jnp.bfloat16) for z in range(CZ)]
+    rows = aggregate_ids((2 * rhs, sites), coarse_y) // CZ
     mixers = []
     for h in range(2):
         mixer = []
-        for a in range(aggregates):
-            weights = column[a]
-            real = weights[:, h * vectors : (h + 1) * vectors]
-            imag = weights[:, (2 + h) * vectors : (3 + h) * vectors]
-            mixer.append(jnp.concatenate([real, -imag], axis=1))
-            mixer.append(jnp.concatenate([imag, real], axis=1))
+        for y in range(coarse_y):
+            real = [column[y * CZ + z][:, h * vectors : (h + 1) * vectors] for z in range(CZ)]
+            imag = [column[y * CZ + z][:, (2 + h) * vectors : (3 + h) * vectors] for z in range(CZ)]
+            mixer.append(jnp.concatenate([part for z in range(CZ) for part in (real[z], -imag[z])], axis=1))
+            mixer.append(jnp.concatenate([part for z in range(CZ) for part in (imag[z], real[z])], axis=1))
         mixers.append(jnp.concatenate(mixer, axis=0))
     copies = []
     for t in range(times):
         for c in range(12):
             null = jnp.concatenate([null_ref[t, 0, c], null_ref[t, 1, c]], axis=0)
+            null = jnp.concatenate([null * mask for mask in masks], axis=0)
             every = jnp.dot(mixers[c // 6], null, preferred_element_type=jnp.float32)
             result = every[: 2 * rhs]
-            for a in range(1, aggregates):
-                result = jnp.where(masks[a], every[a * 2 * rhs : (a + 1) * 2 * rhs], result)
+            for y in range(1, coarse_y):
+                result = jnp.where(rows == y, every[y * 2 * rhs : (y + 1) * 2 * rhs], result)
             result = result.astype(held.dtype)
             held[t, 0, c] = result[:rhs]
             held[t, 1, c] = result[rhs:]
@@ -138,21 +138,26 @@
                 lax.fori_loop(0, extent[2], lambda x, c, y=y, z=z: (body((y, z, x)), c)[1], 0)
 
 
+def nearby(site, extent):
+    found = [site]
+    for axis in range(3):
+        for step in [1] if extent[axis] == 2 else [1, extent[axis] - 1]:
+            moved = site[axis] + step
+            moved = lax.rem(moved, extent[axis]) if axis == 2 else moved % extent[axis]
+            found.append(site[:axis] + (moved,) + site[axis + 1 :])
+    return found
+
+
 def around(operator, site, extent):
-    found = [(operator[(0, 0) + site], site)]
+    blocks = [operator[(0, 0) + site]]
     for axis in range(3):
-        up, down = [
-            site[:axis] + (lax.rem(site[axis] + step, extent[axis]) if axis == 2 else (site[axis] + step) % extent[axis],)
-            + site[axis + 1 :]
-            for step in (1, extent[axis] - 1)
-        ]
         ahead, behind = operator[(0, 3 + 2 * axis) + site], operator[(0, 4 + 2 * axis) + site]
         if extent[axis] == 2:
             both = ahead.astype(jnp.float32) + behind.astype(jnp.float32)
-            found.append((both.astype(jnp.bfloat16), up))
+            blocks.append(both.astype(jnp.bfloat16))
         else:
-            found += [(ahead, up), (behind, down)]
-    return found
+            blocks += [ahead, behind]
+    return list(zip(blocks, nearby(site, extent)))
 
 
 def products(pairs):
@@ -162,6 +167,19 @@
         LANES,
         preferred_element_type=jnp.float32,
     )
+
+
+def packed(operator, site, times):
+    blocks = [block for block, _ in around(operator, site, operator.shape[2:5])]
+    blocks += [operator[(0, d) + site] for d in times]
+    return jnp.concatenate([block.T for block in blocks], axis=0)
+
+
+def packed_stencil(weights, site, here, times):
+    extent = weights.shape[:3]
+    fields = [here[near] for near in nearby(site, extent)] + [field[site] for field in times]
+    depth = len(fields) * weights.shape[4]
+    return jnp.dot(jnp.concatenate(fields, axis=1), weights[site][:depth], preferred_element_type=jnp.float32)
 
 
 def stencil(operator, site, here, times):
@@ -208,18 +226,25 @@
     for_sites(extent, step)
 
 
-def pair_kernel(scaled, operator, rhs_pair, here, other, part_pair):
-    even, _ = time_sides(False)
+def first_pair_kernel(op_mine, op_pair, rhs_pair, here, other, part_pair, packed_mine, packed_pair):
+    sides, pair_sides = time_sides(True), time_sides(False)
 
     def step(site):
-        sums = stencil(operator, site, here, [(even, other)])
-        if scaled:
-            value = RELAX_WEIGHT * rhs_pair[site].astype(jnp.float32)
-        else:
-            value = here[site].astype(jnp.float32)
+        packed_mine[site] = packed(op_mine, site, sides)
+        packed_pair[site] = packed(op_pair, site, pair_sides)
+        sums = packed_stencil(packed_pair, site, here, [other])
+        value = RELAX_WEIGHT * rhs_pair[site].astype(jnp.float32)
         part_pair[site] = relaxed(value, here[site], rhs_pair[site], sums)
 
-    for_sites(operator.shape[2:5], step)
+    for_sites(op_mine.shape[2:5], step)
+
+
+def second_pair_kernel(packed_pair, rhs_pair, here, other, part_pair):
+    def step(site):
+        sums = packed_stencil(packed_pair, site, here, [other])
+        part_pair[site] = relaxed(here[site].astype(jnp.float32), here[site], rhs_pair[site], sums)
+
+    for_sites(packed_pair.shape[:3], step)
 
 
 def second_kernel(
@@ -233,49 +258,50 @@
         value_mine[site] = value
         field_mine[site] = value.astype(jnp.bfloat16)
 
-    for_sites(op_mine.shape[2:5], second)
+    for_sites(op_mine.shape[:3], second)
 
 
 def halfway(op_mine, op_pair, back_near, sent, part_mine, part_pair, near, far, one_mine, one_pair, one_near, x_mine):
-    _, odd = time_sides(True)
-    _, pair_odd = time_sides(False)
+    depth, columns = op_mine.shape[3:]
+    side = slice(depth - columns, depth)
 
     def first(site):
-        value = part_mine[site] - RELAX_WEIGHT * products([(op_mine[(0, odd) + site], near[(0,) + site])])
+        value = part_mine[site] - RELAX_WEIGHT * product(near[(0,) + site], op_mine[site][side])
         x_mine[site] = value
         one_mine[site] = value.astype(jnp.bfloat16)
-        value = part_pair[site] - RELAX_WEIGHT * products([(op_pair[(0, pair_odd) + site], far[site])])
+        value = part_pair[site] - RELAX_WEIGHT * product(far[site], op_pair[site][side])
         one_pair[site] = value.astype(jnp.bfloat16)
         value = near[(1,) + site].astype(jnp.float32) - RELAX_WEIGHT * products([(back_near[site], sent[(0,) + site])])
         one_near[site] = value.astype(jnp.bfloat16)
 
-    for_sites(op_mine.shape[2:5], first)
+    for_sites(op_mine.shape[:3], first)
+
+
+def product(field, weights):
+    return jnp.dot(field, weights, preferred_element_type=jnp.float32)
 
 
 def second_step(op_mine, rhs_mine, one_mine, one_pair, one_near, x_mine, site):
-    even, odd = time_sides(True)
-    sums = stencil(op_mine, site, one_mine, [(even, one_pair), (odd, one_near)])
+    sums = packed_stencil(op_mine, site, one_mine, [one_pair, one_near])
     return relaxed(x_mine[site], one_mine[site], rhs_mine[site], sums)
 
 
 def third_kernel(op_mine, rhs_mine, field_mine, value_mine, field_pair, message, part_next):
-    even, _ = time_sides(True)
-
     def third(site):
-        sums = stencil(op_mine, site, field_mine, [(even, field_pair)])
+        sums = packed_stencil(op_mine, site, field_mine, [field_pair])
         part = relaxed(value_mine[site], field_mine[site], rhs_mine[site], sums)
         part_next[site] = part
         message[(0,) + site] = field_mine[site]
         message[(1,) + site] = part.astype(jnp.bfloat16)
 
-    for_sites(op_mine.shape[2:5], third)
+    for_sites(op_mine.shape[:3], third)
 
 
 def last_kernel(
     op_mine, op_pair, back_near, rhs_mine, sent, part_mine, part_pair, near, far, null,
     fine_out, coarse_out, one_mine, one_pair, one_near, x_mine, result, held, done,
 ):
-    extent = op_mine.shape[2:5]
+    extent = op_mine.shape[:3]
     halfway(op_mine, op_pair, back_near, sent, part_mine, part_pair, near, far, one_mine, one_pair, one_near, x_mine)
 
     def second(site):
@@ -312,6 +338,11 @@
         compiler_params=pltpu.CompilerParams(vmem_limit_bytes=KERNEL_VMEM),
         name="last",
     )(*[in_vmem(operand) for operand in operands])
+
+
+def packed_depth(operator):
+    blocks = 3 + sum(1 if length == 2 else 2 for length in operator.shape[2:5])
+    return blocks * operator.shape[6]
 
 
 def in_hbm(array):
@@ -376,30 +407,33 @@
         flops=GATHER_FLOPS,
     )
     near_message, far_field = send(sent, across), send(start_mine, far)
-    (part_pair,) = kernel_call(
-        functools.partial(pair_kernel, True), "pair_one", [(full, f32)], [],
-        op_pair, rhs_pair, start_pair, start_mine,
+    (part_pair, packed_mine, packed_pair) = kernel_call(
+        first_pair_kernel,
+        "pair_one",
+        [(full, f32)] + [(extent + (packed_depth(operator), operator.shape[6]), bf16)] * 2,
+        [],
+        operator, op_pair, rhs_pair, start_pair, start_mine,
     )
     field_mine, value_mine = kernel_call(
         second_kernel,
         "second",
         [(full, bf16), (full, f32)],
         [(full, bf16)] * 3 + [(full, f32)],
-        operator, op_pair, back_near, rhs_mine, sent, part_mine, part_pair, near_message, far_field,
+        packed_mine, packed_pair, back_near, rhs_mine, sent, part_mine, part_pair, near_message, far_field,
     )
     field_pair = send(field_mine, other)
     sent, part_mine = kernel_call(
         third_kernel, "third", [((2,) + full, bf16), (full, f32)], [],
-        operator, rhs_mine, field_mine, value_mine, field_pair,
+        packed_mine, rhs_mine, field_mine, value_mine, field_pair,
     )
     near_message, far_field = send(sent, across), send(field_mine, far)
     (part_pair,) = kernel_call(
-        functools.partial(pair_kernel, False), "pair_two", [(full, f32)], [],
-        op_pair, rhs_pair, field_pair, field_mine,
+        second_pair_kernel, "pair_two", [(full, f32)], [],
+        packed_pair, rhs_pair, field_pair, field_mine,
     )
     fine_correction, coarse_iterate = last(
         fine_vectors.shape,
-        operator, op_pair, back_near, rhs_mine, sent, part_mine, part_pair, near_message, far_field, null_kept,
+        packed_mine, packed_pair, back_near, rhs_mine, sent, part_mine, part_pair, near_message, far_field, null_kept,
     )
     return (fine_correction, coarse_iterate)
 

time: 31.5 us -> 30.5 us (0.968)
  Pallas kernels: 8.28 us -> 7.35 us
    pallas_call x1, Pallas kernels: 2.68 us -> 1.95 us  [last(): pl.pallas_call(last_kernel, in_specs=[pl.BlockSpec(memory_space=pltpu.VME...]
  transfers between devices with their start and end apart: 10 -> 10, of which waited for: 3 -> 3; matrix products, arithmetic and copies ran while one was open for 0% -> 0% of each run, Pallas kernels for 5% -> 6%
where the time goes in v4:
time: 30.5 us; the launch traced here: 30.3 us
  starting transfers between devices  15.5 us (51%)
  Pallas kernels  7.35 us (24%)
  waiting for transfers between devices  6.76 us (22%)
  between operations  0.66 us (2%)
    ppermute x10, starting transfers between devices, send(): return lax.ppermute(array, ('zt', 'xy'), permutation(target, turn))  15.5 us
    ppermute x10, waiting for transfers between devices, send(): return lax.ppermute(array, ('zt', 'xy'), permutation(target, turn))  6.76 us
    pallas_call x5, Pallas kernels, kernel_call(): pl.pallas_call(kernel, in_specs=[pl.BlockSpec(memory_space=pltpu.VMEM)] *...  2.8 us
    pallas_call x1, Pallas kernels, restrict(): pl.pallas_call(functools.partial(restrict_kernel, coarse_y), in_specs=[pl...  2.6 us
    pallas_call x1, Pallas kernels, last(): pl.pallas_call(last_kernel, in_specs=[pl.BlockSpec(memory_space=pltpu.VME...  1.95 us
  transfers between devices with their start and end apart: 10, of which 3 were waited for; matrix products, arithmetic and copies ran while one was open for 0% of the time, Pallas kernels for 6%

profile of v4, /device:TPU:0, one launch (start us, length us, event | category | flops | bytes accessed | tf_op | source)
XLA Modules:
  0.0 30.3 jit_solution(11279936445654626595)
XLA Ops:
  0.6 2.6 %restrict.1 = (bf16[4,16,128]{2,1,0:T(8,128)(2,1)S(1)}, bf16[4,2,12,32,256]{4,3,2,1,0:T(8,128)(2,1)S(1)}, bf16[1,9,2,2,2,128,128]{6,5,4,3,2,1,0:T(8,128)(2,1)S(1)}, bf16[2,2,2,128,128]{4,3,2,1,0:T(8,128)(2,1)S(1)}) custom-call(bf16[4,2,12,16,256]{4,3,2,1,0:T(8,128)(2,1)} %fine_hbm.1, bf16[4,2,12,32,256]{4,3,2,1,0:T(8,128)(2,1)} %null_hbm.1, ...), custom_call_target="tpu_custom_call" | custom-call | tf_op jit(solution)/shard_map/restrict/pallas_call | solution.py:74
  3.2 0.5 %collective-permute-start = (bf16[1,9,2,2,2,128,128]{6,5,4,3,2,1,0:T(8,128)(2,1)S(1)}, bf16[1,9,2,2,2,128,128]{6,5,4,3,2,1,0:T(8,128)(2,1)S(1)}, u32[]{:S(2)}, u32[]{:S(2)}) collective-permute-start(bf16[1,9,2,2,2,128,128]{6,5,4,3,2,1,0:T(8,128)(2,1)S(1)} %get-tuple-element.19.operator.op_mine), channel_id=1, source_target_pairs={{0,2},{1,3},{2,0},{3,1},{4,6},{5,7},{6,4},{7,5},{8,10},{9,11},{10,... | collective-permute-start | bytes 7077896 | tf_op jit(solution)/shard_map/ppermute | solution.py:380
  3.8 2.6 %collective-permute-start.1 = (bf16[4,16,128]{2,1,0:T(8,128)(2,1)S(1)}, bf16[4,16,128]{2,1,0:T(8,128)(2,1)S(1)}, u32[]{:S(2)}, u32[]{:S(2)}) collective-permute-start(bf16[4,16,128]{2,1,0:T(8,128)(2,1)S(1)} %get-tuple-element.20.refs_0_), channel_id=1, source_target_pairs={{0,1},{1,0},{2,3},{3,2},{4,5},{5,4},{6,7},{7,6},{8,9},{9,8},{10,11... | collective-permute-start | bytes 49160 | tf_op jit(solution)/shard_map/ppermute | solution.py:380
  6.3 0.2 collective-permute-start.2
  6.5 0.0 collective-permute-start.3
  6.5 4.7 %collective-permute-start.4 = (bf16[2,2,2,128,128]{4,3,2,1,0:T(8,128)(2,1)S(1)}, bf16[2,2,2,128,128]{4,3,2,1,0:T(8,128)(2,1)S(1)}, u32[]{:S(2)}, u32[]{:S(2)}) collective-permute-start(bf16[2,2,2,128,128]{4,3,2,1,0:T(8,128)(2,1)S(1)} %get-tuple-element.26), channel_id=1, source_target_pairs={{0,30},{1,31},{2,4},{3,5},{4,2},{5,3},{6,8},{7,9},{8,6},{9,7},{10,... | collective-permute-start | bytes 786440 | tf_op jit(solution)/shard_map/ppermute | solution.py:380
  11.3 0.0 collective-permute-done.1.refs_1_
  11.3 0.0 collective-permute-done.2.refs_2_
  11.3 0.0 collective-permute-done.3.refs_3_
  11.3 0.5 %gather.1 = (bf16[2,2,2,16,128]{4,3,2,1,0:T(8,128)(2,1)S(1)}, bf16[2,2,2,16,128]{4,3,2,1,0:T(8,128)(2,1)S(1)}, bf16[2,2,2,16,128]{4,3,2,1,0:T(8,128)(2,1)S(1)}, ...) custom-call(bf16[1,9,2,2,2,128,128]{6,5,4,3,2,1,0:T(8,128)(2,1)S(1)}, ...), custom_call_target="tpu_custom_call" | custom-call | flops 10000000000 | tf_op jit(solution)/shard_map/gather/pallas_call | solution.py:357
  11.8 3.2 %collective-permute-start.5 = (bf16[2,2,2,2,16,128]{5,4,3,2,1,0:T(8,128)(2,1)S(1)}, bf16[2,2,2,2,16,128]{5,4,3,2,1,0:T(8,128)(2,1)S(1)}, u32[]{:S(2)}, u32[]{:S(2)}) collective-permute-start(bf16[2,2,2,2,16,128]{5,4,3,2,1,0:T(8,128)(2,1)S(1)} %get-tuple-element.28.sent), channel_id=1, source_target_pairs={{0,30},{1,31},{2,4},{3,5},{4,2},{5,3},{6,8},{7,9},{8,6},{9,7},{10,... | collective-permute-start | bytes 196616 | tf_op jit(solution)/shard_map/ppermute | solution.py:380
  15.0 0.2 collective-permute-start.6
  15.2 0.0 collective-permute-done.op_pair
  15.2 1.0 %pair_one.1 = (f32[2,2,2,16,128]{4,3,2,1,0:T(8,128)S(1)}, bf16[2,2,2,768,128]{4,3,2,1,0:T(8,128)(2,1)S(1)}, bf16[2,2,2,768,128]{4,3,2,1,0:T(8,128)(2,1)S(1)}) custom-call(bf16[1,9,2,2,2,128,128]{6,5,4,3,2,1,0:T(8,128)(2,1)S(1)} %get-tuple-element.19.operator.op_mine, bf16[1,9,2,2,2,128,128]{6,5,4,3,2,1,0:T(8,128)(2,1)S(1)} %collective-permute-done.op_pair, ...), custom_call_target="tpu_custom_call" | custom-call | tf_op jit(solution)/shard_map/pair_one/pallas_call | solution.py:357
  16.3 2.6 %collective-permute-done.6.far = bf16[2,2,2,16,128]{4,3,2,1,0:T(8,128)(2,1)S(1)} collective-permute-done((bf16[2,2,2,16,128]{4,3,2,1,0:T(8,128)(2,1)S(1)}, bf16[2,2,2,16,128]{4,3,2,1,0:T(8,128)(2,1)S(1)}, u32[]{:S(2)}, u32[]{:S(2)}) %collective-permute-start.6) | collective-permute-done | bytes 32800 | tf_op jit(solution)/shard_map/ppermute | solution.py:380
  18.9 0.0 collective-permute-done.5.near
  18.9 0.0 collective-permute-done.4.back_near
  18.9 0.6 %second.1 = (bf16[2,2,2,16,128]{4,3,2,1,0:T(8,128)(2,1)S(1)}, f32[2,2,2,16,128]{4,3,2,1,0:T(8,128)S(1)}) custom-call(bf16[2,2,2,768,128]{4,3,2,1,0:T(8,128)(2,1)S(1)} %get-tuple-element.24.op_mine, bf16[2,2,2,768,128]{4,3,2,1,0:T(8,128)(2,1)S(1)} %get-tuple-element.25.op_pair.packed_pair, bf16[2,2,2,128,128]{4,3,2,1,0:T(8,128)(2,1)S(1)} %collective-permute-done.4.back_near, ...), custom_call_target="tpu_custom_call" | custom-call | tf_op jit(solution)/shard_map/second/pallas_call | solution.py:357
  19.5 0.1 collective-permute-start.7
  19.6 1.2 %collective-permute-done.7.field_pair.here = bf16[2,2,2,16,128]{4,3,2,1,0:T(8,128)(2,1)S(1)} collective-permute-done((bf16[2,2,2,16,128]{4,3,2,1,0:T(8,128)(2,1)S(1)}, bf16[2,2,2,16,128]{4,3,2,1,0:T(8,128)(2,1)S(1)}, u32[]{:S(2)}, u32[]{:S(2)}) %collective-permute-start.7) | collective-permute-done | bytes 32800 | tf_op jit(solution)/shard_map/ppermute | solution.py:380
  20.8 0.3 %third.1 = (bf16[2,2,2,2,16,128]{5,4,3,2,1,0:T(8,128)(2,1)S(1)}, f32[2,2,2,16,128]{4,3,2,1,0:T(8,128)S(1)}) custom-call(bf16[2,2,2,768,128]{4,3,2,1,0:T(8,128)(2,1)S(1)} %get-tuple-element.24.op_mine, bf16[2,2,2,16,128]{4,3,2,1,0:T(8,128)(2,1)S(1)} %get-tuple-element.27.rhs_mine, bf16[2,2,2,16,128]{4,3,2,1,0:T(8,128)(2,1)S(1)} %get-tuple-element.31.field_mine.other, ...), custom_call_target="tpu_custom_call" | custom-call | tf_op jit(solution)/shard_map/third/pallas_call | solution.py:357
  21.1 3.3 %collective-permute-start.8 = (bf16[2,2,2,2,16,128]{5,4,3,2,1,0:T(8,128)(2,1)S(1)}, bf16[2,2,2,2,16,128]{5,4,3,2,1,0:T(8,128)(2,1)S(1)}, u32[]{:S(2)}, u32[]{:S(2)}) collective-permute-start(bf16[2,2,2,2,16,128]{5,4,3,2,1,0:T(8,128)(2,1)S(1)} %get-tuple-element.33.sent), channel_id=1, source_target_pairs={{0,30},{1,31},{2,4},{3,5},{4,2},{5,3},{6,8},{7,9},{8,6},{9,7},{10,... | collective-permute-start | bytes 196616 | tf_op jit(solution)/shard_map/ppermute | solution.py:380
  24.4 0.7 %collective-permute-start.9 = (bf16[2,2,2,16,128]{4,3,2,1,0:T(8,128)(2,1)S(1)}, bf16[2,2,2,16,128]{4,3,2,1,0:T(8,128)(2,1)S(1)}, u32[]{:S(2)}, u32[]{:S(2)}) collective-permute-start(bf16[2,2,2,16,128]{4,3,2,1,0:T(8,128)(2,1)S(1)} %get-tuple-element.31.field_mine.other), channel_id=1, source_target_pairs={{0,28},{1,29},{2,6},{3,7},{4,0},{5,1},{6,10},{7,11},{8,4},{9,5},{1... | collective-permute-start | bytes 98312 | tf_op jit(solution)/shard_map/ppermute | solution.py:380
  25.1 0.3 %pair_two.1.part_pair = f32[2,2,2,16,128]{4,3,2,1,0:T(8,128)S(1)} custom-call(bf16[2,2,2,768,128]{4,3,2,1,0:T(8,128)(2,1)S(1)} %get-tuple-element.25.op_pair.packed_pair, bf16[2,2,2,16,128]{4,3,2,1,0:T(8,128)(2,1)S(1)} %get-tuple-element.21.rhs_pair, bf16[2,2,2,16,128]{4,3,2,1,0:T(8,128)(2,1)S(1)} %collective-permute-done.7.field_pair.here, ...), custom_call_target="tpu_custom_call" | custom-call | tf_op jit(solution)/shard_map/pair_two/pallas_call | solution.py:357
  25.4 2.9 %collective-permute-done.9.far = bf16[2,2,2,16,128]{4,3,2,1,0:T(8,128)(2,1)S(1)} collective-permute-done((bf16[2,2,2,16,128]{4,3,2,1,0:T(8,128)(2,1)S(1)}, bf16[2,2,2,16,128]{4,3,2,1,0:T(8,128)(2,1)S(1)}, u32[]{:S(2)}, u32[]{:S(2)}) %collective-permute-start.9) | collective-permute-done | bytes 32800 | tf_op jit(solution)/shard_map/ppermute | solution.py:380
  28.4 0.0 collective-permute-done.8.near
  28.4 2.0 %last.1 = (bf16[4,2,12,16,256]{4,3,2,1,0:T(8,128)(2,1)}, bf16[1,2,2,2,16,128]{5,4,3,2,1,0:T(8,128)(2,1)}) custom-call(bf16[2,2,2,768,128]{4,3,2,1,0:T(8,128)(2,1)S(1)} %get-tuple-element.24.op_mine, bf16[2,2,2,768,128]{4,3,2,1,0:T(8,128)(2,1)S(1)} %get-tuple-element.25.op_pair.packed_pair, bf16[2,2,2,128,128]{4,3,2,1,0:T(8,128)(2,1)S(1)} %collective-permute-done.4.back_near, ...), custom_call_target="tpu_custom_call" | custom-call | tf_op jit(solution)/shard_map/last/pallas_call | solution.py:323
Async XLA Ops:
  3.2 12.0 %collective-permute-start = (bf16[1,9,2,2,2,128,128]{6,5,4,3,2,1,0:T(8,128)(2,1)S(1)}, bf16[1,9,2,2,2,128,128]{6,5,4,3,2,1,0:T(8,128)(2,1)S(1)}, u32[]{:S(2)}, u32[]{:S(2)}) collective-permute-start(bf16[1,9,2,2,2,128,128]{6,5,4,3,2,1,0:T(8,128)(2,1)S(1)} %get-tuple-element.19.operator.op_mine), channel_id=1, source_target_pairs={{0,2},{1,3},{2,0},{3,1},{4,6},{5,7},{6,4},{7,5},{8,10},{9,11},{10,... | collective-permute-start | bytes 7077896 | tf_op jit(solution)/shard_map/ppermute | solution.py:380
  3.8 7.5 %collective-permute-start.1 = (bf16[4,16,128]{2,1,0:T(8,128)(2,1)S(1)}, bf16[4,16,128]{2,1,0:T(8,128)(2,1)S(1)}, u32[]{:S(2)}, u32[]{:S(2)}) collective-permute-start(bf16[4,16,128]{2,1,0:T(8,128)(2,1)S(1)} %get-tuple-element.20.refs_0_), channel_id=1, source_target_pairs={{0,1},{1,0},{2,3},{3,2},{4,5},{5,4},{6,7},{7,6},{8,9},{9,8},{10,11... | collective-permute-start | bytes 49160 | tf_op jit(solution)/shard_map/ppermute | solution.py:380
  6.3 4.9 %collective-permute-start.2 = (bf16[4,16,128]{2,1,0:T(8,128)(2,1)S(1)}, bf16[4,16,128]{2,1,0:T(8,128)(2,1)S(1)}, u32[]{:S(2)}, u32[]{:S(2)}) collective-permute-start(bf16[4,16,128]{2,1,0:T(8,128)(2,1)S(1)} %get-tuple-element.20.refs_0_), channel_id=1, source_target_pairs={{0,2},{1,3},{2,0},{3,1},{4,6},{5,7},{6,4},{7,5},{8,10},{9,11},{10,... | collective-permute-start | bytes 49160 | tf_op jit(solution)/shard_map/ppermute | solution.py:380
  6.5 4.8 %collective-permute-start.3 = (bf16[4,16,128]{2,1,0:T(8,128)(2,1)S(1)}, bf16[4,16,128]{2,1,0:T(8,128)(2,1)S(1)}, u32[]{:S(2)}, u32[]{:S(2)}) collective-permute-start(bf16[4,16,128]{2,1,0:T(8,128)(2,1)S(1)} %get-tuple-element.20.refs_0_), channel_id=1, source_target_pairs={{0,3},{1,2},{2,1},{3,0},{4,7},{5,6},{6,5},{7,4},{8,11},{9,10},{10,... | collective-permute-start | bytes 49160 | tf_op jit(solution)/shard_map/ppermute | solution.py:380
  6.5 12.4 %collective-permute-start.4 = (bf16[2,2,2,128,128]{4,3,2,1,0:T(8,128)(2,1)S(1)}, bf16[2,2,2,128,128]{4,3,2,1,0:T(8,128)(2,1)S(1)}, u32[]{:S(2)}, u32[]{:S(2)}) collective-permute-start(bf16[2,2,2,128,128]{4,3,2,1,0:T(8,128)(2,1)S(1)} %get-tuple-element.26), channel_id=1, source_target_pairs={{0,30},{1,31},{2,4},{3,5},{4,2},{5,3},{6,8},{7,9},{8,6},{9,7},{10,... | collective-permute-start | bytes 786440 | tf_op jit(solution)/shard_map/ppermute | solution.py:380
  11.8 7.1 %collective-permute-start.5 = (bf16[2,2,2,2,16,128]{5,4,3,2,1,0:T(8,128)(2,1)S(1)}, bf16[2,2,2,2,16,128]{5,4,3,2,1,0:T(8,128)(2,1)S(1)}, u32[]{:S(2)}, u32[]{:S(2)}) collective-permute-start(bf16[2,2,2,2,16,128]{5,4,3,2,1,0:T(8,128)(2,1)S(1)} %get-tuple-element.28.sent), channel_id=1, source_target_pairs={{0,30},{1,31},{2,4},{3,5},{4,2},{5,3},{6,8},{7,9},{8,6},{9,7},{10,... | collective-permute-start | bytes 196616 | tf_op jit(solution)/shard_map/ppermute | solution.py:380
  15.0 3.9 %collective-permute-start.6 = (bf16[2,2,2,16,128]{4,3,2,1,0:T(8,128)(2,1)S(1)}, bf16[2,2,2,16,128]{4,3,2,1,0:T(8,128)(2,1)S(1)}, u32[]{:S(2)}, u32[]{:S(2)}) collective-permute-start(bf16[2,2,2,16,128]{4,3,2,1,0:T(8,128)(2,1)S(1)} %get-tuple-element.23.other), channel_id=1, source_target_pairs={{0,28},{1,29},{2,6},{3,7},{4,0},{5,1},{6,10},{7,11},{8,4},{9,5},{1... | collective-permute-start | bytes 98312 | tf_op jit(solution)/shard_map/ppermute | solution.py:380
  19.5 1.3 %collective-permute-start.7 = (bf16[2,2,2,16,128]{4,3,2,1,0:T(8,128)(2,1)S(1)}, bf16[2,2,2,16,128]{4,3,2,1,0:T(8,128)(2,1)S(1)}, u32[]{:S(2)}, u32[]{:S(2)}) collective-permute-start(bf16[2,2,2,16,128]{4,3,2,1,0:T(8,128)(2,1)S(1)} %get-tuple-element.31.field_mine.other), channel_id=1, source_target_pairs={{0,2},{1,3},{2,0},{3,1},{4,6},{5,7},{6,4},{7,5},{8,10},{9,11},{10,... | collective-permute-start | bytes 98312 | tf_op jit(solution)/shard_map/ppermute | solution.py:380
  21.1 7.2 %collective-permute-start.8 = (bf16[2,2,2,2,16,128]{5,4,3,2,1,0:T(8,128)(2,1)S(1)}, bf16[2,2,2,2,16,128]{5,4,3,2,1,0:T(8,128)(2,1)S(1)}, u32[]{:S(2)}, u32[]{:S(2)}) collective-permute-start(bf16[2,2,2,2,16,128]{5,4,3,2,1,0:T(8,128)(2,1)S(1)} %get-tuple-element.33.sent), channel_id=1, source_target_pairs={{0,30},{1,31},{2,4},{3,5},{4,2},{5,3},{6,8},{7,9},{8,6},{9,7},{10,... | collective-permute-start | bytes 196616 | tf_op jit(solution)/shard_map/ppermute | solution.py:380
  24.4 3.9 %collective-permute-start.9 = (bf16[2,2,2,16,128]{4,3,2,1,0:T(8,128)(2,1)S(1)}, bf16[2,2,2,16,128]{4,3,2,1,0:T(8,128)(2,1)S(1)}, u32[]{:S(2)}, u32[]{:S(2)}) collective-permute-start(bf16[2,2,2,16,128]{4,3,2,1,0:T(8,128)(2,1)S(1)} %get-tuple-element.31.field_mine.other), channel_id=1, source_target_pairs={{0,28},{1,29},{2,6},{3,7},{4,0},{5,1},{6,10},{7,11},{8,4},{9,5},{1... | collective-permute-start | bytes 98312 | tf_op jit(solution)/shard_map/ppermute | solution.py:380

commit v5 on v4

--- a/solution.py
+++ b/solution.py
@@ -24,17 +24,15 @@
     return y * CZ + z
 
 
-def restrict_kernel(coarse_y, fine_hbm, null_hbm, operator_hbm, out_ref, null_ref, operator, block, fine_ref, loaded):
+def restrict_kernel(coarse_y, fine_hbm, null_hbm, operator_hbm, out_ref, null_ref, operator, fine_ref, loaded):
     aggregates = coarse_y * CZ
     times, _, _, rhs, sites = fine_ref.shape
     vectors = null_ref.shape[3]
-    _, odd = time_sides(True)
     loads = []
     for t in range(times):
         loads.append(pltpu.make_async_copy(fine_hbm.at[t], fine_ref.at[t], loaded.at[2 * t]))
         loads.append(pltpu.make_async_copy(null_hbm.at[t], null_ref.at[t], loaded.at[2 * t + 1]))
-    loads.append(pltpu.make_async_copy(operator_hbm.at[0, odd], block, loaded.at[2 * times]))
-    loads.append(pltpu.make_async_copy(operator_hbm, operator, loaded.at[2 * times + 1]))
+    loads.append(pltpu.make_async_copy(operator_hbm, operator, loaded.at[2 * times]))
     for load in loads:
         load.start()
     ids = aggregate_ids((2 * rhs, sites), coarse_y)
@@ -64,7 +62,6 @@
             real.append(top[:, :vectors] + low[:, vectors:])
             imag.append(low[:, :vectors] - top[:, vectors:])
         out_ref[a] = jnp.concatenate(real + imag, axis=1).astype(out_ref.dtype)
-    loads[-2].wait()
     loads[-1].wait()
 
 
@@ -74,14 +71,13 @@
     return pl.pallas_call(
         functools.partial(restrict_kernel, coarse_y),
         in_specs=[pl.BlockSpec(memory_space=pl.ANY)] * 3,
-        out_specs=[pl.BlockSpec(memory_space=pltpu.VMEM)] * 4,
+        out_specs=[pl.BlockSpec(memory_space=pltpu.VMEM)] * 3,
         out_shape=[
             pltpu.VMEM((coarse_y * CZ, rhs, 4 * null.shape[3]), jnp.bfloat16),
             pltpu.VMEM(null.shape, null.dtype),
             pltpu.VMEM(operator.shape, operator.dtype),
-            pltpu.VMEM(operator.shape[2:], operator.dtype),
         ],
-        scratch_shapes=[pltpu.VMEM(fine.shape, fine.dtype), pltpu.SemaphoreType.DMA((2 * times + 2,))],
+        scratch_shapes=[pltpu.VMEM(fine.shape, fine.dtype), pltpu.SemaphoreType.DMA((2 * times + 1,))],
         compiler_params=pltpu.CompilerParams(vmem_limit_bytes=KERNEL_VMEM),
         name="restrict",
     )(in_hbm(fine), in_hbm(null), in_hbm(operator))
@@ -194,11 +190,26 @@
     return value + RELAX_WEIGHT * (target.astype(jnp.float32) - image)
 
 
+def block_kernel(op_mine, op_pair, block):
+    _, odd = time_sides(True)
+    _, pair_odd = time_sides(False)
+    first = lax.axis_index("zt") < 2
+
+    @pl.when(first)
+    def _():
+        block[...] = op_pair[0, pair_odd]
+
+    @pl.when(jnp.logical_not(first))
+    def _():
+        block[...] = op_mine[0, odd]
+
+
 def gather_kernel(pieces, operator, *refs):
     parts, (rhs_mine, rhs_pair, start_mine, start_pair, message, part_mine) = refs[: 2 * pieces], refs[2 * pieces :]
     extent = operator.shape[2:5]
     position = lax.axis_index("xy")
     even, _ = time_sides(True)
+    parts = parts[::-1]
     for whole, held in ((rhs_mine, parts[:pieces]), (rhs_pair, parts[pieces:])):
         for y in range(extent[0]):
             for z in range(extent[1]):
@@ -388,22 +399,24 @@
     columns = lax.axis_size("xy")
     extent = coarse_operator.shape[2:5]
     bf16, f32 = jnp.bfloat16, jnp.float32
-    own, null_kept, operator, block = restrict(fine_vectors, null_vectors, coarse_operator)
+    own, null_kept, operator = restrict(fine_vectors, null_vectors, coarse_operator)
     full = extent + own.shape[1:]
     if columns == 2:
-        parts = [own, send(own, same, 1), send(own, other), send(own, other, 1)]
+        corner, pair, beside = send(own, other, 1), send(own, other), send(own, same, 1)
+        parts = [own, beside, pair, corner]
     else:
         every = lax.all_gather(own, "xy")
         parts = [every, send(every, other)]
-    back_near = send(block, across)
-    op_pair = send(operator, other)
+    op_pair = send(coarse_operator, other)
+    (block,) = kernel_call(block_kernel, "block", [(operator.shape[2:], bf16)], [], operator, op_pair)
+    back_near = send(block, [across[1], across[0]] + across[2:])
     rhs_mine, rhs_pair, start_mine, start_pair, sent, part_mine = kernel_call(
         functools.partial(gather_kernel, len(parts) // 2),
         "gather",
         [(full, bf16)] * 4 + [((2,) + full, bf16), (full, f32)],
         [],
         operator,
-        *parts,
+        *parts[::-1],
         flops=GATHER_FLOPS,
     )
     near_message, far_field = send(sent, across), send(start_mine, far)

time: 30.5 us -> 30.2 us (level)
  starting transfers between devices: 15.5 us -> 14.6 us
  waiting for transfers between devices: 6.76 us -> 7.48 us
    ppermute x10, starting transfers between devices: 15.5 us -> 14.6 us  [send(): return lax.ppermute(array, ('zt', 'xy'), permutation(target, turn))]
    ppermute x10, waiting for transfers between devices: 6.76 us -> 7.48 us  [send(): return lax.ppermute(array, ('zt', 'xy'), permutation(target, turn))]
    pallas_call x5 -> x6, Pallas kernels: 2.8 us -> 2.81 us  [kernel_call(): pl.pallas_call(kernel, in_specs=[pl.BlockSpec(memory_space=pltpu.VMEM)] *...]
  transfers between devices with their start and end apart: 10 -> 10, of which waited for: 3 -> 4; matrix products, arithmetic and copies ran while one was open for 0% -> 0% of each run, Pallas kernels for 6% -> 15%
where the time goes in v5:
time: 30.2 us; the launch traced here: 30.1 us
  starting transfers between devices  14.6 us (48%)
  waiting for transfers between devices  7.48 us (25%)
  Pallas kernels  7.28 us (24%)
  between operations  0.67 us (2%)
    ppermute x10, starting transfers between devices, send(): return lax.ppermute(array, ('zt', 'xy'), permutation(target, turn))  14.6 us
    ppermute x10, waiting for transfers between devices, send(): return lax.ppermute(array, ('zt', 'xy'), permutation(target, turn))  7.48 us
    pallas_call x6, Pallas kernels, kernel_call(): pl.pallas_call(kernel, in_specs=[pl.BlockSpec(memory_space=pltpu.VMEM)] *...  2.81 us
    pallas_call x1, Pallas kernels, restrict(): pl.pallas_call(functools.partial(restrict_kernel, coarse_y), in_specs=[pl...  2.52 us
    pallas_call x1, Pallas kernels, last(): pl.pallas_call(last_kernel, in_specs=[pl.BlockSpec(memory_space=pltpu.VME...  1.95 us
  transfers between devices with their start and end apart: 10, of which 4 were waited for; matrix products, arithmetic and copies ran while one was open for 0% of the time, Pallas kernels for 15%

profile of v5, /device:TPU:0, one launch (start us, length us, event | category | flops | bytes accessed | tf_op | source)
XLA Modules:
  0.0 30.1 jit_solution(6108604425433598145)
XLA Ops:
  0.6 0.5 %collective-permute-start = (bf16[1,9,2,2,2,128,128]{6,5,4,3,2,1,0:T(8,128)(2,1)}, bf16[1,9,2,2,2,128,128]{6,5,4,3,2,1,0:T(8,128)(2,1)S(1)}, u32[]{:S(2)}, u32[]{:S(2)}) collective-permute-start(bf16[1,9,2,2,2,128,128]{6,5,4,3,2,1,0:T(8,128)(2,1)} %operator_hbm.1), channel_id=1, source_target_pairs={{0,2},{1,3},{2,0},{3,1},{4,6},{5,7},{6,4},{7,5},{8,10},{9,11},{10,... | collective-permute-start | bytes 7077896 | tf_op jit(solution)/shard_map/ppermute | solution.py:391
  1.1 2.5 %restrict.1 = (bf16[4,16,128]{2,1,0:T(8,128)(2,1)S(1)}, bf16[4,2,12,32,256]{4,3,2,1,0:T(8,128)(2,1)S(1)}, bf16[1,9,2,2,2,128,128]{6,5,4,3,2,1,0:T(8,128)(2,1)S(1)}) custom-call(bf16[4,2,12,16,256]{4,3,2,1,0:T(8,128)(2,1)} %fine_hbm.1, bf16[4,2,12,32,256]{4,3,2,1,0:T(8,128)(2,1)} %null_hbm.1, bf16[1,9,2,2,2,128,128]{6,5,4,3,2,1,0:T(8,128)(2,1)} %operator_hbm.1), custom_call_target="tpu_custom_call" | custom-call | tf_op jit(solution)/shard_map/restrict/pallas_call | solution.py:71
  3.7 2.7 %collective-permute-start.1 = (bf16[4,16,128]{2,1,0:T(8,128)(2,1)S(1)}, bf16[4,16,128]{2,1,0:T(8,128)(2,1)S(1)}, u32[]{:S(2)}, u32[]{:S(2)}) collective-permute-start(bf16[4,16,128]{2,1,0:T(8,128)(2,1)S(1)} %get-tuple-element.19.refs_3_), channel_id=1, source_target_pairs={{0,3},{1,2},{2,1},{3,0},{4,7},{5,6},{6,5},{7,4},{8,11},{9,10},{10,... | collective-permute-start | bytes 49160 | tf_op jit(solution)/shard_map/ppermute | solution.py:391
  6.4 0.0 collective-permute-start.2
  6.4 0.5 %collective-permute-start.3 = (bf16[4,16,128]{2,1,0:T(8,128)(2,1)S(1)}, bf16[4,16,128]{2,1,0:T(8,128)(2,1)S(1)}, u32[]{:S(2)}, u32[]{:S(2)}) collective-permute-start(bf16[4,16,128]{2,1,0:T(8,128)(2,1)S(1)} %get-tuple-element.19.refs_3_), channel_id=1, source_target_pairs={{0,1},{1,0},{2,3},{3,2},{4,5},{5,4},{6,7},{7,6},{8,9},{9,8},{10,11... | collective-permute-start | bytes 49160 | tf_op jit(solution)/shard_map/ppermute | solution.py:391
  6.8 0.0 collective-permute-done.op_pair
  6.9 1.6 %collective-permute-start.4 = (bf16[2,2,2,128,128]{4,3,2,1,0:T(8,128)(2,1)S(1)}, bf16[2,2,2,128,128]{4,3,2,1,0:T(8,128)(2,1)S(1)}, u32[]{:S(2)}, u32[]{:S(2)}) collective-permute-start(bf16[2,2,2,128,128]{4,3,2,1,0:T(8,128)(2,1)S(1)} %block.1), channel_id=1, source_target_pairs={{0,4},{1,5},{2,30},{3,31},{4,2},{5,3},{6,8},{7,9},{8,6},{9,7},{10,... | collective-permute-start | bytes 786440 | tf_op jit(solution)/shard_map/ppermute | solution.py:391
  8.5 0.0 collective-permute-done.1.refs_0_
  8.5 0.0 collective-permute-done.2.refs_1_
  8.5 1.7 %collective-permute-done.3.refs_2_ = bf16[4,16,128]{2,1,0:T(8,128)(2,1)S(1)} collective-permute-done((bf16[4,16,128]{2,1,0:T(8,128)(2,1)S(1)}, bf16[4,16,128]{2,1,0:T(8,128)(2,1)S(1)}, u32[]{:S(2)}, u32[]{:S(2)}) %collective-permute-start.3) | collective-permute-done | bytes 16416 | tf_op jit(solution)/shard_map/ppermute | solution.py:391
  10.1 0.5 %gather.1 = (bf16[2,2,2,16,128]{4,3,2,1,0:T(8,128)(2,1)S(1)}, bf16[2,2,2,16,128]{4,3,2,1,0:T(8,128)(2,1)S(1)}, bf16[2,2,2,16,128]{4,3,2,1,0:T(8,128)(2,1)S(1)}, ...) custom-call(bf16[1,9,2,2,2,128,128]{6,5,4,3,2,1,0:T(8,128)(2,1)S(1)}, ...), custom_call_target="tpu_custom_call" | custom-call | flops 10000000000 | tf_op jit(solution)/shard_map/gather/pallas_call | solution.py:368
  10.6 3.5 %collective-permute-start.5 = (bf16[2,2,2,2,16,128]{5,4,3,2,1,0:T(8,128)(2,1)S(1)}, bf16[2,2,2,2,16,128]{5,4,3,2,1,0:T(8,128)(2,1)S(1)}, u32[]{:S(2)}, u32[]{:S(2)}) collective-permute-start(bf16[2,2,2,2,16,128]{5,4,3,2,1,0:T(8,128)(2,1)S(1)} %get-tuple-element.26.sent), channel_id=1, source_target_pairs={{0,30},{1,31},{2,4},{3,5},{4,2},{5,3},{6,8},{7,9},{8,6},{9,7},{10,... | collective-permute-start | bytes 196616 | tf_op jit(solution)/shard_map/ppermute | solution.py:391
  14.1 1.1 %collective-permute-start.6 = (bf16[2,2,2,16,128]{4,3,2,1,0:T(8,128)(2,1)S(1)}, bf16[2,2,2,16,128]{4,3,2,1,0:T(8,128)(2,1)S(1)}, u32[]{:S(2)}, u32[]{:S(2)}) collective-permute-start(bf16[2,2,2,16,128]{4,3,2,1,0:T(8,128)(2,1)S(1)} %get-tuple-element.22.other), channel_id=1, source_target_pairs={{0,28},{1,29},{2,6},{3,7},{4,0},{5,1},{6,10},{7,11},{8,4},{9,5},{1... | collective-permute-start | bytes 98312 | tf_op jit(solution)/shard_map/ppermute | solution.py:391
  15.2 1.0 %pair_one.1 = (f32[2,2,2,16,128]{4,3,2,1,0:T(8,128)S(1)}, bf16[2,2,2,768,128]{4,3,2,1,0:T(8,128)(2,1)S(1)}, bf16[2,2,2,768,128]{4,3,2,1,0:T(8,128)(2,1)S(1)}) custom-call(bf16[1,9,2,2,2,128,128]{6,5,4,3,2,1,0:T(8,128)(2,1)S(1)} %get-tuple-element.18.operator.op_mine, bf16[1,9,2,2,2,128,128]{6,5,4,3,2,1,0:T(8,128)(2,1)S(1)} %collective-permute-done.op_pair, ...), custom_call_target="tpu_custom_call" | custom-call | tf_op jit(solution)/shard_map/pair_one/pallas_call | solution.py:368
  16.3 2.0 %collective-permute-done.6.far = bf16[2,2,2,16,128]{4,3,2,1,0:T(8,128)(2,1)S(1)} collective-permute-done((bf16[2,2,2,16,128]{4,3,2,1,0:T(8,128)(2,1)S(1)}, bf16[2,2,2,16,128]{4,3,2,1,0:T(8,128)(2,1)S(1)}, u32[]{:S(2)}, u32[]{:S(2)}) %collective-permute-start.6) | collective-permute-done | bytes 32800 | tf_op jit(solution)/shard_map/ppermute | solution.py:391
  18.3 0.0 collective-permute-done.5.near
  18.3 0.0 collective-permute-done.4.back_near
  18.3 0.6 %second.1 = (bf16[2,2,2,16,128]{4,3,2,1,0:T(8,128)(2,1)S(1)}, f32[2,2,2,16,128]{4,3,2,1,0:T(8,128)S(1)}) custom-call(bf16[2,2,2,768,128]{4,3,2,1,0:T(8,128)(2,1)S(1)} %get-tuple-element.23.op_mine, bf16[2,2,2,768,128]{4,3,2,1,0:T(8,128)(2,1)S(1)} %get-tuple-element.24.op_pair.packed_pair, bf16[2,2,2,128,128]{4,3,2,1,0:T(8,128)(2,1)S(1)} %collective-permute-done.4.back_near, ...), custom_call_target="tpu_custom_call" | custom-call | tf_op jit(solution)/shard_map/second/pallas_call | solution.py:368
  18.9 0.1 collective-permute-start.7
  18.9 1.2 %collective-permute-done.7.field_pair.here = bf16[2,2,2,16,128]{4,3,2,1,0:T(8,128)(2,1)S(1)} collective-permute-done((bf16[2,2,2,16,128]{4,3,2,1,0:T(8,128)(2,1)S(1)}, bf16[2,2,2,16,128]{4,3,2,1,0:T(8,128)(2,1)S(1)}, u32[]{:S(2)}, u32[]{:S(2)}) %collective-permute-start.7) | collective-permute-done | bytes 32800 | tf_op jit(solution)/shard_map/ppermute | solution.py:391
  20.1 0.3 %third.1 = (bf16[2,2,2,2,16,128]{5,4,3,2,1,0:T(8,128)(2,1)S(1)}, f32[2,2,2,16,128]{4,3,2,1,0:T(8,128)S(1)}) custom-call(bf16[2,2,2,768,128]{4,3,2,1,0:T(8,128)(2,1)S(1)} %get-tuple-element.23.op_mine, bf16[2,2,2,16,128]{4,3,2,1,0:T(8,128)(2,1)S(1)} %get-tuple-element.25.rhs_mine, bf16[2,2,2,16,128]{4,3,2,1,0:T(8,128)(2,1)S(1)} %get-tuple-element.29.field_mine.other, ...), custom_call_target="tpu_custom_call" | custom-call | tf_op jit(solution)/shard_map/third/pallas_call | solution.py:368
  20.5 3.5 %collective-permute-start.8 = (bf16[2,2,2,2,16,128]{5,4,3,2,1,0:T(8,128)(2,1)S(1)}, bf16[2,2,2,2,16,128]{5,4,3,2,1,0:T(8,128)(2,1)S(1)}, u32[]{:S(2)}, u32[]{:S(2)}) collective-permute-start(bf16[2,2,2,2,16,128]{5,4,3,2,1,0:T(8,128)(2,1)S(1)} %get-tuple-element.31.sent), channel_id=1, source_target_pairs={{0,30},{1,31},{2,4},{3,5},{4,2},{5,3},{6,8},{7,9},{8,6},{9,7},{10,... | collective-permute-start | bytes 196616 | tf_op jit(solution)/shard_map/ppermute | solution.py:391
  23.9 1.2 %collective-permute-start.9 = (bf16[2,2,2,16,128]{4,3,2,1,0:T(8,128)(2,1)S(1)}, bf16[2,2,2,16,128]{4,3,2,1,0:T(8,128)(2,1)S(1)}, u32[]{:S(2)}, u32[]{:S(2)}) collective-permute-start(bf16[2,2,2,16,128]{4,3,2,1,0:T(8,128)(2,1)S(1)} %get-tuple-element.29.field_mine.other), channel_id=1, source_target_pairs={{0,28},{1,29},{2,6},{3,7},{4,0},{5,1},{6,10},{7,11},{8,4},{9,5},{1... | collective-permute-start | bytes 98312 | tf_op jit(solution)/shard_map/ppermute | solution.py:391
  25.2 0.3 %pair_two.1.part_pair = f32[2,2,2,16,128]{4,3,2,1,0:T(8,128)S(1)} custom-call(bf16[2,2,2,768,128]{4,3,2,1,0:T(8,128)(2,1)S(1)} %get-tuple-element.24.op_pair.packed_pair, bf16[2,2,2,16,128]{4,3,2,1,0:T(8,128)(2,1)S(1)} %get-tuple-element.20.rhs_pair, bf16[2,2,2,16,128]{4,3,2,1,0:T(8,128)(2,1)S(1)} %collective-permute-done.7.field_pair.here, ...), custom_call_target="tpu_custom_call" | custom-call | tf_op jit(solution)/shard_map/pair_two/pallas_call | solution.py:368
  25.5 2.6 %collective-permute-done.9.far = bf16[2,2,2,16,128]{4,3,2,1,0:T(8,128)(2,1)S(1)} collective-permute-done((bf16[2,2,2,16,128]{4,3,2,1,0:T(8,128)(2,1)S(1)}, bf16[2,2,2,16,128]{4,3,2,1,0:T(8,128)(2,1)S(1)}, u32[]{:S(2)}, u32[]{:S(2)}) %collective-permute-start.9) | collective-permute-done | bytes 32800 | tf_op jit(solution)/shard_map/ppermute | solution.py:391
  28.1 0.0 collective-permute-done.8.near
  28.1 2.0 %last.1 = (bf16[4,2,12,16,256]{4,3,2,1,0:T(8,128)(2,1)}, bf16[1,2,2,2,16,128]{5,4,3,2,1,0:T(8,128)(2,1)}) custom-call(bf16[2,2,2,768,128]{4,3,2,1,0:T(8,128)(2,1)S(1)} %get-tuple-element.23.op_mine, bf16[2,2,2,768,128]{4,3,2,1,0:T(8,128)(2,1)S(1)} %get-tuple-element.24.op_pair.packed_pair, bf16[2,2,2,128,128]{4,3,2,1,0:T(8,128)(2,1)S(1)} %collective-permute-done.4.back_near, ...), custom_call_target="tpu_custom_call" | custom-call | tf_op jit(solution)/shard_map/last/pallas_call | solution.py:334
  (1 shorter events, 0.0 us)
Async XLA Ops:
  0.6 6.2 %collective-permute-start = (bf16[1,9,2,2,2,128,128]{6,5,4,3,2,1,0:T(8,128)(2,1)}, bf16[1,9,2,2,2,128,128]{6,5,4,3,2,1,0:T(8,128)(2,1)S(1)}, u32[]{:S(2)}, u32[]{:S(2)}) collective-permute-start(bf16[1,9,2,2,2,128,128]{6,5,4,3,2,1,0:T(8,128)(2,1)} %operator_hbm.1), channel_id=1, source_target_pairs={{0,2},{1,3},{2,0},{3,1},{4,6},{5,7},{6,4},{7,5},{8,10},{9,11},{10,... | collective-permute-start | bytes 7077896 | tf_op jit(solution)/shard_map/ppermute | solution.py:391
  3.7 4.8 %collective-permute-start.1 = (bf16[4,16,128]{2,1,0:T(8,128)(2,1)S(1)}, bf16[4,16,128]{2,1,0:T(8,128)(2,1)S(1)}, u32[]{:S(2)}, u32[]{:S(2)}) collective-permute-start(bf16[4,16,128]{2,1,0:T(8,128)(2,1)S(1)} %get-tuple-element.19.refs_3_), channel_id=1, source_target_pairs={{0,3},{1,2},{2,1},{3,0},{4,7},{5,6},{6,5},{7,4},{8,11},{9,10},{10,... | collective-permute-start | bytes 49160 | tf_op jit(solution)/shard_map/ppermute | solution.py:391
  6.4 2.1 %collective-permute-start.2 = (bf16[4,16,128]{2,1,0:T(8,128)(2,1)S(1)}, bf16[4,16,128]{2,1,0:T(8,128)(2,1)S(1)}, u32[]{:S(2)}, u32[]{:S(2)}) collective-permute-start(bf16[4,16,128]{2,1,0:T(8,128)(2,1)S(1)} %get-tuple-element.19.refs_3_), channel_id=1, source_target_pairs={{0,2},{1,3},{2,0},{3,1},{4,6},{5,7},{6,4},{7,5},{8,10},{9,11},{10,... | collective-permute-start | bytes 49160 | tf_op jit(solution)/shard_map/ppermute | solution.py:391
  6.4 3.7 %collective-permute-start.3 = (bf16[4,16,128]{2,1,0:T(8,128)(2,1)S(1)}, bf16[4,16,128]{2,1,0:T(8,128)(2,1)S(1)}, u32[]{:S(2)}, u32[]{:S(2)}) collective-permute-start(bf16[4,16,128]{2,1,0:T(8,128)(2,1)S(1)} %get-tuple-element.19.refs_3_), channel_id=1, source_target_pairs={{0,1},{1,0},{2,3},{3,2},{4,5},{5,4},{6,7},{7,6},{8,9},{9,8},{10,11... | collective-permute-start | bytes 49160 | tf_op jit(solution)/shard_map/ppermute | solution.py:391
  6.9 11.4 %collective-permute-start.4 = (bf16[2,2,2,128,128]{4,3,2,1,0:T(8,128)(2,1)S(1)}, bf16[2,2,2,128,128]{4,3,2,1,0:T(8,128)(2,1)S(1)}, u32[]{:S(2)}, u32[]{:S(2)}) collective-permute-start(bf16[2,2,2,128,128]{4,3,2,1,0:T(8,128)(2,1)S(1)} %block.1), channel_id=1, source_target_pairs={{0,4},{1,5},{2,30},{3,31},{4,2},{5,3},{6,8},{7,9},{8,6},{9,7},{10,... | collective-permute-start | bytes 786440 | tf_op jit(solution)/shard_map/ppermute | solution.py:391
  10.6 7.6 %collective-permute-start.5 = (bf16[2,2,2,2,16,128]{5,4,3,2,1,0:T(8,128)(2,1)S(1)}, bf16[2,2,2,2,16,128]{5,4,3,2,1,0:T(8,128)(2,1)S(1)}, u32[]{:S(2)}, u32[]{:S(2)}) collective-permute-start(bf16[2,2,2,2,16,128]{5,4,3,2,1,0:T(8,128)(2,1)S(1)} %get-tuple-element.26.sent), channel_id=1, source_target_pairs={{0,30},{1,31},{2,4},{3,5},{4,2},{5,3},{6,8},{7,9},{8,6},{9,7},{10,... | collective-permute-start | bytes 196616 | tf_op jit(solution)/shard_map/ppermute | solution.py:391
  14.1 4.1 %collective-permute-start.6 = (bf16[2,2,2,16,128]{4,3,2,1,0:T(8,128)(2,1)S(1)}, bf16[2,2,2,16,128]{4,3,2,1,0:T(8,128)(2,1)S(1)}, u32[]{:S(2)}, u32[]{:S(2)}) collective-permute-start(bf16[2,2,2,16,128]{4,3,2,1,0:T(8,128)(2,1)S(1)} %get-tuple-element.22.other), channel_id=1, source_target_pairs={{0,28},{1,29},{2,6},{3,7},{4,0},{5,1},{6,10},{7,11},{8,4},{9,5},{1... | collective-permute-start | bytes 98312 | tf_op jit(solution)/shard_map/ppermute | solution.py:391
  18.9 1.3 %collective-permute-start.7 = (bf16[2,2,2,16,128]{4,3,2,1,0:T(8,128)(2,1)S(1)}, bf16[2,2,2,16,128]{4,3,2,1,0:T(8,128)(2,1)S(1)}, u32[]{:S(2)}, u32[]{:S(2)}) collective-permute-start(bf16[2,2,2,16,128]{4,3,2,1,0:T(8,128)(2,1)S(1)} %get-tuple-element.29.field_mine.other), channel_id=1, source_target_pairs={{0,2},{1,3},{2,0},{3,1},{4,6},{5,7},{6,4},{7,5},{8,10},{9,11},{10,... | collective-permute-start | bytes 98312 | tf_op jit(solution)/shard_map/ppermute | solution.py:391
  20.5 7.7 %collective-permute-start.8 = (bf16[2,2,2,2,16,128]{5,4,3,2,1,0:T(8,128)(2,1)S(1)}, bf16[2,2,2,2,16,128]{5,4,3,2,1,0:T(8,128)(2,1)S(1)}, u32[]{:S(2)}, u32[]{:S(2)}) collective-permute-start(bf16[2,2,2,2,16,128]{5,4,3,2,1,0:T(8,128)(2,1)S(1)} %get-tuple-element.31.sent), channel_id=1, source_target_pairs={{0,30},{1,31},{2,4},{3,5},{4,2},{5,3},{6,8},{7,9},{8,6},{9,7},{10,... | collective-permute-start | bytes 196616 | tf_op jit(solution)/shard_map/ppermute | solution.py:391
  23.9 4.2 %collective-permute-start.9 = (bf16[2,2,2,16,128]{4,3,2,1,0:T(8,128)(2,1)S(1)}, bf16[2,2,2,16,128]{4,3,2,1,0:T(8,128)(2,1)S(1)}, u32[]{:S(2)}, u32[]{:S(2)}) collective-permute-start(bf16[2,2,2,16,128]{4,3,2,1,0:T(8,128)(2,1)S(1)} %get-tuple-element.29.field_mine.other), channel_id=1, source_target_pairs={{0,28},{1,29},{2,6},{3,7},{4,0},{5,1},{6,10},{7,11},{8,4},{9,5},{1... | collective-permute-start | bytes 98312 | tf_op jit(solution)/shard_map/ppermute | solution.py:391

commit v6 on v5

--- a/solution.py
+++ b/solution.py
@@ -258,54 +258,67 @@
     for_sites(packed_pair.shape[:3], step)
 
 
-def second_kernel(
-    op_mine, op_pair, back_near, rhs_mine, sent, part_mine, part_pair, near, far,
-    field_mine, value_mine, one_mine, one_pair, one_near, x_mine,
-):
-    halfway(op_mine, op_pair, back_near, sent, part_mine, part_pair, near, far, one_mine, one_pair, one_near, x_mine)
+def second_near_kernel(op_mine, back_near, rhs_mine, sent, part_mine, near, rest, one_mine, one_near):
+    def first(site):
+        value = near_step(op_mine, part_mine, near.at[0], site)
+        rest[site] = value
+        one_mine[site] = value.astype(jnp.bfloat16)
+        one_near[site] = return_step(back_near, sent, near, site)
+
+    for_sites(op_mine.shape[:3], first)
 
     def second(site):
-        value = second_step(op_mine, rhs_mine, one_mine, one_pair, one_near, x_mine, site)
+        sums = packed_stencil(op_mine, site, one_mine, []) + side_product(one_near, op_mine, site, 1)
+        rest[site] = relaxed(rest[site], one_mine[site], rhs_mine[site], sums)
+
+    for_sites(op_mine.shape[:3], second)
+
+
+def second_far_kernel(op_mine, op_pair, part_pair, far, rest, field_mine, value_mine):
+    def step(site):
+        one_pair = near_step(op_pair, part_pair, far, site).astype(jnp.bfloat16)
+        sums = jnp.dot(one_pair, op_mine[site][side_rows(op_mine, 2)], preferred_element_type=jnp.float32)
+        value = rest[site] - RELAX_WEIGHT * sums
         value_mine[site] = value
         field_mine[site] = value.astype(jnp.bfloat16)
 
-    for_sites(op_mine.shape[:3], second)
-
-
-def halfway(op_mine, op_pair, back_near, sent, part_mine, part_pair, near, far, one_mine, one_pair, one_near, x_mine):
-    depth, columns = op_mine.shape[3:]
-    side = slice(depth - columns, depth)
-
-    def first(site):
-        value = part_mine[site] - RELAX_WEIGHT * product(near[(0,) + site], op_mine[site][side])
-        x_mine[site] = value
-        one_mine[site] = value.astype(jnp.bfloat16)
-        value = part_pair[site] - RELAX_WEIGHT * product(far[site], op_pair[site][side])
-        one_pair[site] = value.astype(jnp.bfloat16)
-        value = near[(1,) + site].astype(jnp.float32) - RELAX_WEIGHT * products([(back_near[site], sent[(0,) + site])])
-        one_near[site] = value.astype(jnp.bfloat16)
-
-    for_sites(op_mine.shape[:3], first)
-
-
-def product(field, weights):
-    return jnp.dot(field, weights, preferred_element_type=jnp.float32)
-
-
-def second_step(op_mine, rhs_mine, one_mine, one_pair, one_near, x_mine, site):
-    sums = packed_stencil(op_mine, site, one_mine, [one_pair, one_near])
-    return relaxed(x_mine[site], one_mine[site], rhs_mine[site], sums)
-
-
-def third_kernel(op_mine, rhs_mine, field_mine, value_mine, field_pair, message, part_next):
-    def third(site):
-        sums = packed_stencil(op_mine, site, field_mine, [field_pair])
-        part = relaxed(value_mine[site], field_mine[site], rhs_mine[site], sums)
+    for_sites(op_mine.shape[:3], step)
+
+
+def side_rows(weights, last):
+    depth, columns = weights.shape[3:]
+    return slice(depth - last * columns, depth - (last - 1) * columns)
+
+
+def side_product(field, weights, site, last):
+    return jnp.dot(field[site], weights[site][side_rows(weights, last)], preferred_element_type=jnp.float32)
+
+
+def near_step(weights, part, received, site):
+    return part[site] - RELAX_WEIGHT * side_product(received, weights, site, 1)
+
+
+def return_step(back_near, sent, near, site):
+    value = near[(1,) + site].astype(jnp.float32) - RELAX_WEIGHT * products([(back_near[site], sent[(0,) + site])])
+    return value.astype(jnp.bfloat16)
+
+
+def third_own_kernel(op_mine, rhs_mine, field_mine, value_mine, rest):
+    def step(site):
+        sums = packed_stencil(op_mine, site, field_mine, [])
+        rest[site] = relaxed(value_mine[site], field_mine[site], rhs_mine[site], sums)
+
+    for_sites(op_mine.shape[:3], step)
+
+
+def third_kernel(op_mine, rest, field_mine, field_pair, message, part_next):
+    def step(site):
+        part = rest[site] - RELAX_WEIGHT * side_product(field_pair, op_mine, site, 2)
         part_next[site] = part
         message[(0,) + site] = field_mine[site]
         message[(1,) + site] = part.astype(jnp.bfloat16)
 
-    for_sites(op_mine.shape[:3], third)
+    for_sites(op_mine.shape[:3], step)
 
 
 def last_kernel(
@@ -313,10 +326,19 @@
     fine_out, coarse_out, one_mine, one_pair, one_near, x_mine, result, held, done,
 ):
     extent = op_mine.shape[:3]
-    halfway(op_mine, op_pair, back_near, sent, part_mine, part_pair, near, far, one_mine, one_pair, one_near, x_mine)
+
+    def first(site):
+        value = near_step(op_mine, part_mine, near.at[0], site)
+        x_mine[site] = value
+        one_mine[site] = value.astype(jnp.bfloat16)
+        one_pair[site] = near_step(op_pair, part_pair, far, site).astype(jnp.bfloat16)
+        one_near[site] = return_step(back_near, sent, near, site)
+
+    for_sites(extent, first)
 
     def second(site):
-        value = second_step(op_mine, rhs_mine, one_mine, one_pair, one_near, x_mine, site)
+        sums = packed_stencil(op_mine, site, one_mine, [one_pair, one_near])
+        value = relaxed(x_mine[site], one_mine[site], rhs_mine[site], sums)
         result[(0,) + site] = value.astype(jnp.bfloat16)
 
     for_sites(extent, second)
@@ -427,17 +449,20 @@
         [],
         operator, op_pair, rhs_pair, start_pair, start_mine,
     )
+    (rest,) = kernel_call(
+        second_near_kernel, "second_near", [(full, f32)], [(full, bf16)] * 2,
+        packed_mine, back_near, rhs_mine, sent, part_mine, near_message,
+    )
     field_mine, value_mine = kernel_call(
-        second_kernel,
-        "second",
-        [(full, bf16), (full, f32)],
-        [(full, bf16)] * 3 + [(full, f32)],
-        packed_mine, packed_pair, back_near, rhs_mine, sent, part_mine, part_pair, near_message, far_field,
+        second_far_kernel, "second_far", [(full, bf16), (full, f32)], [],
+        packed_mine, packed_pair, part_pair, far_field, rest,
     )
     field_pair = send(field_mine, other)
+    (rest,) = kernel_call(
+        third_own_kernel, "third_own", [(full, f32)], [], packed_mine, rhs_mine, field_mine, value_mine,
+    )
     sent, part_mine = kernel_call(
-        third_kernel, "third", [((2,) + full, bf16), (full, f32)], [],
-        packed_mine, rhs_mine, field_mine, value_mine, field_pair,
+        third_kernel, "third", [((2,) + full, bf16), (full, f32)], [], packed_mine, rest, field_mine, field_pair,
     )
     near_message, far_field = send(sent, across), send(field_mine, far)
     (part_pair,) = kernel_call(

time: 30.2 us -> 29.7 us (0.983)
  waiting for transfers between devices: 7.48 us -> 6.58 us
  Pallas kernels: 7.28 us -> 7.69 us
    ppermute x10, waiting for transfers between devices: 7.48 us -> 6.58 us  [send(): return lax.ppermute(array, ('zt', 'xy'), permutation(target, turn))]
    pallas_call x6 -> x8, Pallas kernels: 2.81 us -> 3.22 us  [kernel_call(): pl.pallas_call(kernel, in_specs=[pl.BlockSpec(memory_space=pltpu.VMEM)] *...]
  transfers between devices with their start and end apart: 10 -> 10, of which waited for: 4 -> 6; matrix products, arithmetic and copies ran while one was open for 0% -> 0% of each run, Pallas kernels for 15% -> 18%
where the time goes in v6:
time: 29.7 us; the launch traced here: 29.6 us
  starting transfers between devices  14.6 us (49%)
  Pallas kernels  7.69 us (26%)
  waiting for transfers between devices  6.58 us (22%)
  between operations  0.68 us (2%)
    ppermute x10, starting transfers between devices, send(): return lax.ppermute(array, ('zt', 'xy'), permutation(target, turn))  14.6 us
    ppermute x10, waiting for transfers between devices, send(): return lax.ppermute(array, ('zt', 'xy'), permutation(target, turn))  6.58 us
    pallas_call x8, Pallas kernels, kernel_call(): pl.pallas_call(kernel, in_specs=[pl.BlockSpec(memory_space=pltpu.VMEM)] *...  3.22 us
    pallas_call x1, Pallas kernels, restrict(): pl.pallas_call(functools.partial(restrict_kernel, coarse_y), in_specs=[pl...  2.52 us
    pallas_call x1, Pallas kernels, last(): pl.pallas_call(last_kernel, in_specs=[pl.BlockSpec(memory_space=pltpu.VME...  1.95 us
  transfers between devices with their start and end apart: 10, of which 6 were waited for; matrix products, arithmetic and copies ran while one was open for 0% of the time, Pallas kernels for 18%

profile of v6, /device:TPU:0, one launch (start us, length us, event | category | flops | bytes accessed | tf_op | source)
XLA Modules:
  0.0 29.6 jit_solution(13349067254936239524)
XLA Ops:
  0.6 0.5 %collective-permute-start = (bf16[1,9,2,2,2,128,128]{6,5,4,3,2,1,0:T(8,128)(2,1)}, bf16[1,9,2,2,2,128,128]{6,5,4,3,2,1,0:T(8,128)(2,1)S(1)}, u32[]{:S(2)}, u32[]{:S(2)}) collective-permute-start(bf16[1,9,2,2,2,128,128]{6,5,4,3,2,1,0:T(8,128)(2,1)} %operator_hbm.1), channel_id=1, source_target_pairs={{0,2},{1,3},{2,0},{3,1},{4,6},{5,7},{6,4},{7,5},{8,10},{9,11},{10,... | collective-permute-start | bytes 7077896 | tf_op jit(solution)/shard_map/ppermute | solution.py:413
  1.1 2.5 %restrict.1 = (bf16[4,16,128]{2,1,0:T(8,128)(2,1)S(1)}, bf16[4,2,12,32,256]{4,3,2,1,0:T(8,128)(2,1)S(1)}, bf16[1,9,2,2,2,128,128]{6,5,4,3,2,1,0:T(8,128)(2,1)S(1)}) custom-call(bf16[4,2,12,16,256]{4,3,2,1,0:T(8,128)(2,1)} %fine_hbm.1, bf16[4,2,12,32,256]{4,3,2,1,0:T(8,128)(2,1)} %null_hbm.1, bf16[1,9,2,2,2,128,128]{6,5,4,3,2,1,0:T(8,128)(2,1)} %operator_hbm.1), custom_call_target="tpu_custom_call" | custom-call | tf_op jit(solution)/shard_map/restrict/pallas_call | solution.py:71
  3.7 2.7 %collective-permute-start.1 = (bf16[4,16,128]{2,1,0:T(8,128)(2,1)S(1)}, bf16[4,16,128]{2,1,0:T(8,128)(2,1)S(1)}, u32[]{:S(2)}, u32[]{:S(2)}) collective-permute-start(bf16[4,16,128]{2,1,0:T(8,128)(2,1)S(1)} %get-tuple-element.19.refs_3_), channel_id=1, source_target_pairs={{0,3},{1,2},{2,1},{3,0},{4,7},{5,6},{6,5},{7,4},{8,11},{9,10},{10,... | collective-permute-start | bytes 49160 | tf_op jit(solution)/shard_map/ppermute | solution.py:413
  6.4 0.0 collective-permute-start.2
  6.4 0.5 %collective-permute-start.3 = (bf16[4,16,128]{2,1,0:T(8,128)(2,1)S(1)}, bf16[4,16,128]{2,1,0:T(8,128)(2,1)S(1)}, u32[]{:S(2)}, u32[]{:S(2)}) collective-permute-start(bf16[4,16,128]{2,1,0:T(8,128)(2,1)S(1)} %get-tuple-element.19.refs_3_), channel_id=1, source_target_pairs={{0,1},{1,0},{2,3},{3,2},{4,5},{5,4},{6,7},{7,6},{8,9},{9,8},{10,11... | collective-permute-start | bytes 49160 | tf_op jit(solution)/shard_map/ppermute | solution.py:413
  6.8 0.0 collective-permute-done.op_pair
  6.9 1.6 %collective-permute-start.4 = (bf16[2,2,2,128,128]{4,3,2,1,0:T(8,128)(2,1)S(1)}, bf16[2,2,2,128,128]{4,3,2,1,0:T(8,128)(2,1)S(1)}, u32[]{:S(2)}, u32[]{:S(2)}) collective-permute-start(bf16[2,2,2,128,128]{4,3,2,1,0:T(8,128)(2,1)S(1)} %block.1), channel_id=1, source_target_pairs={{0,4},{1,5},{2,30},{3,31},{4,2},{5,3},{6,8},{7,9},{8,6},{9,7},{10,... | collective-permute-start | bytes 786440 | tf_op jit(solution)/shard_map/ppermute | solution.py:413
  8.5 0.0 collective-permute-done.1.refs_0_
  8.5 0.0 collective-permute-done.2.refs_1_
  8.5 1.7 %collective-permute-done.3.refs_2_ = bf16[4,16,128]{2,1,0:T(8,128)(2,1)S(1)} collective-permute-done((bf16[4,16,128]{2,1,0:T(8,128)(2,1)S(1)}, bf16[4,16,128]{2,1,0:T(8,128)(2,1)S(1)}, u32[]{:S(2)}, u32[]{:S(2)}) %collective-permute-start.3) | collective-permute-done | bytes 16416 | tf_op jit(solution)/shard_map/ppermute | solution.py:413
  10.1 0.5 %gather.1 = (bf16[2,2,2,16,128]{4,3,2,1,0:T(8,128)(2,1)S(1)}, bf16[2,2,2,16,128]{4,3,2,1,0:T(8,128)(2,1)S(1)}, bf16[2,2,2,16,128]{4,3,2,1,0:T(8,128)(2,1)S(1)}, ...) custom-call(bf16[1,9,2,2,2,128,128]{6,5,4,3,2,1,0:T(8,128)(2,1)S(1)}, ...), custom_call_target="tpu_custom_call" | custom-call | flops 10000000000 | tf_op jit(solution)/shard_map/gather/pallas_call | solution.py:390
  10.6 3.5 %collective-permute-start.6 = (bf16[2,2,2,2,16,128]{5,4,3,2,1,0:T(8,128)(2,1)S(1)}, bf16[2,2,2,2,16,128]{5,4,3,2,1,0:T(8,128)(2,1)S(1)}, u32[]{:S(2)}, u32[]{:S(2)}) collective-permute-start(bf16[2,2,2,2,16,128]{5,4,3,2,1,0:T(8,128)(2,1)S(1)} %get-tuple-element.27.sent), channel_id=1, source_target_pairs={{0,30},{1,31},{2,4},{3,5},{4,2},{5,3},{6,8},{7,9},{8,6},{9,7},{10,... | collective-permute-start | bytes 196616 | tf_op jit(solution)/shard_map/ppermute | solution.py:413
  14.1 1.1 %collective-permute-start.5 = (bf16[2,2,2,16,128]{4,3,2,1,0:T(8,128)(2,1)S(1)}, bf16[2,2,2,16,128]{4,3,2,1,0:T(8,128)(2,1)S(1)}, u32[]{:S(2)}, u32[]{:S(2)}) collective-permute-start(bf16[2,2,2,16,128]{4,3,2,1,0:T(8,128)(2,1)S(1)} %get-tuple-element.22.other), channel_id=1, source_target_pairs={{0,28},{1,29},{2,6},{3,7},{4,0},{5,1},{6,10},{7,11},{8,4},{9,5},{1... | collective-permute-start | bytes 98312 | tf_op jit(solution)/shard_map/ppermute | solution.py:413
  15.2 1.0 %pair_one.1 = (f32[2,2,2,16,128]{4,3,2,1,0:T(8,128)S(1)}, bf16[2,2,2,768,128]{4,3,2,1,0:T(8,128)(2,1)S(1)}, bf16[2,2,2,768,128]{4,3,2,1,0:T(8,128)(2,1)S(1)}) custom-call(bf16[1,9,2,2,2,128,128]{6,5,4,3,2,1,0:T(8,128)(2,1)S(1)} %get-tuple-element.18.operator.op_mine, bf16[1,9,2,2,2,128,128]{6,5,4,3,2,1,0:T(8,128)(2,1)S(1)} %collective-permute-done.op_pair, ...), custom_call_target="tpu_custom_call" | custom-call | tf_op jit(solution)/shard_map/pair_one/pallas_call | solution.py:390
  16.3 0.9 %collective-permute-done.6.near = bf16[2,2,2,2,16,128]{5,4,3,2,1,0:T(8,128)(2,1)S(1)} collective-permute-done((bf16[2,2,2,2,16,128]{5,4,3,2,1,0:T(8,128)(2,1)S(1)}, bf16[2,2,2,2,16,128]{5,4,3,2,1,0:T(8,128)(2,1)S(1)}, u32[]{:S(2)}, u32[]{:S(2)}) %collective-permute-start.6) | collective-permute-done | bytes 65568 | tf_op jit(solution)/shard_map/ppermute | solution.py:413
  17.2 0.1 collective-permute-done.4.back_near
  17.3 0.5 %second_near.1.rest = f32[2,2,2,16,128]{4,3,2,1,0:T(8,128)S(1)} custom-call(bf16[2,2,2,768,128]{4,3,2,1,0:T(8,128)(2,1)S(1)} %get-tuple-element.23.op_mine, bf16[2,2,2,128,128]{4,3,2,1,0:T(8,128)(2,1)S(1)} %collective-permute-done.4.back_near, bf16[2,2,2,16,128]{4,3,2,1,0:T(8,128)(2,1)S(1)} %get-tuple-element.25.rhs_mine, ...), custom_call_target="tpu_custom_call" | custom-call | tf_op jit(solution)/shard_map/second_near/pallas_call | solution.py:390
  17.8 0.5 %collective-permute-done.5.far = bf16[2,2,2,16,128]{4,3,2,1,0:T(8,128)(2,1)S(1)} collective-permute-done((bf16[2,2,2,16,128]{4,3,2,1,0:T(8,128)(2,1)S(1)}, bf16[2,2,2,16,128]{4,3,2,1,0:T(8,128)(2,1)S(1)}, u32[]{:S(2)}, u32[]{:S(2)}) %collective-permute-start.5) | collective-permute-done | bytes 32800 | tf_op jit(solution)/shard_map/ppermute | solution.py:413
  18.3 0.4 %second_far.1 = (bf16[2,2,2,16,128]{4,3,2,1,0:T(8,128)(2,1)S(1)}, f32[2,2,2,16,128]{4,3,2,1,0:T(8,128)S(1)}) custom-call(bf16[2,2,2,768,128]{4,3,2,1,0:T(8,128)(2,1)S(1)} %get-tuple-element.23.op_mine, bf16[2,2,2,768,128]{4,3,2,1,0:T(8,128)(2,1)S(1)} %get-tuple-element.24.op_pair.packed_pair, f32[2,2,2,16,128]{4,3,2,1,0:T(8,128)S(1)} %get-tuple-element.26.part_pair, ...), custom_call_target="tpu_custom_call" | custom-call | tf_op jit(solution)/shard_map/second_far/pallas_call | solution.py:390
  18.6 0.1 collective-permute-start.7
  18.7 0.2 third_own.1.rest
  18.9 0.9 %collective-permute-done.7.field_pair.here = bf16[2,2,2,16,128]{4,3,2,1,0:T(8,128)(2,1)S(1)} collective-permute-done((bf16[2,2,2,16,128]{4,3,2,1,0:T(8,128)(2,1)S(1)}, bf16[2,2,2,16,128]{4,3,2,1,0:T(8,128)(2,1)S(1)}, u32[]{:S(2)}, u32[]{:S(2)}) %collective-permute-start.7) | collective-permute-done | bytes 32800 | tf_op jit(solution)/shard_map/ppermute | solution.py:413
  19.9 0.2 third.1
  20.1 3.6 %collective-permute-start.8 = (bf16[2,2,2,2,16,128]{5,4,3,2,1,0:T(8,128)(2,1)S(1)}, bf16[2,2,2,2,16,128]{5,4,3,2,1,0:T(8,128)(2,1)S(1)}, u32[]{:S(2)}, u32[]{:S(2)}) collective-permute-start(bf16[2,2,2,2,16,128]{5,4,3,2,1,0:T(8,128)(2,1)S(1)} %get-tuple-element.31.sent), channel_id=1, source_target_pairs={{0,30},{1,31},{2,4},{3,5},{4,2},{5,3},{6,8},{7,9},{8,6},{9,7},{10,... | collective-permute-start | bytes 196616 | tf_op jit(solution)/shard_map/ppermute | solution.py:413
  23.7 1.1 %collective-permute-start.9 = (bf16[2,2,2,16,128]{4,3,2,1,0:T(8,128)(2,1)S(1)}, bf16[2,2,2,16,128]{4,3,2,1,0:T(8,128)(2,1)S(1)}, u32[]{:S(2)}, u32[]{:S(2)}) collective-permute-start(bf16[2,2,2,16,128]{4,3,2,1,0:T(8,128)(2,1)S(1)} %get-tuple-element.29.field_mine.other), channel_id=1, source_target_pairs={{0,28},{1,29},{2,6},{3,7},{4,0},{5,1},{6,10},{7,11},{8,4},{9,5},{1... | collective-permute-start | bytes 98312 | tf_op jit(solution)/shard_map/ppermute | solution.py:413
  24.8 0.3 %pair_two.1.part_pair = f32[2,2,2,16,128]{4,3,2,1,0:T(8,128)S(1)} custom-call(bf16[2,2,2,768,128]{4,3,2,1,0:T(8,128)(2,1)S(1)} %get-tuple-element.24.op_pair.packed_pair, bf16[2,2,2,16,128]{4,3,2,1,0:T(8,128)(2,1)S(1)} %get-tuple-element.20.rhs_pair, bf16[2,2,2,16,128]{4,3,2,1,0:T(8,128)(2,1)S(1)} %collective-permute-done.7.field_pair.here, ...), custom_call_target="tpu_custom_call" | custom-call | tf_op jit(solution)/shard_map/pair_two/pallas_call | solution.py:390
  25.1 2.5 %collective-permute-done.9.far = bf16[2,2,2,16,128]{4,3,2,1,0:T(8,128)(2,1)S(1)} collective-permute-done((bf16[2,2,2,16,128]{4,3,2,1,0:T(8,128)(2,1)S(1)}, bf16[2,2,2,16,128]{4,3,2,1,0:T(8,128)(2,1)S(1)}, u32[]{:S(2)}, u32[]{:S(2)}) %collective-permute-start.9) | collective-permute-done | bytes 32800 | tf_op jit(solution)/shard_map/ppermute | solution.py:413
  27.6 0.0 collective-permute-done.8.near
  27.6 2.0 %last.1 = (bf16[4,2,12,16,256]{4,3,2,1,0:T(8,128)(2,1)}, bf16[1,2,2,2,16,128]{5,4,3,2,1,0:T(8,128)(2,1)}) custom-call(bf16[2,2,2,768,128]{4,3,2,1,0:T(8,128)(2,1)S(1)} %get-tuple-element.23.op_mine, bf16[2,2,2,768,128]{4,3,2,1,0:T(8,128)(2,1)S(1)} %get-tuple-element.24.op_pair.packed_pair, bf16[2,2,2,128,128]{4,3,2,1,0:T(8,128)(2,1)S(1)} %collective-permute-done.4.back_near, ...), custom_call_target="tpu_custom_call" | custom-call | tf_op jit(solution)/shard_map/last/pallas_call | solution.py:356
  (1 shorter events, 0.0 us)
Async XLA Ops:
  0.6 6.2 %collective-permute-start = (bf16[1,9,2,2,2,128,128]{6,5,4,3,2,1,0:T(8,128)(2,1)}, bf16[1,9,2,2,2,128,128]{6,5,4,3,2,1,0:T(8,128)(2,1)S(1)}, u32[]{:S(2)}, u32[]{:S(2)}) collective-permute-start(bf16[1,9,2,2,2,128,128]{6,5,4,3,2,1,0:T(8,128)(2,1)} %operator_hbm.1), channel_id=1, source_target_pairs={{0,2},{1,3},{2,0},{3,1},{4,6},{5,7},{6,4},{7,5},{8,10},{9,11},{10,... | collective-permute-start | bytes 7077896 | tf_op jit(solution)/shard_map/ppermute | solution.py:413
  3.7 4.8 %collective-permute-start.1 = (bf16[4,16,128]{2,1,0:T(8,128)(2,1)S(1)}, bf16[4,16,128]{2,1,0:T(8,128)(2,1)S(1)}, u32[]{:S(2)}, u32[]{:S(2)}) collective-permute-start(bf16[4,16,128]{2,1,0:T(8,128)(2,1)S(1)} %get-tuple-element.19.refs_3_), channel_id=1, source_target_pairs={{0,3},{1,2},{2,1},{3,0},{4,7},{5,6},{6,5},{7,4},{8,11},{9,10},{10,... | collective-permute-start | bytes 49160 | tf_op jit(solution)/shard_map/ppermute | solution.py:413
  6.4 2.1 %collective-permute-start.2 = (bf16[4,16,128]{2,1,0:T(8,128)(2,1)S(1)}, bf16[4,16,128]{2,1,0:T(8,128)(2,1)S(1)}, u32[]{:S(2)}, u32[]{:S(2)}) collective-permute-start(bf16[4,16,128]{2,1,0:T(8,128)(2,1)S(1)} %get-tuple-element.19.refs_3_), channel_id=1, source_target_pairs={{0,2},{1,3},{2,0},{3,1},{4,6},{5,7},{6,4},{7,5},{8,10},{9,11},{10,... | collective-permute-start | bytes 49160 | tf_op jit(solution)/shard_map/ppermute | solution.py:413
  6.4 3.7 %collective-permute-start.3 = (bf16[4,16,128]{2,1,0:T(8,128)(2,1)S(1)}, bf16[4,16,128]{2,1,0:T(8,128)(2,1)S(1)}, u32[]{:S(2)}, u32[]{:S(2)}) collective-permute-start(bf16[4,16,128]{2,1,0:T(8,128)(2,1)S(1)} %get-tuple-element.19.refs_3_), channel_id=1, source_target_pairs={{0,1},{1,0},{2,3},{3,2},{4,5},{5,4},{6,7},{7,6},{8,9},{9,8},{10,11... | collective-permute-start | bytes 49160 | tf_op jit(solution)/shard_map/ppermute | solution.py:413
  6.9 10.4 %collective-permute-start.4 = (bf16[2,2,2,128,128]{4,3,2,1,0:T(8,128)(2,1)S(1)}, bf16[2,2,2,128,128]{4,3,2,1,0:T(8,128)(2,1)S(1)}, u32[]{:S(2)}, u32[]{:S(2)}) collective-permute-start(bf16[2,2,2,128,128]{4,3,2,1,0:T(8,128)(2,1)S(1)} %block.1), channel_id=1, source_target_pairs={{0,4},{1,5},{2,30},{3,31},{4,2},{5,3},{6,8},{7,9},{8,6},{9,7},{10,... | collective-permute-start | bytes 786440 | tf_op jit(solution)/shard_map/ppermute | solution.py:413
  10.6 6.5 %collective-permute-start.6 = (bf16[2,2,2,2,16,128]{5,4,3,2,1,0:T(8,128)(2,1)S(1)}, bf16[2,2,2,2,16,128]{5,4,3,2,1,0:T(8,128)(2,1)S(1)}, u32[]{:S(2)}, u32[]{:S(2)}) collective-permute-start(bf16[2,2,2,2,16,128]{5,4,3,2,1,0:T(8,128)(2,1)S(1)} %get-tuple-element.27.sent), channel_id=1, source_target_pairs={{0,30},{1,31},{2,4},{3,5},{4,2},{5,3},{6,8},{7,9},{8,6},{9,7},{10,... | collective-permute-start | bytes 196616 | tf_op jit(solution)/shard_map/ppermute | solution.py:413
  14.1 4.1 %collective-permute-start.5 = (bf16[2,2,2,16,128]{4,3,2,1,0:T(8,128)(2,1)S(1)}, bf16[2,2,2,16,128]{4,3,2,1,0:T(8,128)(2,1)S(1)}, u32[]{:S(2)}, u32[]{:S(2)}) collective-permute-start(bf16[2,2,2,16,128]{4,3,2,1,0:T(8,128)(2,1)S(1)} %get-tuple-element.22.other), channel_id=1, source_target_pairs={{0,28},{1,29},{2,6},{3,7},{4,0},{5,1},{6,10},{7,11},{8,4},{9,5},{1... | collective-permute-start | bytes 98312 | tf_op jit(solution)/shard_map/ppermute | solution.py:413
  18.6 1.3 %collective-permute-start.7 = (bf16[2,2,2,16,128]{4,3,2,1,0:T(8,128)(2,1)S(1)}, bf16[2,2,2,16,128]{4,3,2,1,0:T(8,128)(2,1)S(1)}, u32[]{:S(2)}, u32[]{:S(2)}) collective-permute-start(bf16[2,2,2,16,128]{4,3,2,1,0:T(8,128)(2,1)S(1)} %get-tuple-element.29.field_mine.other), channel_id=1, source_target_pairs={{0,2},{1,3},{2,0},{3,1},{4,6},{5,7},{6,4},{7,5},{8,10},{9,11},{10,... | collective-permute-start | bytes 98312 | tf_op jit(solution)/shard_map/ppermute | solution.py:413
  20.1 7.6 %collective-permute-start.8 = (bf16[2,2,2,2,16,128]{5,4,3,2,1,0:T(8,128)(2,1)S(1)}, bf16[2,2,2,2,16,128]{5,4,3,2,1,0:T(8,128)(2,1)S(1)}, u32[]{:S(2)}, u32[]{:S(2)}) collective-permute-start(bf16[2,2,2,2,16,128]{5,4,3,2,1,0:T(8,128)(2,1)S(1)} %get-tuple-element.31.sent), channel_id=1, source_target_pairs={{0,30},{1,31},{2,4},{3,5},{4,2},{5,3},{6,8},{7,9},{8,6},{9,7},{10,... | collective-permute-start | bytes 196616 | tf_op jit(solution)/shard_map/ppermute | solution.py:413
  23.7 3.9 %collective-permute-start.9 = (bf16[2,2,2,16,128]{4,3,2,1,0:T(8,128)(2,1)S(1)}, bf16[2,2,2,16,128]{4,3,2,1,0:T(8,128)(2,1)S(1)}, u32[]{:S(2)}, u32[]{:S(2)}) collective-permute-start(bf16[2,2,2,16,128]{4,3,2,1,0:T(8,128)(2,1)S(1)} %get-tuple-element.29.field_mine.other), channel_id=1, source_target_pairs={{0,28},{1,29},{2,6},{3,7},{4,0},{5,1},{6,10},{7,11},{8,4},{9,5},{1... | collective-permute-start | bytes 98312 | tf_op jit(solution)/shard_map/ppermute | solution.py:413

commit v7 on v6

--- a/solution.py
+++ b/solution.py
@@ -209,7 +209,8 @@
     extent = operator.shape[2:5]
     position = lax.axis_index("xy")
     even, _ = time_sides(True)
-    parts = parts[::-1]
+    if pieces > 1:
+        parts = (parts[3], parts[1], parts[2], parts[0])
     for whole, held in ((rhs_mine, parts[:pieces]), (rhs_pair, parts[pieces:])):
         for y in range(extent[0]):
             for z in range(extent[1]):
@@ -237,7 +238,7 @@
     for_sites(extent, step)
 
 
-def first_pair_kernel(op_mine, op_pair, rhs_pair, here, other, part_pair, packed_mine, packed_pair):
+def first_pair_kernel(op_mine, op_pair, rhs_pair, here, other, part_pair, packed_mine, packed_pair, through_pair):
     sides, pair_sides = time_sides(True), time_sides(False)
 
     def step(site):
@@ -245,20 +246,47 @@
         packed_pair[site] = packed(op_pair, site, pair_sides)
         sums = packed_stencil(packed_pair, site, here, [other])
         value = RELAX_WEIGHT * rhs_pair[site].astype(jnp.float32)
-        part_pair[site] = relaxed(value, here[site], rhs_pair[site], sums)
+        part_pair[site] = relaxed(value, here[site], rhs_pair[site], sums).astype(jnp.bfloat16)
+        outer, inner = packed_pair[site][side_rows(packed_pair, 1)], packed_mine[site][side_rows(packed_mine, 2)]
+        through_pair[site] = two_steps(outer, inner).astype(jnp.bfloat16)
 
     for_sites(op_mine.shape[2:5], step)
 
 
-def second_pair_kernel(packed_pair, rhs_pair, here, other, part_pair):
-    def step(site):
-        sums = packed_stencil(packed_pair, site, here, [other])
-        part_pair[site] = relaxed(here[site].astype(jnp.float32), here[site], rhs_pair[site], sums)
-
-    for_sites(packed_pair.shape[:3], step)
-
-
-def second_near_kernel(op_mine, back_near, rhs_mine, sent, part_mine, near, rest, one_mine, one_near):
+def second_pair_kernel(
+    op_mine, op_pair, back_near, rhs_mine, rhs_pair, here, other, sent, part_mine, rest, through_near, part_pair, returned,
+):
+    extent = op_mine.shape[:3]
+    columns = op_mine.shape[4]
+    mine = sent.at[1]
+
+    def first(site):
+        sums = packed_stencil(op_pair, site, here, [other])
+        part_pair[site] = relaxed(here[site].astype(jnp.float32), here[site], rhs_pair[site], sums).astype(jnp.bfloat16)
+        value = -RELAX_WEIGHT * products([(back_near[site], other[site])])
+        returned[site] = value.astype(jnp.bfloat16)
+
+    for_sites(extent, first)
+
+    def second(site):
+        sums = packed_stencil(op_mine, site, mine, [part_pair, returned])
+        rest[site] = relaxed(part_mine[site], mine[site], rhs_mine[site], sums)
+        for index, near in enumerate(nearby(site, extent)):
+            side = op_mine[near][side_rows(op_mine, 1)]
+            block = two_steps(side, op_mine[site][index * columns : (index + 1) * columns])
+            if index == 0:
+                kept = RELAX_WEIGHT * (1 - RELAX_WEIGHT * DIAGONAL_SHIFT)
+                block = block - kept * side.astype(jnp.float32)
+            through_near[site + (slice(index * columns, (index + 1) * columns),)] = block.astype(jnp.bfloat16)
+
+    for_sites(extent, second)
+
+
+def two_steps(first, second):
+    return RELAX_WEIGHT * RELAX_WEIGHT * jnp.dot(first, second, preferred_element_type=jnp.float32)
+
+
+def second_near_kernel(op_mine, back_near, rhs_mine, sent, part_mine, part_pair, near, rest, one_mine, one_near):
     def first(site):
         value = near_step(op_mine, part_mine, near.at[0], site)
         rest[site] = value
@@ -268,21 +296,19 @@
     for_sites(op_mine.shape[:3], first)
 
     def second(site):
-        sums = packed_stencil(op_mine, site, one_mine, []) + side_product(one_near, op_mine, site, 1)
+        sums = packed_stencil(op_mine, site, one_mine, [part_pair, one_near])
         rest[site] = relaxed(rest[site], one_mine[site], rhs_mine[site], sums)
 
     for_sites(op_mine.shape[:3], second)
 
 
-def second_far_kernel(op_mine, op_pair, part_pair, far, rest, field_mine, value_mine):
+def second_far_kernel(through_pair, far, rest, field_mine, value_mine):
     def step(site):
-        one_pair = near_step(op_pair, part_pair, far, site).astype(jnp.bfloat16)
-        sums = jnp.dot(one_pair, op_mine[site][side_rows(op_mine, 2)], preferred_element_type=jnp.float32)
-        value = rest[site] - RELAX_WEIGHT * sums
+        value = rest[site] + jnp.dot(far[site], through_pair[site], preferred_element_type=jnp.float32)
         value_mine[site] = value
         field_mine[site] = value.astype(jnp.bfloat16)
 
-    for_sites(op_mine.shape[:3], step)
+    for_sites(rest.shape[:3], step)
 
 
 def side_rows(weights, last):
@@ -322,26 +348,25 @@
 
 
 def last_kernel(
-    op_mine, op_pair, back_near, rhs_mine, sent, part_mine, part_pair, near, far, null,
-    fine_out, coarse_out, one_mine, one_pair, one_near, x_mine, result, held, done,
+    op_mine, through_near, through_pair, rest, near, far, null,
+    fine_out, coarse_out, result, held, done,
 ):
-    extent = op_mine.shape[:3]
-
-    def first(site):
-        value = near_step(op_mine, part_mine, near.at[0], site)
-        x_mine[site] = value
-        one_mine[site] = value.astype(jnp.bfloat16)
-        one_pair[site] = near_step(op_pair, part_pair, far, site).astype(jnp.bfloat16)
-        one_near[site] = return_step(back_near, sent, near, site)
-
-    for_sites(extent, first)
-
-    def second(site):
-        sums = packed_stencil(op_mine, site, one_mine, [one_pair, one_near])
-        value = relaxed(x_mine[site], one_mine[site], rhs_mine[site], sums)
+    extent = rest.shape[:3]
+    field = near.at[0]
+
+    def step(site):
+        sums = jnp.dot(
+            jnp.concatenate([field[other] for other in nearby(site, extent)], axis=1),
+            through_near[site],
+            preferred_element_type=jnp.float32,
+        )
+        sums += jnp.dot(far[site], through_pair[site], preferred_element_type=jnp.float32)
+        value = rest[site] + sums - RELAX_WEIGHT * jnp.dot(
+            near[(1,) + site], op_mine[site][side_rows(op_mine, 1)], preferred_element_type=jnp.float32
+        )
         result[(0,) + site] = value.astype(jnp.bfloat16)
 
-    for_sites(extent, second)
+    for_sites(extent, step)
     times = held.shape[0]
     copy = pltpu.make_async_copy(result, coarse_out, done.at[times])
     copy.start()
@@ -352,7 +377,7 @@
 
 
 def last(shape, *operands):
-    full, times = operands[5].shape, shape[0]
+    full, times = operands[3].shape, shape[0]
     return pl.pallas_call(
         last_kernel,
         in_specs=[pl.BlockSpec(memory_space=pltpu.VMEM)] * len(operands),
@@ -361,9 +386,7 @@
             jax.ShapeDtypeStruct(shape, jnp.bfloat16),
             jax.ShapeDtypeStruct((1,) + full, jnp.bfloat16),
         ],
-        scratch_shapes=[pltpu.VMEM(full, jnp.bfloat16)] * 3
-        + [
-            pltpu.VMEM(full, jnp.float32),
+        scratch_shapes=[
             pltpu.VMEM((1,) + full, jnp.bfloat16),
             pltpu.VMEM(shape, jnp.bfloat16),
             pltpu.SemaphoreType.DMA((times + 1,)),
@@ -425,7 +448,7 @@
     full = extent + own.shape[1:]
     if columns == 2:
         corner, pair, beside = send(own, other, 1), send(own, other), send(own, same, 1)
-        parts = [own, beside, pair, corner]
+        parts = [corner, beside, pair, own]
     else:
         every = lax.all_gather(own, "xy")
         parts = [every, send(every, other)]
@@ -438,24 +461,24 @@
         [(full, bf16)] * 4 + [((2,) + full, bf16), (full, f32)],
         [],
         operator,
-        *parts[::-1],
+        *parts,
         flops=GATHER_FLOPS,
     )
     near_message, far_field = send(sent, across), send(start_mine, far)
-    (part_pair, packed_mine, packed_pair) = kernel_call(
+    packed_shape = extent + (packed_depth(operator), operator.shape[6])
+    part_pair, packed_mine, packed_pair, through_pair = kernel_call(
         first_pair_kernel,
         "pair_one",
-        [(full, f32)] + [(extent + (packed_depth(operator), operator.shape[6]), bf16)] * 2,
+        [(full, bf16), (packed_shape, bf16), (packed_shape, bf16), (operator.shape[2:], bf16)],
         [],
         operator, op_pair, rhs_pair, start_pair, start_mine,
     )
     (rest,) = kernel_call(
         second_near_kernel, "second_near", [(full, f32)], [(full, bf16)] * 2,
-        packed_mine, back_near, rhs_mine, sent, part_mine, near_message,
+        packed_mine, back_near, rhs_mine, sent, part_mine, part_pair, near_message,
     )
     field_mine, value_mine = kernel_call(
-        second_far_kernel, "second_far", [(full, bf16), (full, f32)], [],
-        packed_mine, packed_pair, part_pair, far_field, rest,
+        second_far_kernel, "second_far", [(full, bf16), (full, f32)], [], through_pair, far_field, rest,
     )
     field_pair = send(field_mine, other)
     (rest,) = kernel_call(
@@ -465,13 +488,16 @@
         third_kernel, "third", [((2,) + full, bf16), (full, f32)], [], packed_mine, rest, field_mine, field_pair,
     )
     near_message, far_field = send(sent, across), send(field_mine, far)
-    (part_pair,) = kernel_call(
-        second_pair_kernel, "pair_two", [(full, f32)], [],
-        packed_pair, rhs_pair, field_pair, field_mine,
+    rest, through_near = kernel_call(
+        second_pair_kernel,
+        "pair_two",
+        [(full, f32), (extent + (packed_shape[3] - 2 * packed_shape[4], packed_shape[4]), bf16)],
+        [(full, bf16)] * 2,
+        packed_mine, packed_pair, back_near, rhs_mine, rhs_pair, field_pair, field_mine, sent, part_mine,
     )
     fine_correction, coarse_iterate = last(
         fine_vectors.shape,
-        packed_mine, packed_pair, back_near, rhs_mine, sent, part_mine, part_pair, near_message, far_field, null_kept,
+        packed_mine, through_near, through_pair, rest, near_message, far_field, null_kept,
     )
     return (fine_correction, coarse_iterate)
 

time: 29.7 us -> 29.3 us (0.987)
  waiting for transfers between devices: 6.58 us -> 5.14 us
  starting transfers between devices: 14.6 us -> 15.3 us
  Pallas kernels: 7.69 us -> 8.04 us
    ppermute x10, waiting for transfers between devices: 6.58 us -> 5.14 us  [send(): return lax.ppermute(array, ('zt', 'xy'), permutation(target, turn))]
    ppermute x10, starting transfers between devices: 14.6 us -> 15.3 us  [send(): return lax.ppermute(array, ('zt', 'xy'), permutation(target, turn))]
    pallas_call x8, Pallas kernels: 3.22 us -> 3.8 us  [kernel_call(): pl.pallas_call(kernel, in_specs=[pl.BlockSpec(memory_space=pltpu.VMEM)] *...]
  transfers between devices with their start and end apart: 10 -> 10, of which waited for: 6 -> 5; matrix products, arithmetic and copies ran while one was open for 0% -> 0% of each run, Pallas kernels for 18% -> 20%
where the time goes in v7:
time: 29.3 us; the launch traced here: 29.2 us
  starting transfers between devices  15.3 us (52%)
  Pallas kernels  8.04 us (27%)
  waiting for transfers between devices  5.14 us (18%)
  between operations  0.69 us (2%)
    ppermute x10, starting transfers between devices, send(): return lax.ppermute(array, ('zt', 'xy'), permutation(target, turn))  15.3 us
    ppermute x10, waiting for transfers between devices, send(): return lax.ppermute(array, ('zt', 'xy'), permutation(target, turn))  5.14 us
    pallas_call x8, Pallas kernels, kernel_call(): pl.pallas_call(kernel, in_specs=[pl.BlockSpec(memory_space=pltpu.VMEM)] *...  3.8 us
    pallas_call x1, Pallas kernels, restrict(): pl.pallas_call(functools.partial(restrict_kernel, coarse_y), in_specs=[pl...  2.52 us
    pallas_call x1, Pallas kernels, last(): pl.pallas_call(last_kernel, in_specs=[pl.BlockSpec(memory_space=pltpu.VME...  1.73 us
  transfers between devices with their start and end apart: 10, of which 5 were waited for; matrix products, arithmetic and copies ran while one was open for 0% of the time, Pallas kernels for 20%

profile of v7, /device:TPU:0, one launch (start us, length us, event | category | flops | bytes accessed | tf_op | source)
XLA Modules:
  0.0 29.2 jit_solution(10656125141379492511)
XLA Ops:
  0.6 0.5 %collective-permute-start = (bf16[1,9,2,2,2,128,128]{6,5,4,3,2,1,0:T(8,128)(2,1)}, bf16[1,9,2,2,2,128,128]{6,5,4,3,2,1,0:T(8,128)(2,1)S(1)}, u32[]{:S(2)}, u32[]{:S(2)}) collective-permute-start(bf16[1,9,2,2,2,128,128]{6,5,4,3,2,1,0:T(8,128)(2,1)} %operator_hbm.1), channel_id=1, source_target_pairs={{0,2},{1,3},{2,0},{3,1},{4,6},{5,7},{6,4},{7,5},{8,10},{9,11},{10,... | collective-permute-start | bytes 7077896 | tf_op jit(solution)/shard_map/ppermute | solution.py:436
  1.1 2.5 %restrict.1 = (bf16[4,16,128]{2,1,0:T(8,128)(2,1)S(1)}, bf16[4,2,12,32,256]{4,3,2,1,0:T(8,128)(2,1)S(1)}, bf16[1,9,2,2,2,128,128]{6,5,4,3,2,1,0:T(8,128)(2,1)S(1)}) custom-call(bf16[4,2,12,16,256]{4,3,2,1,0:T(8,128)(2,1)} %fine_hbm.1, bf16[4,2,12,32,256]{4,3,2,1,0:T(8,128)(2,1)} %null_hbm.1, bf16[1,9,2,2,2,128,128]{6,5,4,3,2,1,0:T(8,128)(2,1)} %operator_hbm.1), custom_call_target="tpu_custom_call" | custom-call | tf_op jit(solution)/shard_map/restrict/pallas_call | solution.py:71
  3.7 2.7 %collective-permute-start.1 = (bf16[4,16,128]{2,1,0:T(8,128)(2,1)S(1)}, bf16[4,16,128]{2,1,0:T(8,128)(2,1)S(1)}, u32[]{:S(2)}, u32[]{:S(2)}) collective-permute-start(bf16[4,16,128]{2,1,0:T(8,128)(2,1)S(1)} %get-tuple-element.22.refs_3_), channel_id=1, source_target_pairs={{0,3},{1,2},{2,1},{3,0},{4,7},{5,6},{6,5},{7,4},{8,11},{9,10},{10,... | collective-permute-start | bytes 49160 | tf_op jit(solution)/shard_map/ppermute | solution.py:436
  6.4 0.0 collective-permute-start.2
  6.4 0.2 collective-permute-start.3
  6.6 0.0 collective-permute-done.op_pair
  6.6 1.9 %collective-permute-start.4 = (bf16[2,2,2,128,128]{4,3,2,1,0:T(8,128)(2,1)S(1)}, bf16[2,2,2,128,128]{4,3,2,1,0:T(8,128)(2,1)S(1)}, u32[]{:S(2)}, u32[]{:S(2)}) collective-permute-start(bf16[2,2,2,128,128]{4,3,2,1,0:T(8,128)(2,1)S(1)} %block.1), channel_id=1, source_target_pairs={{0,4},{1,5},{2,30},{3,31},{4,2},{5,3},{6,8},{7,9},{8,6},{9,7},{10,... | collective-permute-start | bytes 786440 | tf_op jit(solution)/shard_map/ppermute | solution.py:436
  8.5 0.0 collective-permute-done.1.refs_0_
  8.5 1.7 %collective-permute-done.2.refs_1_ = bf16[4,16,128]{2,1,0:T(8,128)(2,1)S(1)} collective-permute-done((bf16[4,16,128]{2,1,0:T(8,128)(2,1)S(1)}, bf16[4,16,128]{2,1,0:T(8,128)(2,1)S(1)}, u32[]{:S(2)}, u32[]{:S(2)}) %collective-permute-start.2) | collective-permute-done | bytes 16416 | tf_op jit(solution)/shard_map/ppermute | solution.py:436
  10.1 0.0 collective-permute-done.3.refs_2_
  10.1 0.5 %gather.1 = (bf16[2,2,2,16,128]{4,3,2,1,0:T(8,128)(2,1)S(1)}, bf16[2,2,2,16,128]{4,3,2,1,0:T(8,128)(2,1)S(1)}, bf16[2,2,2,16,128]{4,3,2,1,0:T(8,128)(2,1)S(1)}, ...) custom-call(bf16[1,9,2,2,2,128,128]{6,5,4,3,2,1,0:T(8,128)(2,1)S(1)}, ...), custom_call_target="tpu_custom_call" | custom-call | flops 10000000000 | tf_op jit(solution)/shard_map/gather/pallas_call | solution.py:413
  10.6 3.0 %collective-permute-start.6 = (bf16[2,2,2,2,16,128]{5,4,3,2,1,0:T(8,128)(2,1)S(1)}, bf16[2,2,2,2,16,128]{5,4,3,2,1,0:T(8,128)(2,1)S(1)}, u32[]{:S(2)}, u32[]{:S(2)}) collective-permute-start(bf16[2,2,2,2,16,128]{5,4,3,2,1,0:T(8,128)(2,1)S(1)} %get-tuple-element.30.sent), channel_id=1, source_target_pairs={{0,30},{1,31},{2,4},{3,5},{4,2},{5,3},{6,8},{7,9},{8,6},{9,7},{10,... | collective-permute-start | bytes 196616 | tf_op jit(solution)/shard_map/ppermute | solution.py:436
  13.6 1.6 %collective-permute-start.5 = (bf16[2,2,2,16,128]{4,3,2,1,0:T(8,128)(2,1)S(1)}, bf16[2,2,2,16,128]{4,3,2,1,0:T(8,128)(2,1)S(1)}, u32[]{:S(2)}, u32[]{:S(2)}) collective-permute-start(bf16[2,2,2,16,128]{4,3,2,1,0:T(8,128)(2,1)S(1)} %get-tuple-element.25.other), channel_id=1, source_target_pairs={{0,28},{1,29},{2,6},{3,7},{4,0},{5,1},{6,10},{7,11},{8,4},{9,5},{1... | collective-permute-start | bytes 98312 | tf_op jit(solution)/shard_map/ppermute | solution.py:436
  15.2 1.1 %pair_one.1 = (bf16[2,2,2,16,128]{4,3,2,1,0:T(8,128)(2,1)S(1)}, bf16[2,2,2,768,128]{4,3,2,1,0:T(8,128)(2,1)S(1)}, bf16[2,2,2,768,128]{4,3,2,1,0:T(8,128)(2,1)S(1)}, bf16[2,2,2,128,128]{4,3,2,1,0:T(8,128)(2,1)S(1)}) custom-call(bf16[1,9,2,2,2,128,128]{6,5,4,3,2,1,0:T(8,128)(2,1)S(1)} %get-tuple-element.21.operator.op_mine, ...), custom_call_target="tpu_custom_call" | custom-call | tf_op jit(solution)/shard_map/pair_one/pallas_call | solution.py:413
  16.3 0.9 %collective-permute-done.6.near = bf16[2,2,2,2,16,128]{5,4,3,2,1,0:T(8,128)(2,1)S(1)} collective-permute-done((bf16[2,2,2,2,16,128]{5,4,3,2,1,0:T(8,128)(2,1)S(1)}, bf16[2,2,2,2,16,128]{5,4,3,2,1,0:T(8,128)(2,1)S(1)}, u32[]{:S(2)}, u32[]{:S(2)}) %collective-permute-start.6) | collective-permute-done | bytes 65568 | tf_op jit(solution)/shard_map/ppermute | solution.py:436
  17.2 0.1 collective-permute-done.4.back_near
  17.3 0.5 %second_near.1.rest = f32[2,2,2,16,128]{4,3,2,1,0:T(8,128)S(1)} custom-call(bf16[2,2,2,768,128]{4,3,2,1,0:T(8,128)(2,1)S(1)} %get-tuple-element.26.op_mine, bf16[2,2,2,128,128]{4,3,2,1,0:T(8,128)(2,1)S(1)} %collective-permute-done.4.back_near, bf16[2,2,2,16,128]{4,3,2,1,0:T(8,128)(2,1)S(1)} %get-tuple-element.28.rhs_mine, ...), custom_call_target="tpu_custom_call" | custom-call | tf_op jit(solution)/shard_map/second_near/pallas_call | solution.py:413
  17.8 0.0 collective-permute-done.5.far
  17.8 0.2 second_far.1
  18.0 0.1 collective-permute-start.7
  18.1 0.2 third_own.1.rest
  18.3 0.9 %collective-permute-done.7.field_pair.here = bf16[2,2,2,16,128]{4,3,2,1,0:T(8,128)(2,1)S(1)} collective-permute-done((bf16[2,2,2,16,128]{4,3,2,1,0:T(8,128)(2,1)S(1)}, bf16[2,2,2,16,128]{4,3,2,1,0:T(8,128)(2,1)S(1)}, u32[]{:S(2)}, u32[]{:S(2)}) %collective-permute-start.7) | collective-permute-done | bytes 32800 | tf_op jit(solution)/shard_map/ppermute | solution.py:436
  19.3 0.2 third.1
  19.5 4.1 %collective-permute-start.8 = (bf16[2,2,2,2,16,128]{5,4,3,2,1,0:T(8,128)(2,1)S(1)}, bf16[2,2,2,2,16,128]{5,4,3,2,1,0:T(8,128)(2,1)S(1)}, u32[]{:S(2)}, u32[]{:S(2)}) collective-permute-start(bf16[2,2,2,2,16,128]{5,4,3,2,1,0:T(8,128)(2,1)S(1)} %get-tuple-element.35.sent), channel_id=1, source_target_pairs={{0,30},{1,31},{2,4},{3,5},{4,2},{5,3},{6,8},{7,9},{8,6},{9,7},{10,... | collective-permute-start | bytes 196616 | tf_op jit(solution)/shard_map/ppermute | solution.py:436
  23.5 1.3 %collective-permute-start.9 = (bf16[2,2,2,16,128]{4,3,2,1,0:T(8,128)(2,1)S(1)}, bf16[2,2,2,16,128]{4,3,2,1,0:T(8,128)(2,1)S(1)}, u32[]{:S(2)}, u32[]{:S(2)}) collective-permute-start(bf16[2,2,2,16,128]{4,3,2,1,0:T(8,128)(2,1)S(1)} %get-tuple-element.33.field_mine.other), channel_id=1, source_target_pairs={{0,28},{1,29},{2,6},{3,7},{4,0},{5,1},{6,10},{7,11},{8,4},{9,5},{1... | collective-permute-start | bytes 98312 | tf_op jit(solution)/shard_map/ppermute | solution.py:436
  24.9 1.0 %pair_two.1 = (f32[2,2,2,16,128]{4,3,2,1,0:T(8,128)S(1)}, bf16[2,2,2,512,128]{4,3,2,1,0:T(8,128)(2,1)S(1)}) custom-call(bf16[2,2,2,768,128]{4,3,2,1,0:T(8,128)(2,1)S(1)} %get-tuple-element.26.op_mine, bf16[2,2,2,768,128]{4,3,2,1,0:T(8,128)(2,1)S(1)} %get-tuple-element.27.op_pair, bf16[2,2,2,128,128]{4,3,2,1,0:T(8,128)(2,1)S(1)} %collective-permute-done.4.back_near, ...), custom_call_target="tpu_custom_call" | custom-call | tf_op jit(solution)/shard_map/pair_two/pallas_call | solution.py:413
  25.9 1.6 %collective-permute-done.9.far = bf16[2,2,2,16,128]{4,3,2,1,0:T(8,128)(2,1)S(1)} collective-permute-done((bf16[2,2,2,16,128]{4,3,2,1,0:T(8,128)(2,1)S(1)}, bf16[2,2,2,16,128]{4,3,2,1,0:T(8,128)(2,1)S(1)}, u32[]{:S(2)}, u32[]{:S(2)}) %collective-permute-start.9) | collective-permute-done | bytes 32800 | tf_op jit(solution)/shard_map/ppermute | solution.py:436
  27.5 0.0 collective-permute-done.8.near
  27.5 1.7 %last.1 = (bf16[4,2,12,16,256]{4,3,2,1,0:T(8,128)(2,1)}, bf16[1,2,2,2,16,128]{5,4,3,2,1,0:T(8,128)(2,1)}) custom-call(bf16[2,2,2,768,128]{4,3,2,1,0:T(8,128)(2,1)S(1)} %get-tuple-element.26.op_mine, bf16[2,2,2,512,128]{4,3,2,1,0:T(8,128)(2,1)S(1)} %get-tuple-element.37.through_near, bf16[2,2,2,128,128]{4,3,2,1,0:T(8,128)(2,1)S(1)} %get-tuple-element.29.through_pair, ...), custom_call_target="tpu_custom_call" | custom-call | tf_op jit(solution)/shard_map/last/pallas_call | solution.py:381
  (1 shorter events, 0.0 us)
Async XLA Ops:
  0.6 5.9 %collective-permute-start = (bf16[1,9,2,2,2,128,128]{6,5,4,3,2,1,0:T(8,128)(2,1)}, bf16[1,9,2,2,2,128,128]{6,5,4,3,2,1,0:T(8,128)(2,1)S(1)}, u32[]{:S(2)}, u32[]{:S(2)}) collective-permute-start(bf16[1,9,2,2,2,128,128]{6,5,4,3,2,1,0:T(8,128)(2,1)} %operator_hbm.1), channel_id=1, source_target_pairs={{0,2},{1,3},{2,0},{3,1},{4,6},{5,7},{6,4},{7,5},{8,10},{9,11},{10,... | collective-permute-start | bytes 7077896 | tf_op jit(solution)/shard_map/ppermute | solution.py:436
  3.7 4.8 %collective-permute-start.1 = (bf16[4,16,128]{2,1,0:T(8,128)(2,1)S(1)}, bf16[4,16,128]{2,1,0:T(8,128)(2,1)S(1)}, u32[]{:S(2)}, u32[]{:S(2)}) collective-permute-start(bf16[4,16,128]{2,1,0:T(8,128)(2,1)S(1)} %get-tuple-element.22.refs_3_), channel_id=1, source_target_pairs={{0,3},{1,2},{2,1},{3,0},{4,7},{5,6},{6,5},{7,4},{8,11},{9,10},{10,... | collective-permute-start | bytes 49160 | tf_op jit(solution)/shard_map/ppermute | solution.py:436
  6.4 3.7 %collective-permute-start.2 = (bf16[4,16,128]{2,1,0:T(8,128)(2,1)S(1)}, bf16[4,16,128]{2,1,0:T(8,128)(2,1)S(1)}, u32[]{:S(2)}, u32[]{:S(2)}) collective-permute-start(bf16[4,16,128]{2,1,0:T(8,128)(2,1)S(1)} %get-tuple-element.22.refs_3_), channel_id=1, source_target_pairs={{0,1},{1,0},{2,3},{3,2},{4,5},{5,4},{6,7},{7,6},{8,9},{9,8},{10,11... | collective-permute-start | bytes 49160 | tf_op jit(solution)/shard_map/ppermute | solution.py:436
  6.4 3.7 %collective-permute-start.3 = (bf16[4,16,128]{2,1,0:T(8,128)(2,1)S(1)}, bf16[4,16,128]{2,1,0:T(8,128)(2,1)S(1)}, u32[]{:S(2)}, u32[]{:S(2)}) collective-permute-start(bf16[4,16,128]{2,1,0:T(8,128)(2,1)S(1)} %get-tuple-element.22.refs_3_), channel_id=1, source_target_pairs={{0,2},{1,3},{2,0},{3,1},{4,6},{5,7},{6,4},{7,5},{8,10},{9,11},{10,... | collective-permute-start | bytes 49160 | tf_op jit(solution)/shard_map/ppermute | solution.py:436
  6.6 10.7 %collective-permute-start.4 = (bf16[2,2,2,128,128]{4,3,2,1,0:T(8,128)(2,1)S(1)}, bf16[2,2,2,128,128]{4,3,2,1,0:T(8,128)(2,1)S(1)}, u32[]{:S(2)}, u32[]{:S(2)}) collective-permute-start(bf16[2,2,2,128,128]{4,3,2,1,0:T(8,128)(2,1)S(1)} %block.1), channel_id=1, source_target_pairs={{0,4},{1,5},{2,30},{3,31},{4,2},{5,3},{6,8},{7,9},{8,6},{9,7},{10,... | collective-permute-start | bytes 786440 | tf_op jit(solution)/shard_map/ppermute | solution.py:436
  10.6 6.5 %collective-permute-start.6 = (bf16[2,2,2,2,16,128]{5,4,3,2,1,0:T(8,128)(2,1)S(1)}, bf16[2,2,2,2,16,128]{5,4,3,2,1,0:T(8,128)(2,1)S(1)}, u32[]{:S(2)}, u32[]{:S(2)}) collective-permute-start(bf16[2,2,2,2,16,128]{5,4,3,2,1,0:T(8,128)(2,1)S(1)} %get-tuple-element.30.sent), channel_id=1, source_target_pairs={{0,30},{1,31},{2,4},{3,5},{4,2},{5,3},{6,8},{7,9},{8,6},{9,7},{10,... | collective-permute-start | bytes 196616 | tf_op jit(solution)/shard_map/ppermute | solution.py:436
  13.6 4.2 %collective-permute-start.5 = (bf16[2,2,2,16,128]{4,3,2,1,0:T(8,128)(2,1)S(1)}, bf16[2,2,2,16,128]{4,3,2,1,0:T(8,128)(2,1)S(1)}, u32[]{:S(2)}, u32[]{:S(2)}) collective-permute-start(bf16[2,2,2,16,128]{4,3,2,1,0:T(8,128)(2,1)S(1)} %get-tuple-element.25.other), channel_id=1, source_target_pairs={{0,28},{1,29},{2,6},{3,7},{4,0},{5,1},{6,10},{7,11},{8,4},{9,5},{1... | collective-permute-start | bytes 98312 | tf_op jit(solution)/shard_map/ppermute | solution.py:436
  18.0 1.3 %collective-permute-start.7 = (bf16[2,2,2,16,128]{4,3,2,1,0:T(8,128)(2,1)S(1)}, bf16[2,2,2,16,128]{4,3,2,1,0:T(8,128)(2,1)S(1)}, u32[]{:S(2)}, u32[]{:S(2)}) collective-permute-start(bf16[2,2,2,16,128]{4,3,2,1,0:T(8,128)(2,1)S(1)} %get-tuple-element.33.field_mine.other), channel_id=1, source_target_pairs={{0,2},{1,3},{2,0},{3,1},{4,6},{5,7},{6,4},{7,5},{8,10},{9,11},{10,... | collective-permute-start | bytes 98312 | tf_op jit(solution)/shard_map/ppermute | solution.py:436
  19.5 8.0 %collective-permute-start.8 = (bf16[2,2,2,2,16,128]{5,4,3,2,1,0:T(8,128)(2,1)S(1)}, bf16[2,2,2,2,16,128]{5,4,3,2,1,0:T(8,128)(2,1)S(1)}, u32[]{:S(2)}, u32[]{:S(2)}) collective-permute-start(bf16[2,2,2,2,16,128]{5,4,3,2,1,0:T(8,128)(2,1)S(1)} %get-tuple-element.35.sent), channel_id=1, source_target_pairs={{0,30},{1,31},{2,4},{3,5},{4,2},{5,3},{6,8},{7,9},{8,6},{9,7},{10,... | collective-permute-start | bytes 196616 | tf_op jit(solution)/shard_map/ppermute | solution.py:436
  23.5 3.9 %collective-permute-start.9 = (bf16[2,2,2,16,128]{4,3,2,1,0:T(8,128)(2,1)S(1)}, bf16[2,2,2,16,128]{4,3,2,1,0:T(8,128)(2,1)S(1)}, u32[]{:S(2)}, u32[]{:S(2)}) collective-permute-start(bf16[2,2,2,16,128]{4,3,2,1,0:T(8,128)(2,1)S(1)} %get-tuple-element.33.field_mine.other), channel_id=1, source_target_pairs={{0,28},{1,29},{2,6},{3,7},{4,0},{5,1},{6,10},{7,11},{8,4},{9,5},{1... | collective-permute-start | bytes 98312 | tf_op jit(solution)/shard_map/ppermute | solution.py:436

commit v8 on v7

--- a/solution.py
+++ b/solution.py
@@ -238,7 +238,10 @@
     for_sites(extent, step)
 
 
-def first_pair_kernel(op_mine, op_pair, rhs_pair, here, other, part_pair, packed_mine, packed_pair, through_pair):
+def first_pair_kernel(
+    op_mine, op_pair, rhs_mine, rhs_pair, here, other, sent, part_mine,
+    packed_mine, packed_pair, rest, through_near, through_pair, through_mine, part_pair,
+):
     sides, pair_sides = time_sides(True), time_sides(False)
 
     def step(site):
@@ -249,15 +252,32 @@
         part_pair[site] = relaxed(value, here[site], rhs_pair[site], sums).astype(jnp.bfloat16)
         outer, inner = packed_pair[site][side_rows(packed_pair, 1)], packed_mine[site][side_rows(packed_mine, 2)]
         through_pair[site] = two_steps(outer, inner).astype(jnp.bfloat16)
-
-    for_sites(op_mine.shape[2:5], step)
+        outer, inner = packed_mine[site][side_rows(packed_mine, 1)], packed_pair[site][side_rows(packed_pair, 2)]
+        through_mine[site] = two_steps(outer, inner).astype(jnp.bfloat16)
+
+    extent = op_mine.shape[2:5]
+    columns = op_mine.shape[6]
+    mine = sent.at[1]
+    for_sites(extent, step)
+
+    def ahead(site):
+        sums = packed_stencil(packed_mine, site, mine, [part_pair])
+        rest[site] = relaxed(part_mine[site], mine[site], rhs_mine[site], sums)
+        for index, near in enumerate(nearby(site, extent)):
+            side = packed_mine[near][side_rows(packed_mine, 1)]
+            block = two_steps(side, packed_mine[site][index * columns : (index + 1) * columns])
+            if index == 0:
+                kept = RELAX_WEIGHT * (1 - RELAX_WEIGHT * DIAGONAL_SHIFT)
+                block = block - kept * side.astype(jnp.float32)
+            through_near[site + (slice(index * columns, (index + 1) * columns),)] = block.astype(jnp.bfloat16)
+
+    for_sites(extent, ahead)
 
 
 def second_pair_kernel(
-    op_mine, op_pair, back_near, rhs_mine, rhs_pair, here, other, sent, part_mine, rest, through_near, part_pair, returned,
+    op_mine, op_pair, back_near, rhs_mine, rhs_pair, here, other, sent, part_mine, rest, part_pair, returned,
 ):
     extent = op_mine.shape[:3]
-    columns = op_mine.shape[4]
     mine = sent.at[1]
 
     def first(site):
@@ -271,13 +291,6 @@
     def second(site):
         sums = packed_stencil(op_mine, site, mine, [part_pair, returned])
         rest[site] = relaxed(part_mine[site], mine[site], rhs_mine[site], sums)
-        for index, near in enumerate(nearby(site, extent)):
-            side = op_mine[near][side_rows(op_mine, 1)]
-            block = two_steps(side, op_mine[site][index * columns : (index + 1) * columns])
-            if index == 0:
-                kept = RELAX_WEIGHT * (1 - RELAX_WEIGHT * DIAGONAL_SHIFT)
-                block = block - kept * side.astype(jnp.float32)
-            through_near[site + (slice(index * columns, (index + 1) * columns),)] = block.astype(jnp.bfloat16)
 
     for_sites(extent, second)
 
@@ -286,29 +299,30 @@
     return RELAX_WEIGHT * RELAX_WEIGHT * jnp.dot(first, second, preferred_element_type=jnp.float32)
 
 
-def second_near_kernel(op_mine, back_near, rhs_mine, sent, part_mine, part_pair, near, rest, one_mine, one_near):
+def second_kernel(op_mine, through_near, through_mine, back_near, sent, rest, near, value, swapped, one_near):
+    extent = rest.shape[:3]
+    field = near.at[0]
+
     def first(site):
-        value = near_step(op_mine, part_mine, near.at[0], site)
-        rest[site] = value
-        one_mine[site] = value.astype(jnp.bfloat16)
-        one_near[site] = return_step(back_near, sent, near, site)
-
-    for_sites(op_mine.shape[:3], first)
+        sums = products([(back_near[site], sent[(0,) + site])])
+        one_near[site] = (near[(1,) + site].astype(jnp.float32) - RELAX_WEIGHT * sums).astype(jnp.bfloat16)
+        sums = jnp.dot(field[site], through_mine[site], preferred_element_type=jnp.float32)
+        swapped[(1,) + site] = sums.astype(jnp.bfloat16)
+
+    for_sites(extent, first)
 
     def second(site):
-        sums = packed_stencil(op_mine, site, one_mine, [part_pair, one_near])
-        rest[site] = relaxed(rest[site], one_mine[site], rhs_mine[site], sums)
-
-    for_sites(op_mine.shape[:3], second)
-
-
-def second_far_kernel(through_pair, far, rest, field_mine, value_mine):
-    def step(site):
-        value = rest[site] + jnp.dot(far[site], through_pair[site], preferred_element_type=jnp.float32)
-        value_mine[site] = value
-        field_mine[site] = value.astype(jnp.bfloat16)
-
-    for_sites(rest.shape[:3], step)
+        result = rest[site] + answer(op_mine, through_near, field, one_near, site)
+        value[site] = result
+        swapped[(0,) + site] = result.astype(jnp.bfloat16)
+
+    for_sites(extent, second)
+
+
+def answer(op_mine, through_near, field, one_near, site):
+    fields = [field[other] for other in nearby(site, through_near.shape[:3])]
+    sums = jnp.dot(jnp.concatenate(fields, axis=1), through_near[site], preferred_element_type=jnp.float32)
+    return sums - RELAX_WEIGHT * side_product(one_near, op_mine, site, 1)
 
 
 def side_rows(weights, last):
@@ -320,31 +334,36 @@
     return jnp.dot(field[site], weights[site][side_rows(weights, last)], preferred_element_type=jnp.float32)
 
 
-def near_step(weights, part, received, site):
-    return part[site] - RELAX_WEIGHT * side_product(received, weights, site, 1)
-
-
-def return_step(back_near, sent, near, site):
-    value = near[(1,) + site].astype(jnp.float32) - RELAX_WEIGHT * products([(back_near[site], sent[(0,) + site])])
-    return value.astype(jnp.bfloat16)
-
-
-def third_own_kernel(op_mine, rhs_mine, field_mine, value_mine, rest):
+def third_own_kernel(op_mine, rhs_mine, swapped, value, rest):
+    field = swapped.at[0]
+
     def step(site):
-        sums = packed_stencil(op_mine, site, field_mine, [])
-        rest[site] = relaxed(value_mine[site], field_mine[site], rhs_mine[site], sums)
+        sums = packed_stencil(op_mine, site, field, [])
+        rest[site] = relaxed(value[site], field[site], rhs_mine[site], sums)
 
     for_sites(op_mine.shape[:3], step)
 
 
-def third_kernel(op_mine, rest, field_mine, field_pair, message, part_next):
-    def step(site):
-        part = rest[site] - RELAX_WEIGHT * side_product(field_pair, op_mine, site, 2)
+def third_kernel(op_mine, rest, value, swapped, received, message, field_mine, field_pair, part_next):
+    late = received.at[1]
+
+    def first(site):
+        field = received[(0,) + site].astype(jnp.float32) + swapped[(1,) + site].astype(jnp.float32)
+        field_pair[site] = field.astype(jnp.bfloat16)
+        field = (value[site] + late[site].astype(jnp.float32)).astype(jnp.bfloat16)
+        field_mine[site] = field
+        message[(0,) + site] = field
+
+    for_sites(op_mine.shape[:3], first)
+
+    def second(site):
+        sums = packed_stencil(op_mine, site, late, [field_pair])
+        kept = (1 - RELAX_WEIGHT * DIAGONAL_SHIFT) * late[site].astype(jnp.float32)
+        part = rest[site] + kept - RELAX_WEIGHT * sums
         part_next[site] = part
-        message[(0,) + site] = field_mine[site]
         message[(1,) + site] = part.astype(jnp.bfloat16)
 
-    for_sites(op_mine.shape[:3], step)
+    for_sites(op_mine.shape[:3], second)
 
 
 def last_kernel(
@@ -352,18 +371,11 @@
     fine_out, coarse_out, result, held, done,
 ):
     extent = rest.shape[:3]
-    field = near.at[0]
+    field, part = near.at[0], near.at[1]
 
     def step(site):
-        sums = jnp.dot(
-            jnp.concatenate([field[other] for other in nearby(site, extent)], axis=1),
-            through_near[site],
-            preferred_element_type=jnp.float32,
-        )
-        sums += jnp.dot(far[site], through_pair[site], preferred_element_type=jnp.float32)
-        value = rest[site] + sums - RELAX_WEIGHT * jnp.dot(
-            near[(1,) + site], op_mine[site][side_rows(op_mine, 1)], preferred_element_type=jnp.float32
-        )
+        value = rest[site] + answer(op_mine, through_near, field, part, site)
+        value += jnp.dot(far[site], through_pair[site], preferred_element_type=jnp.float32)
         result[(0,) + site] = value.astype(jnp.bfloat16)
 
     for_sites(extent, step)
@@ -464,35 +476,31 @@
         *parts,
         flops=GATHER_FLOPS,
     )
-    near_message, far_field = send(sent, across), send(start_mine, far)
+    near_message = send(sent, across)
     packed_shape = extent + (packed_depth(operator), operator.shape[6])
-    part_pair, packed_mine, packed_pair, through_pair = kernel_call(
+    near_shape = extent + (packed_shape[3] - 2 * packed_shape[4], packed_shape[4])
+    packed_mine, packed_pair, rest, through_near, through_pair, through_mine = kernel_call(
         first_pair_kernel,
         "pair_one",
-        [(full, bf16), (packed_shape, bf16), (packed_shape, bf16), (operator.shape[2:], bf16)],
-        [],
-        operator, op_pair, rhs_pair, start_pair, start_mine,
-    )
+        [(packed_shape, bf16), (packed_shape, bf16), (full, f32), (near_shape, bf16)] + [(operator.shape[2:], bf16)] * 2,
+        [(full, bf16)],
+        operator, op_pair, rhs_mine, rhs_pair, start_pair, start_mine, sent, part_mine,
+    )
+    value, swapped = kernel_call(
+        second_kernel, "second", [(full, f32), ((2,) + full, bf16)], [(full, bf16)],
+        packed_mine, through_near, through_mine, back_near, sent, rest, near_message,
+    )
+    received = send(swapped, other)
     (rest,) = kernel_call(
-        second_near_kernel, "second_near", [(full, f32)], [(full, bf16)] * 2,
-        packed_mine, back_near, rhs_mine, sent, part_mine, part_pair, near_message,
-    )
-    field_mine, value_mine = kernel_call(
-        second_far_kernel, "second_far", [(full, bf16), (full, f32)], [], through_pair, far_field, rest,
-    )
-    field_pair = send(field_mine, other)
+        third_own_kernel, "third_own", [(full, f32)], [], packed_mine, rhs_mine, swapped, value,
+    )
+    sent, field_mine, field_pair, part_mine = kernel_call(
+        third_kernel, "third", [((2,) + full, bf16), (full, bf16), (full, bf16), (full, f32)], [],
+        packed_mine, rest, value, swapped, received,
+    )
+    near_message, far_field = send(sent, across), send(field_mine, far)
     (rest,) = kernel_call(
-        third_own_kernel, "third_own", [(full, f32)], [], packed_mine, rhs_mine, field_mine, value_mine,
-    )
-    sent, part_mine = kernel_call(
-        third_kernel, "third", [((2,) + full, bf16), (full, f32)], [], packed_mine, rest, field_mine, field_pair,
-    )
-    near_message, far_field = send(sent, across), send(field_mine, far)
-    rest, through_near = kernel_call(
-        second_pair_kernel,
-        "pair_two",
-        [(full, f32), (extent + (packed_shape[3] - 2 * packed_shape[4], packed_shape[4]), bf16)],
-        [(full, bf16)] * 2,
+        second_pair_kernel, "pair_two", [(full, f32)], [(full, bf16)] * 2,
         packed_mine, packed_pair, back_near, rhs_mine, rhs_pair, field_pair, field_mine, sent, part_mine,
     )
     fine_correction, coarse_iterate = last(

time: 29.3 us -> 29.3 us (level)
  starting transfers between devices: 15.3 us -> 13.4 us
  waiting for transfers between devices: 5.14 us -> 7.01 us
    ppermute x10 -> x9, starting transfers between devices: 15.3 us -> 13.4 us  [send(): return lax.ppermute(array, ('zt', 'xy'), permutation(target, turn))]
    ppermute x10 -> x9, waiting for transfers between devices: 5.14 us -> 7.01 us  [send(): return lax.ppermute(array, ('zt', 'xy'), permutation(target, turn))]
    pallas_call x8 -> x7, Pallas kernels: 3.8 us -> 3.82 us  [kernel_call(): pl.pallas_call(kernel, in_specs=[pl.BlockSpec(memory_space=pltpu.VMEM)] *...]
  transfers between devices with their start and end apart: 10 -> 9, of which waited for: 5 -> 4; matrix products, arithmetic and copies ran while one was open for 0% -> 0% of each run, Pallas kernels for 20% -> 19%
where the time goes in v8:
time: 29.3 us; the launch traced here: 29.2 us
  starting transfers between devices  13.4 us (46%)
  Pallas kernels  8.07 us (28%)
  waiting for transfers between devices  7.01 us (24%)
  between operations  0.69 us (2%)
    ppermute x9, starting transfers between devices, send(): return lax.ppermute(array, ('zt', 'xy'), permutation(target, turn))  13.4 us
    ppermute x9, waiting for transfers between devices, send(): return lax.ppermute(array, ('zt', 'xy'), permutation(target, turn))  7.01 us
    pallas_call x7, Pallas kernels, kernel_call(): pl.pallas_call(kernel, in_specs=[pl.BlockSpec(memory_space=pltpu.VMEM)] *...  3.82 us
    pallas_call x1, Pallas kernels, restrict(): pl.pallas_call(functools.partial(restrict_kernel, coarse_y), in_specs=[pl...  2.52 us
    pallas_call x1, Pallas kernels, last(): pl.pallas_call(last_kernel, in_specs=[pl.BlockSpec(memory_space=pltpu.VME...  1.73 us
  transfers between devices with their start and end apart: 9, of which 4 were waited for; matrix products, arithmetic and copies ran while one was open for 0% of the time, Pallas kernels for 19%

profile of v8, /device:TPU:0, one launch (start us, length us, event | category | flops | bytes accessed | tf_op | source)
XLA Modules:
  0.0 29.2 jit_solution(14688352938934324728)
XLA Ops:
  0.6 0.5 %collective-permute-start = (bf16[1,9,2,2,2,128,128]{6,5,4,3,2,1,0:T(8,128)(2,1)}, bf16[1,9,2,2,2,128,128]{6,5,4,3,2,1,0:T(8,128)(2,1)S(1)}, u32[]{:S(2)}, u32[]{:S(2)}) collective-permute-start(bf16[1,9,2,2,2,128,128]{6,5,4,3,2,1,0:T(8,128)(2,1)} %operator_hbm.1), channel_id=1, source_target_pairs={{0,2},{1,3},{2,0},{3,1},{4,6},{5,7},{6,4},{7,5},{8,10},{9,11},{10,... | collective-permute-start | bytes 7077896 | tf_op jit(solution)/shard_map/ppermute | solution.py:448
  1.1 2.5 %restrict.1 = (bf16[4,16,128]{2,1,0:T(8,128)(2,1)S(1)}, bf16[4,2,12,32,256]{4,3,2,1,0:T(8,128)(2,1)S(1)}, bf16[1,9,2,2,2,128,128]{6,5,4,3,2,1,0:T(8,128)(2,1)S(1)}) custom-call(bf16[4,2,12,16,256]{4,3,2,1,0:T(8,128)(2,1)} %fine_hbm.1, bf16[4,2,12,32,256]{4,3,2,1,0:T(8,128)(2,1)} %null_hbm.1, bf16[1,9,2,2,2,128,128]{6,5,4,3,2,1,0:T(8,128)(2,1)} %operator_hbm.1), custom_call_target="tpu_custom_call" | custom-call | tf_op jit(solution)/shard_map/restrict/pallas_call | solution.py:71
  3.7 2.7 %collective-permute-start.1 = (bf16[4,16,128]{2,1,0:T(8,128)(2,1)S(1)}, bf16[4,16,128]{2,1,0:T(8,128)(2,1)S(1)}, u32[]{:S(2)}, u32[]{:S(2)}) collective-permute-start(bf16[4,16,128]{2,1,0:T(8,128)(2,1)S(1)} %get-tuple-element.24.refs_3_), channel_id=1, source_target_pairs={{0,3},{1,2},{2,1},{3,0},{4,7},{5,6},{6,5},{7,4},{8,11},{9,10},{10,... | collective-permute-start | bytes 49160 | tf_op jit(solution)/shard_map/ppermute | solution.py:448
  6.4 0.0 collective-permute-start.2
  6.4 0.2 collective-permute-start.3
  6.6 0.0 collective-permute-done.op_pair
  6.6 1.9 %collective-permute-start.4 = (bf16[2,2,2,128,128]{4,3,2,1,0:T(8,128)(2,1)S(1)}, bf16[2,2,2,128,128]{4,3,2,1,0:T(8,128)(2,1)S(1)}, u32[]{:S(2)}, u32[]{:S(2)}) collective-permute-start(bf16[2,2,2,128,128]{4,3,2,1,0:T(8,128)(2,1)S(1)} %block.1), channel_id=1, source_target_pairs={{0,4},{1,5},{2,30},{3,31},{4,2},{5,3},{6,8},{7,9},{8,6},{9,7},{10,... | collective-permute-start | bytes 786440 | tf_op jit(solution)/shard_map/ppermute | solution.py:448
  8.5 0.0 collective-permute-done.1.refs_0_
  8.5 1.7 %collective-permute-done.2.refs_1_ = bf16[4,16,128]{2,1,0:T(8,128)(2,1)S(1)} collective-permute-done((bf16[4,16,128]{2,1,0:T(8,128)(2,1)S(1)}, bf16[4,16,128]{2,1,0:T(8,128)(2,1)S(1)}, u32[]{:S(2)}, u32[]{:S(2)}) %collective-permute-start.2) | collective-permute-done | bytes 16416 | tf_op jit(solution)/shard_map/ppermute | solution.py:448
  10.1 0.0 collective-permute-done.3.refs_2_
  10.1 0.5 %gather.1 = (bf16[2,2,2,16,128]{4,3,2,1,0:T(8,128)(2,1)S(1)}, bf16[2,2,2,16,128]{4,3,2,1,0:T(8,128)(2,1)S(1)}, bf16[2,2,2,16,128]{4,3,2,1,0:T(8,128)(2,1)S(1)}, ...) custom-call(bf16[1,9,2,2,2,128,128]{6,5,4,3,2,1,0:T(8,128)(2,1)S(1)}, ...), custom_call_target="tpu_custom_call" | custom-call | flops 10000000000 | tf_op jit(solution)/shard_map/gather/pallas_call | solution.py:425
  10.6 3.0 %collective-permute-start.5 = (bf16[2,2,2,2,16,128]{5,4,3,2,1,0:T(8,128)(2,1)S(1)}, bf16[2,2,2,2,16,128]{5,4,3,2,1,0:T(8,128)(2,1)S(1)}, u32[]{:S(2)}, u32[]{:S(2)}) collective-permute-start(bf16[2,2,2,2,16,128]{5,4,3,2,1,0:T(8,128)(2,1)S(1)} %get-tuple-element.29.sent), channel_id=1, source_target_pairs={{0,30},{1,31},{2,4},{3,5},{4,2},{5,3},{6,8},{7,9},{8,6},{9,7},{10,... | collective-permute-start | bytes 196616 | tf_op jit(solution)/shard_map/ppermute | solution.py:448
  13.6 1.5 %pair_one.1 = (bf16[2,2,2,768,128]{4,3,2,1,0:T(8,128)(2,1)S(1)}, bf16[2,2,2,768,128]{4,3,2,1,0:T(8,128)(2,1)S(1)}, f32[2,2,2,16,128]{4,3,2,1,0:T(8,128)S(1)}, bf...) custom-call(bf16[1,9,2,2,2,128,128]{6,5,4,3,2,1,0:T(8,128)(2,1)S(1)}, ...), custom_call_target="tpu_custom_call" | custom-call | tf_op jit(solution)/shard_map/pair_one/pallas_call | solution.py:425
  15.2 2.0 %collective-permute-done.5.near = bf16[2,2,2,2,16,128]{5,4,3,2,1,0:T(8,128)(2,1)S(1)} collective-permute-done((bf16[2,2,2,2,16,128]{5,4,3,2,1,0:T(8,128)(2,1)S(1)}, bf16[2,2,2,2,16,128]{5,4,3,2,1,0:T(8,128)(2,1)S(1)}, u32[]{:S(2)}, u32[]{:S(2)}) %collective-permute-start.5) | collective-permute-done | bytes 65568 | tf_op jit(solution)/shard_map/ppermute | solution.py:448
  17.2 0.0 collective-permute-done.4.back_near
  17.2 0.5 %second.1 = (f32[2,2,2,16,128]{4,3,2,1,0:T(8,128)S(1)}, bf16[2,2,2,2,16,128]{5,4,3,2,1,0:T(8,128)(2,1)S(1)}) custom-call(bf16[2,2,2,768,128]{4,3,2,1,0:T(8,128)(2,1)S(1)} %get-tuple-element.31.op_mine, bf16[2,2,2,512,128]{4,3,2,1,0:T(8,128)(2,1)S(1)} %get-tuple-element.32.through_near, bf16[2,2,2,128,128]{4,3,2,1,0:T(8,128)(2,1)S(1)} %get-tuple-element.35.through_mine, ...), custom_call_target="tpu_custom_call" | custom-call | tf_op jit(solution)/shard_map/second/pallas_call | solution.py:425
  17.7 0.1 collective-permute-start.6
  17.8 0.2 third_own.1.rest
  18.0 1.0 %collective-permute-done.6.received = bf16[2,2,2,2,16,128]{5,4,3,2,1,0:T(8,128)(2,1)S(1)} collective-permute-done((bf16[2,2,2,2,16,128]{5,4,3,2,1,0:T(8,128)(2,1)S(1)}, bf16[2,2,2,2,16,128]{5,4,3,2,1,0:T(8,128)(2,1)S(1)}, u32[]{:S(2)}, u32[]{:S(2)}) %collective-permute-start.6) | collective-permute-done | bytes 65568 | tf_op jit(solution)/shard_map/ppermute | solution.py:448
  19.0 0.3 %third.1 = (bf16[2,2,2,2,16,128]{5,4,3,2,1,0:T(8,128)(2,1)S(1)}, bf16[2,2,2,16,128]{4,3,2,1,0:T(8,128)(2,1)S(1)}, bf16[2,2,2,16,128]{4,3,2,1,0:T(8,128)(2,1)S(1)}, f32[2,2,2,16,128]{4,3,2,1,0:T(8,128)S(1)}) custom-call(bf16[2,2,2,768,128]{4,3,2,1,0:T(8,128)(2,1)S(1)} %get-tuple-element.31.op_mine, f32[2,2,2,16,128]{4,3,2,1,0:T(8,128)S(1)} %third_own.1.rest, ...), custom_call_target="tpu_custom_call" | custom-call | tf_op jit(solution)/shard_map/third/pallas_call | solution.py:425
  19.3 4.2 %collective-permute-start.7 = (bf16[2,2,2,2,16,128]{5,4,3,2,1,0:T(8,128)(2,1)S(1)}, bf16[2,2,2,2,16,128]{5,4,3,2,1,0:T(8,128)(2,1)S(1)}, u32[]{:S(2)}, u32[]{:S(2)}) collective-permute-start(bf16[2,2,2,2,16,128]{5,4,3,2,1,0:T(8,128)(2,1)S(1)} %get-tuple-element.41.sent), channel_id=1, source_target_pairs={{0,30},{1,31},{2,4},{3,5},{4,2},{5,3},{6,8},{7,9},{8,6},{9,7},{10,... | collective-permute-start | bytes 196616 | tf_op jit(solution)/shard_map/ppermute | solution.py:448
  23.5 0.9 %collective-permute-start.8 = (bf16[2,2,2,16,128]{4,3,2,1,0:T(8,128)(2,1)S(1)}, bf16[2,2,2,16,128]{4,3,2,1,0:T(8,128)(2,1)S(1)}, u32[]{:S(2)}, u32[]{:S(2)}) collective-permute-start(bf16[2,2,2,16,128]{4,3,2,1,0:T(8,128)(2,1)S(1)} %get-tuple-element.40.other), channel_id=1, source_target_pairs={{0,28},{1,29},{2,6},{3,7},{4,0},{5,1},{6,10},{7,11},{8,4},{9,5},{1... | collective-permute-start | bytes 98312 | tf_op jit(solution)/shard_map/ppermute | solution.py:448
  24.4 0.7 %pair_two.1.rest = f32[2,2,2,16,128]{4,3,2,1,0:T(8,128)S(1)} custom-call(bf16[2,2,2,768,128]{4,3,2,1,0:T(8,128)(2,1)S(1)} %get-tuple-element.31.op_mine, bf16[2,2,2,768,128]{4,3,2,1,0:T(8,128)(2,1)S(1)} %get-tuple-element.34.op_pair, bf16[2,2,2,128,128]{4,3,2,1,0:T(8,128)(2,1)S(1)} %collective-permute-done.4.back_near, ...), custom_call_target="tpu_custom_call" | custom-call | tf_op jit(solution)/shard_map/pair_two/pallas_call | solution.py:425
  25.1 2.4 %collective-permute-done.8.far = bf16[2,2,2,16,128]{4,3,2,1,0:T(8,128)(2,1)S(1)} collective-permute-done((bf16[2,2,2,16,128]{4,3,2,1,0:T(8,128)(2,1)S(1)}, bf16[2,2,2,16,128]{4,3,2,1,0:T(8,128)(2,1)S(1)}, u32[]{:S(2)}, u32[]{:S(2)}) %collective-permute-start.8) | collective-permute-done | bytes 32800 | tf_op jit(solution)/shard_map/ppermute | solution.py:448
  27.4 0.0 collective-permute-done.7.near
  27.4 1.7 %last.1 = (bf16[4,2,12,16,256]{4,3,2,1,0:T(8,128)(2,1)}, bf16[1,2,2,2,16,128]{5,4,3,2,1,0:T(8,128)(2,1)}) custom-call(bf16[2,2,2,768,128]{4,3,2,1,0:T(8,128)(2,1)S(1)} %get-tuple-element.31.op_mine, bf16[2,2,2,512,128]{4,3,2,1,0:T(8,128)(2,1)S(1)} %get-tuple-element.32.through_near, bf16[2,2,2,128,128]{4,3,2,1,0:T(8,128)(2,1)S(1)} %get-tuple-element.33.through_pair, ...), custom_call_target="tpu_custom_call" | custom-call | tf_op jit(solution)/shard_map/last/pallas_call | solution.py:393
  (1 shorter events, 0.0 us)
Async XLA Ops:
  0.6 5.9 %collective-permute-start = (bf16[1,9,2,2,2,128,128]{6,5,4,3,2,1,0:T(8,128)(2,1)}, bf16[1,9,2,2,2,128,128]{6,5,4,3,2,1,0:T(8,128)(2,1)S(1)}, u32[]{:S(2)}, u32[]{:S(2)}) collective-permute-start(bf16[1,9,2,2,2,128,128]{6,5,4,3,2,1,0:T(8,128)(2,1)} %operator_hbm.1), channel_id=1, source_target_pairs={{0,2},{1,3},{2,0},{3,1},{4,6},{5,7},{6,4},{7,5},{8,10},{9,11},{10,... | collective-permute-start | bytes 7077896 | tf_op jit(solution)/shard_map/ppermute | solution.py:448
  3.7 4.8 %collective-permute-start.1 = (bf16[4,16,128]{2,1,0:T(8,128)(2,1)S(1)}, bf16[4,16,128]{2,1,0:T(8,128)(2,1)S(1)}, u32[]{:S(2)}, u32[]{:S(2)}) collective-permute-start(bf16[4,16,128]{2,1,0:T(8,128)(2,1)S(1)} %get-tuple-element.24.refs_3_), channel_id=1, source_target_pairs={{0,3},{1,2},{2,1},{3,0},{4,7},{5,6},{6,5},{7,4},{8,11},{9,10},{10,... | collective-permute-start | bytes 49160 | tf_op jit(solution)/shard_map/ppermute | solution.py:448
  6.4 3.7 %collective-permute-start.2 = (bf16[4,16,128]{2,1,0:T(8,128)(2,1)S(1)}, bf16[4,16,128]{2,1,0:T(8,128)(2,1)S(1)}, u32[]{:S(2)}, u32[]{:S(2)}) collective-permute-start(bf16[4,16,128]{2,1,0:T(8,128)(2,1)S(1)} %get-tuple-element.24.refs_3_), channel_id=1, source_target_pairs={{0,1},{1,0},{2,3},{3,2},{4,5},{5,4},{6,7},{7,6},{8,9},{9,8},{10,11... | collective-permute-start | bytes 49160 | tf_op jit(solution)/shard_map/ppermute | solution.py:448
  6.4 3.7 %collective-permute-start.3 = (bf16[4,16,128]{2,1,0:T(8,128)(2,1)S(1)}, bf16[4,16,128]{2,1,0:T(8,128)(2,1)S(1)}, u32[]{:S(2)}, u32[]{:S(2)}) collective-permute-start(bf16[4,16,128]{2,1,0:T(8,128)(2,1)S(1)} %get-tuple-element.24.refs_3_), channel_id=1, source_target_pairs={{0,2},{1,3},{2,0},{3,1},{4,6},{5,7},{6,4},{7,5},{8,10},{9,11},{10,... | collective-permute-start | bytes 49160 | tf_op jit(solution)/shard_map/ppermute | solution.py:448
  6.6 10.6 %collective-permute-start.4 = (bf16[2,2,2,128,128]{4,3,2,1,0:T(8,128)(2,1)S(1)}, bf16[2,2,2,128,128]{4,3,2,1,0:T(8,128)(2,1)S(1)}, u32[]{:S(2)}, u32[]{:S(2)}) collective-permute-start(bf16[2,2,2,128,128]{4,3,2,1,0:T(8,128)(2,1)S(1)} %block.1), channel_id=1, source_target_pairs={{0,4},{1,5},{2,30},{3,31},{4,2},{5,3},{6,8},{7,9},{8,6},{9,7},{10,... | collective-permute-start | bytes 786440 | tf_op jit(solution)/shard_map/ppermute | solution.py:448
  10.6 6.5 %collective-permute-start.5 = (bf16[2,2,2,2,16,128]{5,4,3,2,1,0:T(8,128)(2,1)S(1)}, bf16[2,2,2,2,16,128]{5,4,3,2,1,0:T(8,128)(2,1)S(1)}, u32[]{:S(2)}, u32[]{:S(2)}) collective-permute-start(bf16[2,2,2,2,16,128]{5,4,3,2,1,0:T(8,128)(2,1)S(1)} %get-tuple-element.29.sent), channel_id=1, source_target_pairs={{0,30},{1,31},{2,4},{3,5},{4,2},{5,3},{6,8},{7,9},{8,6},{9,7},{10,... | collective-permute-start | bytes 196616 | tf_op jit(solution)/shard_map/ppermute | solution.py:448
  17.7 1.3 %collective-permute-start.6 = (bf16[2,2,2,2,16,128]{5,4,3,2,1,0:T(8,128)(2,1)S(1)}, bf16[2,2,2,2,16,128]{5,4,3,2,1,0:T(8,128)(2,1)S(1)}, u32[]{:S(2)}, u32[]{:S(2)}) collective-permute-start(bf16[2,2,2,2,16,128]{5,4,3,2,1,0:T(8,128)(2,1)S(1)} %get-tuple-element.37.swapped), channel_id=1, source_target_pairs={{0,2},{1,3},{2,0},{3,1},{4,6},{5,7},{6,4},{7,5},{8,10},{9,11},{10,... | collective-permute-start | bytes 196616 | tf_op jit(solution)/shard_map/ppermute | solution.py:448
  19.3 8.1 %collective-permute-start.7 = (bf16[2,2,2,2,16,128]{5,4,3,2,1,0:T(8,128)(2,1)S(1)}, bf16[2,2,2,2,16,128]{5,4,3,2,1,0:T(8,128)(2,1)S(1)}, u32[]{:S(2)}, u32[]{:S(2)}) collective-permute-start(bf16[2,2,2,2,16,128]{5,4,3,2,1,0:T(8,128)(2,1)S(1)} %get-tuple-element.41.sent), channel_id=1, source_target_pairs={{0,30},{1,31},{2,4},{3,5},{4,2},{5,3},{6,8},{7,9},{8,6},{9,7},{10,... | collective-permute-start | bytes 196616 | tf_op jit(solution)/shard_map/ppermute | solution.py:448
  23.5 3.9 %collective-permute-start.8 = (bf16[2,2,2,16,128]{4,3,2,1,0:T(8,128)(2,1)S(1)}, bf16[2,2,2,16,128]{4,3,2,1,0:T(8,128)(2,1)S(1)}, u32[]{:S(2)}, u32[]{:S(2)}) collective-permute-start(bf16[2,2,2,16,128]{4,3,2,1,0:T(8,128)(2,1)S(1)} %get-tuple-element.40.other), channel_id=1, source_target_pairs={{0,28},{1,29},{2,6},{3,7},{4,0},{5,1},{6,10},{7,11},{8,4},{9,5},{1... | collective-permute-start | bytes 98312 | tf_op jit(solution)/shard_map/ppermute | solution.py:448

commit v9 on v8

--- a/solution.py
+++ b/solution.py
@@ -240,7 +240,7 @@
 
 def first_pair_kernel(
     op_mine, op_pair, rhs_mine, rhs_pair, here, other, sent, part_mine,
-    packed_mine, packed_pair, rest, through_near, through_pair, through_mine, part_pair,
+    packed_mine, packed_pair, rest, through_near, through_pair, part_pair,
 ):
     sides, pair_sides = time_sides(True), time_sides(False)
 
@@ -252,8 +252,6 @@
         part_pair[site] = relaxed(value, here[site], rhs_pair[site], sums).astype(jnp.bfloat16)
         outer, inner = packed_pair[site][side_rows(packed_pair, 1)], packed_mine[site][side_rows(packed_mine, 2)]
         through_pair[site] = two_steps(outer, inner).astype(jnp.bfloat16)
-        outer, inner = packed_mine[site][side_rows(packed_mine, 1)], packed_pair[site][side_rows(packed_pair, 2)]
-        through_mine[site] = two_steps(outer, inner).astype(jnp.bfloat16)
 
     extent = op_mine.shape[2:5]
     columns = op_mine.shape[6]
@@ -299,22 +297,18 @@
     return RELAX_WEIGHT * RELAX_WEIGHT * jnp.dot(first, second, preferred_element_type=jnp.float32)
 
 
-def second_kernel(op_mine, through_near, through_mine, back_near, sent, rest, near, value, swapped, one_near):
+def second_near_kernel(op_mine, through_near, back_near, sent, rest, near, value, one_near):
     extent = rest.shape[:3]
     field = near.at[0]
 
     def first(site):
         sums = products([(back_near[site], sent[(0,) + site])])
         one_near[site] = (near[(1,) + site].astype(jnp.float32) - RELAX_WEIGHT * sums).astype(jnp.bfloat16)
-        sums = jnp.dot(field[site], through_mine[site], preferred_element_type=jnp.float32)
-        swapped[(1,) + site] = sums.astype(jnp.bfloat16)
 
     for_sites(extent, first)
 
     def second(site):
-        result = rest[site] + answer(op_mine, through_near, field, one_near, site)
-        value[site] = result
-        swapped[(0,) + site] = result.astype(jnp.bfloat16)
+        value[site] = rest[site] + answer(op_mine, through_near, field, one_near, site)
 
     for_sites(extent, second)
 
@@ -325,6 +319,15 @@
     return sums - RELAX_WEIGHT * side_product(one_near, op_mine, site, 1)
 
 
+def second_far_kernel(through_pair, far, rest, field_mine, value_mine):
+    def step(site):
+        value = rest[site] + jnp.dot(far[site], through_pair[site], preferred_element_type=jnp.float32)
+        value_mine[site] = value
+        field_mine[site] = value.astype(jnp.bfloat16)
+
+    for_sites(rest.shape[:3], step)
+
+
 def side_rows(weights, last):
     depth, columns = weights.shape[3:]
     return slice(depth - last * columns, depth - (last - 1) * columns)
@@ -334,36 +337,22 @@
     return jnp.dot(field[site], weights[site][side_rows(weights, last)], preferred_element_type=jnp.float32)
 
 
-def third_own_kernel(op_mine, rhs_mine, swapped, value, rest):
-    field = swapped.at[0]
-
+def third_own_kernel(op_mine, rhs_mine, field_mine, value_mine, rest):
     def step(site):
-        sums = packed_stencil(op_mine, site, field, [])
-        rest[site] = relaxed(value[site], field[site], rhs_mine[site], sums)
+        sums = packed_stencil(op_mine, site, field_mine, [])
+        rest[site] = relaxed(value_mine[site], field_mine[site], rhs_mine[site], sums)
 
     for_sites(op_mine.shape[:3], step)
 
 
-def third_kernel(op_mine, rest, value, swapped, received, message, field_mine, field_pair, part_next):
-    late = received.at[1]
-
-    def first(site):
-        field = received[(0,) + site].astype(jnp.float32) + swapped[(1,) + site].astype(jnp.float32)
-        field_pair[site] = field.astype(jnp.bfloat16)
-        field = (value[site] + late[site].astype(jnp.float32)).astype(jnp.bfloat16)
-        field_mine[site] = field
-        message[(0,) + site] = field
-
-    for_sites(op_mine.shape[:3], first)
-
-    def second(site):
-        sums = packed_stencil(op_mine, site, late, [field_pair])
-        kept = (1 - RELAX_WEIGHT * DIAGONAL_SHIFT) * late[site].astype(jnp.float32)
-        part = rest[site] + kept - RELAX_WEIGHT * sums
+def third_kernel(op_mine, rest, field_mine, field_pair, message, part_next):
+    def step(site):
+        part = rest[site] - RELAX_WEIGHT * side_product(field_pair, op_mine, site, 2)
         part_next[site] = part
+        message[(0,) + site] = field_mine[site]
         message[(1,) + site] = part.astype(jnp.bfloat16)
 
-    for_sites(op_mine.shape[:3], second)
+    for_sites(op_mine.shape[:3], step)
 
 
 def last_kernel(
@@ -476,27 +465,29 @@
         *parts,
         flops=GATHER_FLOPS,
     )
-    near_message = send(sent, across)
+    near_message, far_field = send(sent, across), send(start_mine, far)
     packed_shape = extent + (packed_depth(operator), operator.shape[6])
     near_shape = extent + (packed_shape[3] - 2 * packed_shape[4], packed_shape[4])
-    packed_mine, packed_pair, rest, through_near, through_pair, through_mine = kernel_call(
+    packed_mine, packed_pair, rest, through_near, through_pair = kernel_call(
         first_pair_kernel,
         "pair_one",
-        [(packed_shape, bf16), (packed_shape, bf16), (full, f32), (near_shape, bf16)] + [(operator.shape[2:], bf16)] * 2,
+        [(packed_shape, bf16), (packed_shape, bf16), (full, f32), (near_shape, bf16), (operator.shape[2:], bf16)],
         [(full, bf16)],
         operator, op_pair, rhs_mine, rhs_pair, start_pair, start_mine, sent, part_mine,
     )
-    value, swapped = kernel_call(
-        second_kernel, "second", [(full, f32), ((2,) + full, bf16)], [(full, bf16)],
-        packed_mine, through_near, through_mine, back_near, sent, rest, near_message,
-    )
-    received = send(swapped, other)
     (rest,) = kernel_call(
-        third_own_kernel, "third_own", [(full, f32)], [], packed_mine, rhs_mine, swapped, value,
-    )
-    sent, field_mine, field_pair, part_mine = kernel_call(
-        third_kernel, "third", [((2,) + full, bf16), (full, bf16), (full, bf16), (full, f32)], [],
-        packed_mine, rest, value, swapped, received,
+        second_near_kernel, "second_near", [(full, f32)], [(full, bf16)],
+        packed_mine, through_near, back_near, sent, rest, near_message,
+    )
+    field_mine, value_mine = kernel_call(
+        second_far_kernel, "second_far", [(full, bf16), (full, f32)], [], through_pair, far_field, rest,
+    )
+    field_pair = send(field_mine, other)
+    (rest,) = kernel_call(
+        third_own_kernel, "third_own", [(full, f32)], [], packed_mine, rhs_mine, field_mine, value_mine,
+    )
+    sent, part_mine = kernel_call(
+        third_kernel, "third", [((2,) + full, bf16), (full, f32)], [], packed_mine, rest, field_mine, field_pair,
     )
     near_message, far_field = send(sent, across), send(field_mine, far)
     (rest,) = kernel_call(

time: 29.3 us -> 29.2 us (level)
  waiting for transfers between devices: 7.01 us -> 4.95 us
  starting transfers between devices: 13.4 us -> 15.4 us
    ppermute x9 -> x10, starting transfers between devices: 13.4 us -> 15.4 us  [send(): return lax.ppermute(array, ('zt', 'xy'), permutation(target, turn))]
    ppermute x9 -> x10, waiting for transfers between devices: 7.01 us -> 4.95 us  [send(): return lax.ppermute(array, ('zt', 'xy'), permutation(target, turn))]
    pallas_call x7 -> x8, Pallas kernels: 3.82 us -> 3.77 us  [kernel_call(): pl.pallas_call(kernel, in_specs=[pl.BlockSpec(memory_space=pltpu.VMEM)] *...]
  transfers between devices with their start and end apart: 9 -> 10, of which waited for: 4 -> 5; matrix products, arithmetic and copies ran while one was open for 0% -> 0% of each run, Pallas kernels for 19% -> 20%
where the time goes in v9:
time: 29.2 us; the launch traced here: 29.1 us
  starting transfers between devices  15.4 us (53%)
  Pallas kernels  8.02 us (27%)
  waiting for transfers between devices  4.95 us (17%)
  between operations  0.67 us (2%)
    ppermute x10, starting transfers between devices, send(): return lax.ppermute(array, ('zt', 'xy'), permutation(target, turn))  15.4 us
    ppermute x10, waiting for transfers between devices, send(): return lax.ppermute(array, ('zt', 'xy'), permutation(target, turn))  4.95 us
    pallas_call x8, Pallas kernels, kernel_call(): pl.pallas_call(kernel, in_specs=[pl.BlockSpec(memory_space=pltpu.VMEM)] *...  3.77 us
    pallas_call x1, Pallas kernels, restrict(): pl.pallas_call(functools.partial(restrict_kernel, coarse_y), in_specs=[pl...  2.52 us
    pallas_call x1, Pallas kernels, last(): pl.pallas_call(last_kernel, in_specs=[pl.BlockSpec(memory_space=pltpu.VME...  1.73 us
  transfers between devices with their start and end apart: 10, of which 5 were waited for; matrix products, arithmetic and copies ran while one was open for 0% of the time, Pallas kernels for 20%

profile of v9, /device:TPU:0, one launch (start us, length us, event | category | flops | bytes accessed | tf_op | source)
XLA Modules:
  0.0 29.1 jit_solution(4878425916149112741)
XLA Ops:
  0.6 0.5 %collective-permute-start = (bf16[1,9,2,2,2,128,128]{6,5,4,3,2,1,0:T(8,128)(2,1)}, bf16[1,9,2,2,2,128,128]{6,5,4,3,2,1,0:T(8,128)(2,1)S(1)}, u32[]{:S(2)}, u32[]{:S(2)}) collective-permute-start(bf16[1,9,2,2,2,128,128]{6,5,4,3,2,1,0:T(8,128)(2,1)} %operator_hbm.1), channel_id=1, source_target_pairs={{0,2},{1,3},{2,0},{3,1},{4,6},{5,7},{6,4},{7,5},{8,10},{9,11},{10,... | collective-permute-start | bytes 7077896 | tf_op jit(solution)/shard_map/ppermute | solution.py:437
  1.1 2.5 %restrict.1 = (bf16[4,16,128]{2,1,0:T(8,128)(2,1)S(1)}, bf16[4,2,12,32,256]{4,3,2,1,0:T(8,128)(2,1)S(1)}, bf16[1,9,2,2,2,128,128]{6,5,4,3,2,1,0:T(8,128)(2,1)S(1)}) custom-call(bf16[4,2,12,16,256]{4,3,2,1,0:T(8,128)(2,1)} %fine_hbm.1, bf16[4,2,12,32,256]{4,3,2,1,0:T(8,128)(2,1)} %null_hbm.1, bf16[1,9,2,2,2,128,128]{6,5,4,3,2,1,0:T(8,128)(2,1)} %operator_hbm.1), custom_call_target="tpu_custom_call" | custom-call | tf_op jit(solution)/shard_map/restrict/pallas_call | solution.py:71
  3.7 2.7 %collective-permute-start.1 = (bf16[4,16,128]{2,1,0:T(8,128)(2,1)S(1)}, bf16[4,16,128]{2,1,0:T(8,128)(2,1)S(1)}, u32[]{:S(2)}, u32[]{:S(2)}) collective-permute-start(bf16[4,16,128]{2,1,0:T(8,128)(2,1)S(1)} %get-tuple-element.21.refs_3_), channel_id=1, source_target_pairs={{0,3},{1,2},{2,1},{3,0},{4,7},{5,6},{6,5},{7,4},{8,11},{9,10},{10,... | collective-permute-start | bytes 49160 | tf_op jit(solution)/shard_map/ppermute | solution.py:437
  6.4 0.0 collective-permute-start.2
  6.4 0.2 collective-permute-start.3
  6.6 0.0 collective-permute-done.op_pair
  6.6 1.9 %collective-permute-start.4 = (bf16[2,2,2,128,128]{4,3,2,1,0:T(8,128)(2,1)S(1)}, bf16[2,2,2,128,128]{4,3,2,1,0:T(8,128)(2,1)S(1)}, u32[]{:S(2)}, u32[]{:S(2)}) collective-permute-start(bf16[2,2,2,128,128]{4,3,2,1,0:T(8,128)(2,1)S(1)} %block.1), channel_id=1, source_target_pairs={{0,4},{1,5},{2,30},{3,31},{4,2},{5,3},{6,8},{7,9},{8,6},{9,7},{10,... | collective-permute-start | bytes 786440 | tf_op jit(solution)/shard_map/ppermute | solution.py:437
  8.5 0.0 collective-permute-done.1.refs_0_
  8.5 1.7 %collective-permute-done.2.refs_1_ = bf16[4,16,128]{2,1,0:T(8,128)(2,1)S(1)} collective-permute-done((bf16[4,16,128]{2,1,0:T(8,128)(2,1)S(1)}, bf16[4,16,128]{2,1,0:T(8,128)(2,1)S(1)}, u32[]{:S(2)}, u32[]{:S(2)}) %collective-permute-start.2) | collective-permute-done | bytes 16416 | tf_op jit(solution)/shard_map/ppermute | solution.py:437
  10.1 0.0 collective-permute-done.3.refs_2_
  10.1 0.5 %gather.1 = (bf16[2,2,2,16,128]{4,3,2,1,0:T(8,128)(2,1)S(1)}, bf16[2,2,2,16,128]{4,3,2,1,0:T(8,128)(2,1)S(1)}, bf16[2,2,2,16,128]{4,3,2,1,0:T(8,128)(2,1)S(1)}, ...) custom-call(bf16[1,9,2,2,2,128,128]{6,5,4,3,2,1,0:T(8,128)(2,1)S(1)}, ...), custom_call_target="tpu_custom_call" | custom-call | flops 10000000000 | tf_op jit(solution)/shard_map/gather/pallas_call | solution.py:414
  10.6 3.0 %collective-permute-start.6 = (bf16[2,2,2,2,16,128]{5,4,3,2,1,0:T(8,128)(2,1)S(1)}, bf16[2,2,2,2,16,128]{5,4,3,2,1,0:T(8,128)(2,1)S(1)}, u32[]{:S(2)}, u32[]{:S(2)}) collective-permute-start(bf16[2,2,2,2,16,128]{5,4,3,2,1,0:T(8,128)(2,1)S(1)} %get-tuple-element.26.sent), channel_id=1, source_target_pairs={{0,30},{1,31},{2,4},{3,5},{4,2},{5,3},{6,8},{7,9},{8,6},{9,7},{10,... | collective-permute-start | bytes 196616 | tf_op jit(solution)/shard_map/ppermute | solution.py:437
  13.6 1.6 %collective-permute-start.5 = (bf16[2,2,2,16,128]{4,3,2,1,0:T(8,128)(2,1)S(1)}, bf16[2,2,2,16,128]{4,3,2,1,0:T(8,128)(2,1)S(1)}, u32[]{:S(2)}, u32[]{:S(2)}) collective-permute-start(bf16[2,2,2,16,128]{4,3,2,1,0:T(8,128)(2,1)S(1)} %get-tuple-element.25.other), channel_id=1, source_target_pairs={{0,28},{1,29},{2,6},{3,7},{4,0},{5,1},{6,10},{7,11},{8,4},{9,5},{1... | collective-permute-start | bytes 98312 | tf_op jit(solution)/shard_map/ppermute | solution.py:437
  15.2 1.5 %pair_one.1 = (bf16[2,2,2,768,128]{4,3,2,1,0:T(8,128)(2,1)S(1)}, bf16[2,2,2,768,128]{4,3,2,1,0:T(8,128)(2,1)S(1)}, f32[2,2,2,16,128]{4,3,2,1,0:T(8,128)S(1)}, bf...) custom-call(bf16[1,9,2,2,2,128,128]{6,5,4,3,2,1,0:T(8,128)(2,1)S(1)} %get-tuple-element.20.operator.op_mine, ...), custom_call_target="tpu_custom_call" | custom-call | tf_op jit(solution)/shard_map/pair_one/pallas_call | solution.py:414
  16.7 0.4 %collective-permute-done.6.near = bf16[2,2,2,2,16,128]{5,4,3,2,1,0:T(8,128)(2,1)S(1)} collective-permute-done((bf16[2,2,2,2,16,128]{5,4,3,2,1,0:T(8,128)(2,1)S(1)}, bf16[2,2,2,2,16,128]{5,4,3,2,1,0:T(8,128)(2,1)S(1)}, u32[]{:S(2)}, u32[]{:S(2)}) %collective-permute-start.6) | collective-permute-done | bytes 65568 | tf_op jit(solution)/shard_map/ppermute | solution.py:437
  17.2 0.1 collective-permute-done.4.back_near
  17.3 0.4 %second_near.1.rest = f32[2,2,2,16,128]{4,3,2,1,0:T(8,128)S(1)} custom-call(bf16[2,2,2,768,128]{4,3,2,1,0:T(8,128)(2,1)S(1)} %get-tuple-element.28.op_mine, bf16[2,2,2,512,128]{4,3,2,1,0:T(8,128)(2,1)S(1)} %get-tuple-element.29.through_near, bf16[2,2,2,128,128]{4,3,2,1,0:T(8,128)(2,1)S(1)} %collective-permute-done.4.back_near, ...), custom_call_target="tpu_custom_call" | custom-call | tf_op jit(solution)/shard_map/second_near/pallas_call | solution.py:414
  17.7 0.0 collective-permute-done.5.far
  17.7 0.2 second_far.1
  17.9 0.1 collective-permute-start.7
  18.0 0.2 third_own.1.rest
  18.2 0.9 %collective-permute-done.7.field_pair.here = bf16[2,2,2,16,128]{4,3,2,1,0:T(8,128)(2,1)S(1)} collective-permute-done((bf16[2,2,2,16,128]{4,3,2,1,0:T(8,128)(2,1)S(1)}, bf16[2,2,2,16,128]{4,3,2,1,0:T(8,128)(2,1)S(1)}, u32[]{:S(2)}, u32[]{:S(2)}) %collective-permute-start.7) | collective-permute-done | bytes 32800 | tf_op jit(solution)/shard_map/ppermute | solution.py:437
  19.2 0.2 third.1
  19.4 4.1 %collective-permute-start.8 = (bf16[2,2,2,2,16,128]{5,4,3,2,1,0:T(8,128)(2,1)S(1)}, bf16[2,2,2,2,16,128]{5,4,3,2,1,0:T(8,128)(2,1)S(1)}, u32[]{:S(2)}, u32[]{:S(2)}) collective-permute-start(bf16[2,2,2,2,16,128]{5,4,3,2,1,0:T(8,128)(2,1)S(1)} %get-tuple-element.35.sent), channel_id=1, source_target_pairs={{0,30},{1,31},{2,4},{3,5},{4,2},{5,3},{6,8},{7,9},{8,6},{9,7},{10,... | collective-permute-start | bytes 196616 | tf_op jit(solution)/shard_map/ppermute | solution.py:437
  23.4 1.4 %collective-permute-start.9 = (bf16[2,2,2,16,128]{4,3,2,1,0:T(8,128)(2,1)S(1)}, bf16[2,2,2,16,128]{4,3,2,1,0:T(8,128)(2,1)S(1)}, u32[]{:S(2)}, u32[]{:S(2)}) collective-permute-start(bf16[2,2,2,16,128]{4,3,2,1,0:T(8,128)(2,1)S(1)} %get-tuple-element.33.field_mine.other), channel_id=1, source_target_pairs={{0,28},{1,29},{2,6},{3,7},{4,0},{5,1},{6,10},{7,11},{8,4},{9,5},{1... | collective-permute-start | bytes 98312 | tf_op jit(solution)/shard_map/ppermute | solution.py:437
  24.9 0.7 %pair_two.1.rest = f32[2,2,2,16,128]{4,3,2,1,0:T(8,128)S(1)} custom-call(bf16[2,2,2,768,128]{4,3,2,1,0:T(8,128)(2,1)S(1)} %get-tuple-element.28.op_mine, bf16[2,2,2,768,128]{4,3,2,1,0:T(8,128)(2,1)S(1)} %get-tuple-element.31.op_pair, bf16[2,2,2,128,128]{4,3,2,1,0:T(8,128)(2,1)S(1)} %collective-permute-done.4.back_near, ...), custom_call_target="tpu_custom_call" | custom-call | tf_op jit(solution)/shard_map/pair_two/pallas_call | solution.py:414
  25.5 1.8 %collective-permute-done.9.far = bf16[2,2,2,16,128]{4,3,2,1,0:T(8,128)(2,1)S(1)} collective-permute-done((bf16[2,2,2,16,128]{4,3,2,1,0:T(8,128)(2,1)S(1)}, bf16[2,2,2,16,128]{4,3,2,1,0:T(8,128)(2,1)S(1)}, u32[]{:S(2)}, u32[]{:S(2)}) %collective-permute-start.9) | collective-permute-done | bytes 32800 | tf_op jit(solution)/shard_map/ppermute | solution.py:437
  27.4 0.0 collective-permute-done.8.near
  27.4 1.7 %last.1 = (bf16[4,2,12,16,256]{4,3,2,1,0:T(8,128)(2,1)}, bf16[1,2,2,2,16,128]{5,4,3,2,1,0:T(8,128)(2,1)}) custom-call(bf16[2,2,2,768,128]{4,3,2,1,0:T(8,128)(2,1)S(1)} %get-tuple-element.28.op_mine, bf16[2,2,2,512,128]{4,3,2,1,0:T(8,128)(2,1)S(1)} %get-tuple-element.29.through_near, bf16[2,2,2,128,128]{4,3,2,1,0:T(8,128)(2,1)S(1)} %get-tuple-element.30.through_pair, ...), custom_call_target="tpu_custom_call" | custom-call | tf_op jit(solution)/shard_map/last/pallas_call | solution.py:382
  (1 shorter events, 0.0 us)
Async XLA Ops:
  0.6 5.9 %collective-permute-start = (bf16[1,9,2,2,2,128,128]{6,5,4,3,2,1,0:T(8,128)(2,1)}, bf16[1,9,2,2,2,128,128]{6,5,4,3,2,1,0:T(8,128)(2,1)S(1)}, u32[]{:S(2)}, u32[]{:S(2)}) collective-permute-start(bf16[1,9,2,2,2,128,128]{6,5,4,3,2,1,0:T(8,128)(2,1)} %operator_hbm.1), channel_id=1, source_target_pairs={{0,2},{1,3},{2,0},{3,1},{4,6},{5,7},{6,4},{7,5},{8,10},{9,11},{10,... | collective-permute-start | bytes 7077896 | tf_op jit(solution)/shard_map/ppermute | solution.py:437
  3.7 4.8 %collective-permute-start.1 = (bf16[4,16,128]{2,1,0:T(8,128)(2,1)S(1)}, bf16[4,16,128]{2,1,0:T(8,128)(2,1)S(1)}, u32[]{:S(2)}, u32[]{:S(2)}) collective-permute-start(bf16[4,16,128]{2,1,0:T(8,128)(2,1)S(1)} %get-tuple-element.21.refs_3_), channel_id=1, source_target_pairs={{0,3},{1,2},{2,1},{3,0},{4,7},{5,6},{6,5},{7,4},{8,11},{9,10},{10,... | collective-permute-start | bytes 49160 | tf_op jit(solution)/shard_map/ppermute | solution.py:437
  6.4 3.7 %collective-permute-start.2 = (bf16[4,16,128]{2,1,0:T(8,128)(2,1)S(1)}, bf16[4,16,128]{2,1,0:T(8,128)(2,1)S(1)}, u32[]{:S(2)}, u32[]{:S(2)}) collective-permute-start(bf16[4,16,128]{2,1,0:T(8,128)(2,1)S(1)} %get-tuple-element.21.refs_3_), channel_id=1, source_target_pairs={{0,1},{1,0},{2,3},{3,2},{4,5},{5,4},{6,7},{7,6},{8,9},{9,8},{10,11... | collective-permute-start | bytes 49160 | tf_op jit(solution)/shard_map/ppermute | solution.py:437
  6.4 3.7 %collective-permute-start.3 = (bf16[4,16,128]{2,1,0:T(8,128)(2,1)S(1)}, bf16[4,16,128]{2,1,0:T(8,128)(2,1)S(1)}, u32[]{:S(2)}, u32[]{:S(2)}) collective-permute-start(bf16[4,16,128]{2,1,0:T(8,128)(2,1)S(1)} %get-tuple-element.21.refs_3_), channel_id=1, source_target_pairs={{0,2},{1,3},{2,0},{3,1},{4,6},{5,7},{6,4},{7,5},{8,10},{9,11},{10,... | collective-permute-start | bytes 49160 | tf_op jit(solution)/shard_map/ppermute | solution.py:437
  6.6 10.7 %collective-permute-start.4 = (bf16[2,2,2,128,128]{4,3,2,1,0:T(8,128)(2,1)S(1)}, bf16[2,2,2,128,128]{4,3,2,1,0:T(8,128)(2,1)S(1)}, u32[]{:S(2)}, u32[]{:S(2)}) collective-permute-start(bf16[2,2,2,128,128]{4,3,2,1,0:T(8,128)(2,1)S(1)} %block.1), channel_id=1, source_target_pairs={{0,4},{1,5},{2,30},{3,31},{4,2},{5,3},{6,8},{7,9},{8,6},{9,7},{10,... | collective-permute-start | bytes 786440 | tf_op jit(solution)/shard_map/ppermute | solution.py:437
  10.6 6.5 %collective-permute-start.6 = (bf16[2,2,2,2,16,128]{5,4,3,2,1,0:T(8,128)(2,1)S(1)}, bf16[2,2,2,2,16,128]{5,4,3,2,1,0:T(8,128)(2,1)S(1)}, u32[]{:S(2)}, u32[]{:S(2)}) collective-permute-start(bf16[2,2,2,2,16,128]{5,4,3,2,1,0:T(8,128)(2,1)S(1)} %get-tuple-element.26.sent), channel_id=1, source_target_pairs={{0,30},{1,31},{2,4},{3,5},{4,2},{5,3},{6,8},{7,9},{8,6},{9,7},{10,... | collective-permute-start | bytes 196616 | tf_op jit(solution)/shard_map/ppermute | solution.py:437
  13.6 4.1 %collective-permute-start.5 = (bf16[2,2,2,16,128]{4,3,2,1,0:T(8,128)(2,1)S(1)}, bf16[2,2,2,16,128]{4,3,2,1,0:T(8,128)(2,1)S(1)}, u32[]{:S(2)}, u32[]{:S(2)}) collective-permute-start(bf16[2,2,2,16,128]{4,3,2,1,0:T(8,128)(2,1)S(1)} %get-tuple-element.25.other), channel_id=1, source_target_pairs={{0,28},{1,29},{2,6},{3,7},{4,0},{5,1},{6,10},{7,11},{8,4},{9,5},{1... | collective-permute-start | bytes 98312 | tf_op jit(solution)/shard_map/ppermute | solution.py:437
  17.9 1.3 %collective-permute-start.7 = (bf16[2,2,2,16,128]{4,3,2,1,0:T(8,128)(2,1)S(1)}, bf16[2,2,2,16,128]{4,3,2,1,0:T(8,128)(2,1)S(1)}, u32[]{:S(2)}, u32[]{:S(2)}) collective-permute-start(bf16[2,2,2,16,128]{4,3,2,1,0:T(8,128)(2,1)S(1)} %get-tuple-element.33.field_mine.other), channel_id=1, source_target_pairs={{0,2},{1,3},{2,0},{3,1},{4,6},{5,7},{6,4},{7,5},{8,10},{9,11},{10,... | collective-permute-start | bytes 98312 | tf_op jit(solution)/shard_map/ppermute | solution.py:437
  19.4 8.0 %collective-permute-start.8 = (bf16[2,2,2,2,16,128]{5,4,3,2,1,0:T(8,128)(2,1)S(1)}, bf16[2,2,2,2,16,128]{5,4,3,2,1,0:T(8,128)(2,1)S(1)}, u32[]{:S(2)}, u32[]{:S(2)}) collective-permute-start(bf16[2,2,2,2,16,128]{5,4,3,2,1,0:T(8,128)(2,1)S(1)} %get-tuple-element.35.sent), channel_id=1, source_target_pairs={{0,30},{1,31},{2,4},{3,5},{4,2},{5,3},{6,8},{7,9},{8,6},{9,7},{10,... | collective-permute-start | bytes 196616 | tf_op jit(solution)/shard_map/ppermute | solution.py:437
  23.4 3.9 %collective-permute-start.9 = (bf16[2,2,2,16,128]{4,3,2,1,0:T(8,128)(2,1)S(1)}, bf16[2,2,2,16,128]{4,3,2,1,0:T(8,128)(2,1)S(1)}, u32[]{:S(2)}, u32[]{:S(2)}) collective-permute-start(bf16[2,2,2,16,128]{4,3,2,1,0:T(8,128)(2,1)S(1)} %get-tuple-element.33.field_mine.other), channel_id=1, source_target_pairs={{0,28},{1,29},{2,6},{3,7},{4,0},{5,1},{6,10},{7,11},{8,4},{9,5},{1... | collective-permute-start | bytes 98312 | tf_op jit(solution)/shard_map/ppermute | solution.py:437
